TPU v7x, 256 devices: a whole 4x4x8 slice. The times are simulated.
256 devices in a mesh: dp: 8 (over z), ctx: 32 (over x, y, core).
Axes of the slice: x: 4, y: 4, z: 8, core: 2. Of those that a mesh axis runs over, the one named last changes fastest.
Arguments:
- queries: bfloat16 [8, 8192, 4096], P('dp', 'ctx'), may hold values from -64 to 64
- latent_kv: bfloat16 [8, 512, 8192], P('dp', 'ctx'), may hold values from -8 to 8
- media: int32 [8, 128], P('dp', 'ctx'), may hold values from 0 to 7, as said below
- gate: float32 [32], replicated, may hold values from 0.3 to 1.5
- grad_out: bfloat16 [8, 8192, 4096], P('dp', 'ctx'), may hold values from -16 to 16
Outputs:
- attended: bfloat16 [8, 8192, 4096], P('dp', 'ctx')
- query_grad: bfloat16 [8, 8192, 4096], P('dp', 'ctx')
- latent_grad: bfloat16 [8, 512, 8192], P('dp', 'ctx')
- gate_grad: float32 [32], replicated
Inputs may be any that keep to these rules, and one draw needn't show every extreme that they name: Along each sequence the media index never falls; one image of each sequence is named by exactly 121 consecutive blocks and every other image by exactly one block.
All inputs are finite; a program needn't handle non-finite values.
Results may differ from a plain program's by a relative error of at most 0.0059.
Values may be sent and summed in bfloat16 or wider, within the bound.
No kernel may reach another device: no remote copies, remote signals or barrier semaphores. Data moves between devices by JAX's collectives and lax.ppermute only.
A program may use at most 128 MiB of HBM per device.

v0:
```python
import jax
import jax.numpy as jnp
from jax import lax
from jax.sharding import PartitionSpec as P

NLAT = 64


def image_terms(terms, media_row, count_img):
    ident = jnp.arange(count_img, dtype=jnp.int32)
    onehot = (ident[:, None] == media_row[None, :]).astype(jnp.float32)
    summed = jnp.einsum("ib,bjc->ijc", onehot, terms, precision=lax.Precision.HIGHEST)
    return summed.reshape(count_img * NLAT, terms.shape[2])


def body(queries, latent_kv, media, gate, grad_out):
    heads = gate.shape[0]
    width = queries.shape[2]
    head_size = width // heads
    tokens = queries.shape[1]
    blocks = media.shape[1]
    block_len = tokens // blocks
    scale = head_size ** (-0.5)
    gathered = lax.all_gather(latent_kv, "ctx", axis=1, tiled=True)[0]
    images = gathered.shape[0] // NLAT
    table = gathered.reshape(images, NLAT, 2 * width)
    media_row = media[0]
    chosen = jnp.take(table, media_row, axis=0)
    keys = chosen[..., :width].reshape(blocks, NLAT, heads, head_size)
    values = chosen[..., width:].reshape(blocks, NLAT, heads, head_size)
    query_blocks = queries[0].reshape(blocks, block_len, heads, head_size)
    scores = (
        jnp.einsum("bthd,bjhd->bhtj", query_blocks, keys, preferred_element_type=jnp.float32)
        * scale
    )
    probs = jax.nn.softmax(scores, axis=-1)
    probs_b = probs.astype(jnp.bfloat16)
    mix = jnp.einsum("bhtj,bjhd->bthd", probs_b, values, preferred_element_type=jnp.float32)
    tgate = jnp.tanh(gate)[None, None, :, None]
    attended = (tgate * mix).astype(jnp.bfloat16).reshape(1, tokens, width)
    upstream = grad_out[0].reshape(blocks, block_len, heads, head_size).astype(jnp.float32)
    gate_part = jnp.einsum("bthd,bthd->h", upstream, mix, precision=lax.Precision.HIGHEST)
    gate_sum = lax.psum(gate_part, ("dp", "ctx"))
    dmix = (tgate * upstream).astype(jnp.bfloat16)
    dprob = jnp.einsum("bthd,bjhd->bhtj", dmix, values, preferred_element_type=jnp.float32)
    inner = jnp.sum(probs * dprob, axis=-1, keepdims=True)
    dscore = (probs * (dprob - inner)).astype(jnp.bfloat16)
    query_grad = (
        jnp.einsum("bhtj,bjhd->bthd", dscore, keys, preferred_element_type=jnp.float32) * scale
    )
    query_grad = query_grad.astype(jnp.bfloat16).reshape(1, tokens, width)
    key_part = (
        jnp.einsum("bhtj,bthd->bjhd", dscore, query_blocks, preferred_element_type=jnp.float32)
        * scale
    )
    value_part = jnp.einsum("bhtj,bthd->bjhd", probs_b, dmix, preferred_element_type=jnp.float32)
    terms = jnp.concatenate(
        [key_part.reshape(blocks, NLAT, width), value_part.reshape(blocks, NLAT, width)], axis=-1
    )
    every = image_terms(terms, media_row, images)
    latent_grad = lax.psum_scatter(every, "ctx", scatter_dimension=0, tiled=True).astype(
        jnp.bfloat16
    )
    tanh_gate = jnp.tanh(gate)
    gate_grad = (1.0 - tanh_gate * tanh_gate) * gate_sum
    return (attended, query_grad, latent_grad[None], gate_grad)


def solution(mesh):
    in_specs = (
        P("dp", "ctx", None),
        P("dp", "ctx", None),
        P("dp", "ctx"),
        P(),
        P("dp", "ctx", None),
    )
    out_specs = (P("dp", "ctx", None), P("dp", "ctx", None), P("dp", "ctx", None), P())
    return jax.shard_map(body, mesh=mesh, in_specs=in_specs, out_specs=out_specs, check_vma=False)
```

profile of v0, /device:TPU:24, one launch (start us, length us, event | category | flops | bytes accessed | tf_op | source)
XLA Modules:
  0.0 363.3 jit_solution(13424886105351501940)
XLA Ops:
  7.2 0.7 all-gather.2.cloned.1.call-update
  8.0 3.4 copy.44
  11.4 1.8 copy.43
  13.2 57.8 %all-gather.2.cloned.1.call-done = bf16[1,512,8192]{2,1,0:T(8,128)(2,1)} async-done(((bf16[1,16,8192]{2,1,0:T(8,128)(2,1)}), bf16[1,512,8192]{2,1,0:T(8,128)(2,1)}) %all-gather.2.cloned.1.call-update) | async-done | bytes 8388624 | tf_op jit(solution)/shard_map/all_gather | solution.py:24
  71.0 6.1 %gather_fusion = bf16[4,64,8192]{2,1,0:T(8,128)(2,1)} fusion(bf16[8,64,8192]{2,1,0:T(8,128)(2,1)} %bitcast.90, s32[1024]{0:T(1024)S(1)} %pad_clamp_fusion), kind=kCustom, calls=%fused_computation | custom fusion | bytes 8388624 | tf_op jit(solution)/shard_map/jit(_take)/gather | solution.py:28
  77.1 2.7 broadcast_select_fusion
  80.2 1.8 copy-done.1
  82.0 1.3 fusion.12
  83.3 6.2 %fusion.36 = (f32[4,32,64]{2,1,0:T(8,128)S(1)}, f32[4,32,64,64]{2,3,1,0:T(8,128)S(1)}) fusion(f32[4,32,64,64]{3,2,1,0:T(8,128)S(1)} %fusion.12), kind=kOutput, calls=%fused_computation.53 | output fusion | flops 2097215 | bytes 4227072 | tf_op jit(solution)/shard_map/sub | solution.py:36
  89.4 0.9 fusion.16
  90.3 1.2 copy-done.4
  91.6 1.9 copy-done.3
  93.5 2.4 multiply_reduce_fusion
  95.9 76.3 %psum.7 = f32[32]{0:T(128)S(1)} all-reduce(f32[32]{0:T(128)S(1)} %multiply_reduce_fusion), channel_id=1, replica_groups=mesh['dp'=8,'ctx'=32] {'dp','ctx'}, use_global_device_ids=true, to_apply=%region_4.5 | all-reduce | flops 32 | bytes 256 | tf_op jit(solution)/shard_map/psum | solution.py:43
  172.8 7.2 %multiply_reduce_fusion.1 = (f32[4,32,64]{2,1,0:T(8,128)S(1)}, f32[4,32,64,64]{2,3,1,0:T(8,128)}) fusion(f32[4,32,64,64]{2,3,1,0:T(8,128)} %copy-done.4, f32[4,32,64]{2,1,0:T(8,128)S(1)} %get-tuple-element.8, bf16[4,8,32,8,128]{4,3,2,1,0:T(8,128)(2,1)} %copy-done.9, bf16[4,64,32,128]{3,2,1,0:T(8,128)(2,1)} %bitcast.87, f32[32]{0:T(128)S(1)} %get-tuple-element.7), kind=kOutput, calls=%fused_computation.16 | convolution fusion | flops 138928128 | bytes 8454272 | tf_op jit(solution)/shard_map/bthd,bjhd->bhtj/dot_general | solution.py:45
  180.0 1.2 convolution_bitcast_fusion
  181.2 4.4 %copy.38 = f32[4,64,32,128]{3,2,0,1:T(8,128)} copy(f32[4,64,32,128]{3,1,2,0:T(8,128)S(1)} %convolution_bitcast_fusion) | data formatting | bytes 8388608 | tf_op jit(solution)/shard_map/reshape | solution.py:58
  185.6 5.3 %reshape.87 = f32[4,64,4096]{2,0,1:T(4,128)} reshape(f32[4,64,32,128]{3,2,0,1:T(8,128)} %copy.38) | data formatting | bytes 8388608 | tf_op jit(solution)/shard_map/reshape | solution.py:58
  190.8 4.8 %multiply_convert_fusion.1 = bf16[4,32,64,64]{2,3,1,0:T(8,128)(2,1)S(1)} fusion(f32[4,32,64,64]{2,3,1,0:T(8,128)} %get-tuple-element.11, f32[4,32,64]{2,1,0:T(8,128)S(1)} %get-tuple-element.10, f32[4,32,64,64]{2,3,1,0:T(8,128)} %copy-done.4, f32[4,32,64]{2,1,0:T(8,128)S(1)} %get-tuple-element.8), kind=kLoop, calls=%fused_computation.15 | loop fusion | flops 2097152 | bytes 5308416 | tf_op jit(solution)/shard_map/convert_element_type | solution.py:47
  195.7 1.0 multiply_bitcast_fusion
  197.0 4.4 %copy.37 = f32[4,64,32,128]{3,2,0,1:T(8,128)} copy(f32[4,64,32,128]{3,1,2,0:T(8,128)S(1)} %multiply_bitcast_fusion) | data formatting | bytes 8388608 | tf_op jit(solution)/shard_map/reshape | solution.py:58
  201.4 5.3 %reshape.86 = f32[4,64,4096]{2,0,1:T(4,128)} reshape(f32[4,64,32,128]{3,2,0,1:T(8,128)} %copy.37) | data formatting | bytes 8388608 | tf_op jit(solution)/shard_map/reshape | solution.py:58
  206.6 12.8 %fusion.1 = f32[8,64,8192]{2,0,1:T(8,128)S(1)} fusion(f32[4,64,4096]{2,0,1:T(4,128)} %reshape.87, f32[4,64,4096]{2,0,1:T(4,128)} %reshape.86, s32[4]{0:T(128)S(1)} %bitcast.93), kind=kOutput, calls=%fused_computation.2 | convolution fusion | flops 203423776 | bytes 25165840 | tf_op jit(solution)/shard_map/ib,bjc->ijc/dot_general | solution.py:12
  219.5 15.0 %copy.28 = f32[8,64,8192]{2,1,0:T(8,128)} copy(f32[8,64,8192]{2,0,1:T(8,128)S(1)} %fusion.1) | data formatting | bytes 33554432 | tf_op jit(solution)/shard_map/ib,bjc->ijc/dot_general | solution.py:12
  234.5 2.8 fusion.5
  237.4 2.7 copy.17
  240.0 4.3 %reshape.69 = bf16[1,256,4096]{2,1,0:T(8,128)(2,1)} reshape(bf16[4,64,32,128]{3,2,1,0:T(8,128)(2,1)} %copy.17) | data formatting | bytes 4194304 | tf_op jit(solution)/shard_map/reshape | solution.py:40
  244.3 2.8 fusion.25
  247.1 1.4 copy.22
  248.5 2.3 reshape.70
  250.7 103.9 %reduce-scatter.2.cloned.1.call-done = f32[16,8192]{1,0:T(8,128)} async-done(((f32[512,8192]{1,0:T(8,128)}), f32[16,8192]{1,0:T(8,128)}) %reduce-scatter.2.cloned.1.call-update) | async-done | bytes 524304 | tf_op jit(solution)/shard_map/reduce_scatter | solution.py:61
  354.7 1.8 convert_bitcast_fusion
  (29 shorter events, 1.3 us)
Async XLA Ops:
  7.2 4.2 %copy-start.8 = (bf16[1,256,4096]{2,1,0:T(8,128)(2,1)S(1)}, bf16[1,256,4096]{2,1,0:T(8,128)(2,1)}, u32[]{:S(2)}) copy-start(bf16[1,256,4096]{2,1,0:T(8,128)(2,1)} %param.5) | copy-start | bytes 6291460
  7.2 63.8 %all-gather.2.cloned.1.call-start = ((), (), s32[]{:S(2)}) async-start(), calls=%async_computation.1 | async-start | bytes 8650752 | tf_op jit(solution)/shard_map/all_gather | solution.py:24
  7.9 346.8 %reduce-scatter.2.cloned.1.call-start = ((), (), s32[]{:S(2)}) async-start(), calls=%async_computation.2 | async-start | bytes 17301504 | tf_op jit(solution)/shard_map/reduce_scatter | solution.py:61
  8.0 5.2 %copy-start.10 = (s32[1,4]{1,0:T(1,128)S(1)}, s32[1,4]{1,0:T(1,128)}, u32[]{:S(2)}) copy-start(s32[1,4]{1,0:T(1,128)} %param.7) | copy-start | bytes 52
  79.8 2.2 copy-start.1
  80.2 9.3 %copy-start.9 = (bf16[4,8,32,8,128]{4,3,2,1,0:T(8,128)(2,1)}, bf16[4,8,32,8,128]{4,3,2,1,0:T(8,128)(2,1)S(1)}, u32[]{:S(2)}) copy-start(bf16[4,8,32,8,128]{4,3,2,1,0:T(8,128)(2,1)S(1)} %get-tuple-element.5) | copy-start | bytes 6291460
  89.4 2.1 copy-start.4
  89.4 4.1 %copy-start.6 = (bf16[32,8,32,128]{3,2,1,0:T(8,128)(2,1)S(1)}, bf16[32,8,32,128]{3,2,1,0:T(8,128)(2,1)}, u32[]{:S(2)}) copy-start(bf16[32,8,32,128]{3,2,1,0:T(8,128)(2,1)} %copy.44) | copy-start | bytes 6291460
  91.6 1.9 copy-start.3
  91.6 80.7 %copy-start.11 = (f32[32]{0:T(128)S(1)}, f32[32]{0:T(128)}, u32[]{:S(2)}) copy-start(f32[32]{0:T(128)} %param.8) | copy-start | bytes 388
  172.8 7.2 %copy-start.5 = (f32[4,32,64,64]{2,3,1,0:T(8,128)S(1)}, f32[4,32,64,64]{2,3,1,0:T(8,128)}, u32[]{:S(2)}) copy-start(f32[4,32,64,64]{2,3,1,0:T(8,128)} %copy-done.4) | copy-start | bytes 6291460
  172.8 7.2 %copy-start.7 = (bf16[32,8,32,128]{3,2,1,0:T(8,128)(2,1)S(1)}, bf16[32,8,32,128]{3,2,1,0:T(8,128)(2,1)}, u32[]{:S(2)}) copy-start(bf16[32,8,32,128]{3,2,1,0:T(8,128)(2,1)} %copy.44) | copy-start | bytes 6291460
  190.8 4.9 %copy-start.2 = (bf16[32,8,32,128]{3,2,1,0:T(8,128)(2,1)S(1)}, bf16[32,8,32,128]{3,2,1,0:T(8,128)(2,1)}, u32[]{:S(2)}) copy-start(bf16[32,8,32,128]{3,2,1,0:T(8,128)(2,1)} %copy.43) | copy-start | bytes 6291460
  195.7 1.3 copy-start
Sparse Core Ops, SparseCore 0:
  10.6 60.3 all-gather.1
  234.6 120.0 reduce-scatter.1
where the time goes:
time: 364 us; the launch traced here: 363 us
  waiting for transfers between devices  162 us (45%)
  blocking collectives  76.3 us (21%)
  local copies, waits for them, and re-layouts  61.8 us (17%)
  matrix products  27.2 us (7%)
  other arithmetic  21.2 us (6%)
  between operations  14.2 us (4%)
    reduce_scatter x1, waiting for transfers between devices, body(): lax.psum_scatter(every, 'ctx', scatter_dimension=0, tiled=True)  104 us
    psum x1, blocking collectives, body(): gate_sum = lax.psum(gate_part, ('dp', 'ctx'))  76.3 us
    all_gather x1, waiting for transfers between devices, body(): gathered = lax.all_gather(latent_kv, 'ctx', axis=1, tiled=True)[0]  57.8 us
    dot_general x1, local copies, waits for them, and re-layouts, image_terms(): jnp.einsum('ib,bjc->ijc', onehot, terms, precision=lax.Precision.HIGHEST)  15 us
    dot_general x1, matrix products, image_terms(): jnp.einsum('ib,bjc->ijc', onehot, terms, precision=lax.Precision.HIGHEST)  12.8 us
    unnamed x27, local copies, waits for them, and re-layouts  10.8 us
    reshape x2, local copies, waits for them, and re-layouts, body(): key_part.reshape(blocks, NLAT, width)  9.65 us
    reshape x2, local copies, waits for them, and re-layouts, body(): value_part.reshape(blocks, NLAT, width)  9.62 us
  transfers between devices with their start and end apart: 2, of which 2 were waited for; matrix products, arithmetic and copies ran while one was open for 6% of the time, Pallas kernels for 0%

commit v1 on v0

v1 whole, which is shorter than its diff:
```python
import functools

import jax
import jax.numpy as jnp
import numpy as np
from jax import lax
from jax.experimental import pallas as pl
from jax.experimental.pallas import tpu as pltpu
from jax.sharding import Mesh
from jax.sharding import PartitionSpec as P

CTX = ("x", "yh", "yl", "c")
IMG = ("x", "yh")
NLAT = 64
HEADS = 32
HS = 128
GRP = 8
COLS = GRP * HS
WIDE = COLS + 128
SCALE = HS**-0.5

NEAR0 = (2, 8, 6, 24)
NEAR1 = (28, 22, 6, 24)
OWNER0 = [NEAR0[j % 4] + j // 4 for j in range(8)]
OWNER1 = [NEAR1[j % 4] + j // 4 for j in range(8)]
IMAGE_OF = [0] * 32
for _j in range(8):
    IMAGE_OF[OWNER0[_j]] = _j
    IMAGE_OF[OWNER1[_j]] = _j
STEP0 = (0, 1, 2, 3)
STEP1 = (0, 1, 3, 2)


def pairs_out(s):
    a, b = NEAR0[STEP0[s]], NEAR1[STEP1[s]]
    return [(0, a), (1, a + 1), (30, b), (31, b + 1)]


def pairs_back(s):
    return [(b, a) for a, b in pairs_out(s)]


def nt(a, b):
    return lax.dot_general(a, b, (((1,), (1,)), ((), ())), preferred_element_type=jnp.float32)


def tn(a, b):
    return lax.dot_general(a, b, (((0,), (0,)), ((), ())), preferred_element_type=jnp.float32)


def nn(a, b):
    return lax.dot_general(a, b, (((1,), (0,)), ((), ())), preferred_element_type=jnp.float32)


def spread_kernel(lead, got, out):
    sel = got[lead[0]]
    for p in range(32):
        out[p, 0] = sel
        out[p, 1] = got[IMAGE_OF[p]]


def one_head(q, g, k, v, tg, keep):
    s = nt(k, q) * SCALE
    e = jnp.exp(s - jnp.max(s, axis=0, keepdims=True))
    p = e * (keep / jnp.sum(e, axis=0, keepdims=True))
    pb = p.astype(jnp.bfloat16)
    mix = tn(pb, v)
    gf = g.astype(jnp.float32)
    gsum = jnp.sum(gf * mix, axis=0, keepdims=True)
    dm = (tg * gf).astype(jnp.bfloat16)
    dp = nt(v, dm)
    inner = jnp.sum(p * dp, axis=0, keepdims=True)
    ds = (p * (dp - inner)).astype(jnp.bfloat16)
    dq = tn(ds, k) * SCALE
    dk = nn(ds, q) * SCALE
    dv = nn(pb, dm)
    bf = jnp.bfloat16
    return (tg * mix).astype(bf), dq.astype(bf), dk.astype(bf), dv.astype(bf), gsum


def attention_kernel(flags, tg, q, g, kv, x0, x1, x2, x3, o, dq, xo, pay, xbuf, gacc, sem):
    c = pl.program_id(0)
    tokens = q.shape[0]
    active = flags[4] == 1

    @pl.when(c == 0)
    def _():
        gacc[...] = jnp.zeros_like(gacc)
        for n, x in enumerate((x0, x1, x2, x3)):

            @pl.when(active & (flags[5] == n))
            def _():
                pltpu.make_async_copy(x, xbuf, sem).start()

    block = lax.broadcasted_iota(jnp.int32, (1, tokens), 1) // (tokens // 4)
    keep = jnp.zeros((1, tokens), jnp.float32)
    for b in range(4):
        keep = jnp.where((block == b) & (flags[b] == 1), 1.0, keep)

    def work(slot, qf, gf, of, dqf, keep):
        for n in range(GRP):
            cols = slice(n * HS, n * HS + HS)
            h = c * GRP + n
            k = kv[0, 0, :, slot, :, cols].reshape(NLAT, HS)
            v = kv[1, 0, :, slot, :, cols].reshape(NLAT, HS)
            ob, dqb, dkb, dvb, gsum = one_head(qf(cols), gf(cols), k, v, tg[h], keep)
            of(cols, ob)
            dqf(cols, dqb)
            rows = slice(16 * slot, 16 * slot + 16)
            pay[0, c, :, rows, cols] = dkb.reshape(4, 16, HS)
            pay[1, c, :, rows, cols] = dvb.reshape(4, 16, HS)
            gacc[pl.ds(h, 1), :] += gsum

    def put(ref, *lead):
        def f(cols, val):
            ref[(*lead, slice(None), cols)] = val

        return f

    work(0, lambda s: q[:, s], lambda s: g[:, s], put(o), put(dq), keep)

    @pl.when(active)
    def _():
        @pl.when(c == 0)
        def _():
            pltpu.make_async_copy(x0, xbuf, sem).wait()

        work(
            1,
            lambda s: xbuf[0, c, :, s],
            lambda s: xbuf[1, c, :, s],
            put(xo, 0),
            put(xo, 1),
            jnp.ones((1, NLAT), jnp.float32),
        )

    @pl.when(c == pl.num_programs(0) - 1)
    def _():
        gs = jnp.sum(gacc[...].T, axis=0, keepdims=True)
        hi = gs.astype(jnp.bfloat16).astype(jnp.float32)
        mid = (gs - hi).astype(jnp.bfloat16).astype(jnp.float32)
        lo = gs - hi - mid
        row = lax.broadcasted_iota(jnp.int32, (16, HS), 0)
        val = jnp.where(row == 0, hi, jnp.where(row == 1, mid, jnp.where(row == 2, lo, 0.0)))
        val = val.astype(jnp.bfloat16)
        for a in range(2):
            for b in range(4):
                for r in range(4):
                    pay[a, b, r, 0:16, COLS:WIDE] = val


def collect_kernel(lead, got, out, gsum):
    total = jnp.zeros((16, COLS), jnp.float32)
    gates = jnp.zeros((16, 128), jnp.float32)
    for p in range(32):
        total += got[p, 0:16, 0:COLS].astype(jnp.float32)
        gates += got[p, 0:16, COLS:WIDE].astype(jnp.float32)
    gsum[...] = jnp.sum(gates, axis=0, keepdims=True)
    first = lead[0]
    for j in range(8):

        @pl.when(j < first)
        def _():
            out[j] = got[OWNER0[j], 16:32, 0:COLS]

        @pl.when(j > first)
        def _():
            out[j] = got[OWNER1[j], 16:32, 0:COLS]

        @pl.when(j == first)
        def _():
            out[j] = total.astype(jnp.bfloat16)


def merge_kernel(flags, o_in, dq_in, r0, r1, r2, r3, o, dq, sem):
    del o_in, dq_in
    for s, r in enumerate((r0, r1, r2, r3)):
        k = flags[8 + s]
        rows = pl.ds(pl.multiple_of(k * NLAT, NLAT), NLAT)

        @pl.when(flags[12 + s] == 1)
        def _():
            first = pltpu.make_async_copy(r.at[0], o.at[rows], sem.at[0])
            second = pltpu.make_async_copy(r.at[1], dq.at[rows], sem.at[1])
            first.start()
            second.start()
            first.wait()
            second.wait()


VM = pl.BlockSpec(memory_space=pltpu.VMEM)
SM = pl.BlockSpec(memory_space=pltpu.SMEM)
ANY = pl.BlockSpec(memory_space=pl.ANY)
LIMIT = 48 * 1024 * 1024


def body(queries, latent_kv, media, gate, grad_out):
    bf = jnp.bfloat16
    q, g = queries[0], grad_out[0]
    tokens, width = q.shape
    ctx = lax.axis_index(CTX)
    core = lax.axis_index("c")
    mine = media[0]
    other = lax.ppermute(mine, "c", [(0, 1), (1, 0)])
    early = jnp.where(core == 0, mine, other)
    late = jnp.where(core == 0, other, mine)
    lead = jnp.where(ctx < 2, late[3], early[0])

    qb = q.reshape(4, NLAT, width)
    gb = g.reshape(4, NLAT, width)
    high = ctx >= 16
    sent = []
    for s in range(4):
        k = jnp.where(high, STEP1[s], STEP0[s])
        both = jnp.stack([qb[k], gb[k]])
        both = both.reshape(2, NLAT, 4, COLS).transpose(0, 2, 1, 3)
        sent.append(lax.ppermute(both, CTX, pairs_out(s)))

    image = jnp.asarray(np.array(IMAGE_OF, np.int32))[ctx]
    is0 = np.isin(np.arange(32), OWNER0)
    is1 = np.isin(np.arange(32), OWNER1)
    from0 = jnp.asarray(is0)[ctx] & (image < lead)
    from1 = jnp.asarray(is1)[ctx] & (image > lead)
    step0 = np.zeros(32, np.int32)
    step1 = np.zeros(32, np.int32)
    for s in range(4):
        for core_ in range(2):
            step0[NEAR0[STEP0[s]] + core_] = s
            step1[NEAR1[STEP1[s]] + core_] = s
    source = jnp.where(from0, jnp.asarray(step0)[ctx], jnp.asarray(step1)[ctx])
    main = (mine == lead).astype(jnp.int32)
    hot = (ctx < 2) | (ctx >= 30)
    order = jnp.where(high, jnp.array(STEP1, jnp.int32), jnp.array(STEP0, jnp.int32))
    odd = jnp.where(hot, 1 - jnp.where(high, main[np.array(STEP1)], main[np.array(STEP0)]), 0)
    zero = jnp.zeros((2,), jnp.int32)
    flags = jnp.concatenate(
        [main, (from0 | from1).astype(jnp.int32)[None], source[None], zero, order, odd]
    ).astype(jnp.int32)
    lead1 = lead[None]

    chunks = latent_kv[0].reshape(16, 8, COLS).transpose(1, 0, 2)
    mixed = lax.all_to_all(chunks, IMG, 0, 0, tiled=True)
    spread = pl.pallas_call(
        spread_kernel,
        out_shape=jax.ShapeDtypeStruct((32, 2, 16, COLS), bf),
        in_specs=[SM, VM],
        out_specs=VM,
        name="spread",
    )(lead1, mixed)
    kv = lax.all_to_all(spread, CTX, 0, 0, tiled=True).reshape(2, 4, 4, 2, 16, COLS)

    tanh_gate = jnp.tanh(gate)
    wide = pl.BlockSpec((tokens, COLS), lambda c: (0, c))
    o, dq, xo, pay = pl.pallas_call(
        attention_kernel,
        grid=(4,),
        out_shape=[
            jax.ShapeDtypeStruct((tokens, width), bf),
            jax.ShapeDtypeStruct((tokens, width), bf),
            jax.ShapeDtypeStruct((2, NLAT, width), bf),
            jax.ShapeDtypeStruct((2, 4, 4, 32, WIDE), bf),
        ],
        in_specs=[
            SM,
            SM,
            wide,
            wide,
            pl.BlockSpec((2, 1, 4, 2, 16, COLS), lambda c: (0, c, 0, 0, 0, 0)),
            ANY,
            ANY,
            ANY,
            ANY,
        ],
        out_specs=[
            wide,
            wide,
            pl.BlockSpec((2, NLAT, COLS), lambda c: (0, 0, c)),
            pl.BlockSpec((2, 4, 4, 32, WIDE), lambda c: (0, 0, 0, 0, 0)),
        ],
        scratch_shapes=[
            pltpu.VMEM((2, 4, NLAT, COLS), bf),
            pltpu.VMEM((128, HS), jnp.float32),
            pltpu.SemaphoreType.DMA,
        ],
        compiler_params=pltpu.CompilerParams(vmem_limit_bytes=LIMIT),
        name="attention",
    )(flags, tanh_gate, q, g, kv, *sent)

    back = [lax.ppermute(xo, CTX, pairs_back(s)) for s in range(4)]
    parts = lax.all_to_all(pay.reshape(32, 32, WIDE), CTX, 0, 0, tiled=True)
    owned, gsum = pl.pallas_call(
        collect_kernel,
        out_shape=[
            jax.ShapeDtypeStruct((8, 16, COLS), bf),
            jax.ShapeDtypeStruct((1, 128), jnp.float32),
        ],
        in_specs=[SM, VM],
        out_specs=[VM, VM],
        compiler_params=pltpu.CompilerParams(vmem_limit_bytes=LIMIT),
        name="collect",
    )(lead1, parts)
    gates = gsum
    for n in range(1, 8):
        gates = gates + lax.ppermute(gsum, "dp", [(s, (s + n) % 8) for s in range(8)])
    final = lax.all_to_all(owned, IMG, 0, 0, tiled=True)
    latent_grad = final.transpose(1, 0, 2).reshape(1, 16, 8 * COLS)
    o, dq = pl.pallas_call(
        merge_kernel,
        out_shape=[
            jax.ShapeDtypeStruct((tokens, width), bf),
            jax.ShapeDtypeStruct((tokens, width), bf),
        ],
        in_specs=[SM] + [ANY] * 6,
        out_specs=[ANY, ANY],
        scratch_shapes=[pltpu.SemaphoreType.DMA((2,))],
        input_output_aliases={1: 0, 2: 1},
        name="merge",
    )(flags, o, dq, *back)
    gate_grad = (1.0 - tanh_gate * tanh_gate) * gates[0, :HEADS]
    return o[None], dq[None], latent_grad, gate_grad


def solution(mesh):
    fine = Mesh(mesh.devices.reshape(8, 4, 2, 2, 2), ("dp", "x", "yh", "yl", "c"))
    wide = P("dp", CTX, None)
    return jax.shard_map(
        body,
        mesh=fine,
        in_specs=(wide, wide, P("dp", CTX), P(), wide),
        out_specs=(wide, wide, wide, P()),
        check_vma=False,
    )
```

time: 364 us -> 327 us (0.90)
  the two profiles are of different devices: /device:TPU:24 before, /device:TPU:64 now
where the time goes in v1:
time: 327 us; the launch traced here: 326 us
  Pallas kernels  150 us (46%)
  waiting for transfers between devices  79.9 us (24%)
  starting transfers between devices  72.7 us (22%)
  local copies, waits for them, and re-layouts  17 us (5%)
  between operations  5.32 us (2%)
    pallas_call x1, Pallas kernels, body(): pl.pallas_call(merge_kernel, out_shape=[jax.ShapeDtypeStruct((tokens, wid...  132 us
    all_to_all x1, waiting for transfers between devices, body(): parts = lax.all_to_all(pay.reshape(32, 32, WIDE), CTX, 0, 0, tiled=True)  26.6 us
    ppermute x4, waiting for transfers between devices, body(): sent.append(lax.ppermute(both, CTX, pairs_out(s)))  26.3 us
    all_to_all x1, starting transfers between devices, body(): parts = lax.all_to_all(pay.reshape(32, 32, WIDE), CTX, 0, 0, tiled=True)  22.9 us
    ppermute x4, waiting for transfers between devices, body(): back = [lax.ppermute(xo, CTX, pairs_back(s)) for s in range(4)]  19.2 us
    ppermute x7, starting transfers between devices, body(): lax.ppermute(gsum, 'dp', [(s, (s + n) % 8) for s in range(8)])  15.6 us
    pallas_call x1, Pallas kernels, body(): pl.pallas_call(attention_kernel, grid=(4,), out_shape=[jax.ShapeDtypeStru...  14.5 us
    ppermute x4, starting transfers between devices, body(): sent.append(lax.ppermute(both, CTX, pairs_out(s)))  12.5 us
  transfers between devices with their start and end apart: 20, of which 5 were waited for; matrix products, arithmetic and copies ran while one was open for 5% of the time, Pallas kernels for 42%

profile of v1, /device:TPU:64, one launch (start us, length us, event | category | flops | bytes accessed | tf_op | source)
XLA Modules:
  0.0 325.9 jit_solution(13766400350616650447)
XLA Ops:
  0.7 1.2 copy.32
  2.8 6.9 %all-to-all-start = ((bf16[8,16,1024]{2,1,0:T(8,128)(2,1)}), bf16[8,16,1024]{2,1,0:T(8,128)(2,1)S(1)}, u32[]{:S(2)}, u32[]{:S(2)}) async-start(bf16[8,16,1024]{2,1,0:T(8,128)(2,1)} %bitcast.58), calls=%async_computation | async-start | bytes 524288 | tf_op jit(solution)/shard_map/all_to_all | solution.py:242
  9.8 1.3 fusion.1
  11.3 1.1 copy.40
  12.4 4.0 %collective-permute-start.2 = (bf16[2,4,64,1024]{3,2,1,0:T(8,128)(2,1)}, bf16[2,4,64,1024]{3,2,1,0:T(8,128)(2,1)S(1)}, u32[]{:S(2)}, u32[]{:S(2)}) collective-permute-start(bf16[2,4,64,1024]{3,2,1,0:T(8,128)(2,1)} %bitcast.55), channel_id=1, source_target_pairs={{0,8},{1,9},{30,22},{31,23},{32,40},{33,41},{62,54},{63,55},{64,72... | collective-permute-start | bytes 3145736 | tf_op jit(solution)/shard_map/ppermute | solution.py:217
  16.4 1.0 copy.41
  17.4 1.3 collective-permute-start.1
  20.8 2.5 spread.1
  23.3 6.1 %all-to-all-start.1 = ((bf16[32,2,16,1024]{3,2,1,0:T(8,128)(2,1)}), bf16[32,2,16,1024]{3,2,1,0:T(8,128)(2,1)}, u32[]{:S(2)}, u32[]{:S(2)}) async-start(bf16[32,2,16,1024]{3,2,1,0:T(8,128)(2,1)} %spread.1), calls=%async_computation.1 | async-start | bytes 4194304 | tf_op jit(solution)/shard_map/all_to_all | solution.py:250
  29.3 1.7 constant_dynamic-slice_fusion
  31.1 1.1 copy.39
  32.2 4.9 %collective-permute-start.3 = (bf16[2,4,64,1024]{3,2,1,0:T(8,128)(2,1)}, bf16[2,4,64,1024]{3,2,1,0:T(8,128)(2,1)S(1)}, u32[]{:S(2)}, u32[]{:S(2)}) collective-permute-start(bf16[2,4,64,1024]{3,2,1,0:T(8,128)(2,1)} %bitcast.53), channel_id=1, source_target_pairs={{0,6},{1,7},{30,24},{31,25},{32,38},{33,39},{62,56},{63,57},{64,70... | collective-permute-start | bytes 3145736 | tf_op jit(solution)/shard_map/ppermute | solution.py:217
  37.3 1.1 copy.38
  38.4 2.3 collective-permute-start.4
  48.7 10.7 %collective-permute-done.1.x0 = bf16[2,4,64,1024]{3,2,1,0:T(8,128)(2,1)S(1)} collective-permute-done((bf16[2,4,64,1024]{3,2,1,0:T(8,128)(2,1)}, bf16[2,4,64,1024]{3,2,1,0:T(8,128)(2,1)S(1)}, u32[]{:S(2)}, u32[]{:S(2)}) %collective-permute-start.1) | collective-permute-done | bytes 1048608 | tf_op jit(solution)/shard_map/ppermute | solution.py:217
  59.4 15.6 %collective-permute-done.3.x2 = bf16[2,4,64,1024]{3,2,1,0:T(8,128)(2,1)S(1)} collective-permute-done((bf16[2,4,64,1024]{3,2,1,0:T(8,128)(2,1)}, bf16[2,4,64,1024]{3,2,1,0:T(8,128)(2,1)S(1)}, u32[]{:S(2)}, u32[]{:S(2)}) %collective-permute-start.3) | collective-permute-done | bytes 1048608 | tf_op jit(solution)/shard_map/ppermute | solution.py:217
  75.0 14.5 %attention.1 = (bf16[256,4096]{1,0:T(8,128)(2,1)}, bf16[256,4096]{1,0:T(8,128)(2,1)}, bf16[2,64,4096]{2,1,0:T(8,128)(2,1)S(1)}, bf16[2,4,4,32,1152]{4,3,2,1,0:T(8,128)(2,1)}) custom-call(s32[16]{0:T(128)S(1)} %concatenate.3.flags, f32[32]{0:T(128)S(1)} %tanh.3.tg, bf16[256,4096]{1,0:T(8,128)(2,1)} %bitcast.61, bf16[256,4096]{1,0:T(8,128)(2,1)} %bitcast.63, ...), custom_call_target="tpu_custom_call" | custom-call | tf_op jit(solution)/shard_map/attention/pallas_call | solution.py:254
  89.6 1.0 copy-done.1
  90.6 22.9 %all-to-all-start.2 = ((bf16[32,32,1152]{2,1,0:T(8,128)(2,1)}), bf16[32,32,1152]{2,1,0:T(8,128)(2,1)S(1)}, u32[]{:S(2)}, u32[]{:S(2)}) async-start(bf16[32,32,1152]{2,1,0:T(8,128)(2,1)} %bitcast.68), calls=%async_computation.2 | async-start | bytes 4718592 | tf_op jit(solution)/shard_map/all_to_all | solution.py:290
  113.5 1.3 collective-permute-start.8
  114.8 1.3 collective-permute-start.7
  116.1 1.3 collective-permute-start.6
  117.4 1.3 collective-permute-start.5
  118.7 26.6 %all-to-all-done.2.got = bf16[32,32,1152]{2,1,0:T(8,128)(2,1)S(1)} async-done(((bf16[32,32,1152]{2,1,0:T(8,128)(2,1)}), bf16[32,32,1152]{2,1,0:T(8,128)(2,1)S(1)}, u32[]{:S(2)}, u32[]{:S(2)}) %all-to-all-start.2) | async-done | bytes 2359328 | tf_op jit(solution)/shard_map/all_to_all | solution.py:290
  146.3 19.2 %collective-permute-done.8.r3 = bf16[2,64,4096]{2,1,0:T(8,128)(2,1)} collective-permute-done((bf16[2,64,4096]{2,1,0:T(8,128)(2,1)S(1)}, bf16[2,64,4096]{2,1,0:T(8,128)(2,1)}, u32[]{:S(2)}, u32[]{:S(2)}) %collective-permute-start.8) | collective-permute-done | bytes 1048608 | tf_op jit(solution)/shard_map/ppermute | solution.py:289
  165.5 6.4 %collective-permute-start.13 = (f32[1,128]{1,0:T(1,128)S(1)}, f32[1,128]{1,0:T(1,128)S(1)}, u32[]{:S(2)}, u32[]{:S(2)}) collective-permute-start(f32[1,128]{1,0:T(1,128)S(1)} %get-tuple-element.19), channel_id=1, source_target_pairs={{0,160},{32,192},{64,224},{96,0},{128,32},{160,64},{192,96},{224,1... | collective-permute-start | bytes 1544 | tf_op jit(solution)/shard_map/ppermute | solution.py:304
  172.4 4.9 %collective-permute-start.11 = (f32[1,128]{1,0:T(1,128)S(1)}, f32[1,128]{1,0:T(1,128)S(1)}, u32[]{:S(2)}, u32[]{:S(2)}) collective-permute-start(f32[1,128]{1,0:T(1,128)S(1)} %get-tuple-element.19), channel_id=1, source_target_pairs={{0,96},{32,128},{64,160},{96,192},{128,224},{160,0},{192,32},{224,... | collective-permute-start | bytes 1544 | tf_op jit(solution)/shard_map/ppermute | solution.py:304
  177.4 1.5 collective-permute-start.10
  178.9 2.2 collective-permute-start.9
  181.0 132.1 %merge.1 = (bf16[256,4096]{1,0:T(8,128)(2,1)}, bf16[256,4096]{1,0:T(8,128)(2,1)}) custom-call(s32[16]{0:T(128)} %copy-done, bf16[256,4096]{1,0:T(8,128)(2,1)} %get-tuple-element.12.o_in, bf16[256,4096]{1,0:T(8,128)(2,1)} %get-tuple-element.13.dq_in, bf16[2,64,4096]{2,1,0:T(8,128)(2,1)} %collective-permute-done.5.r0, ...), custom_call_target="tpu_custom_call", output_to_operand_aliasing={{0}: (1, {}), {1}: (2, {})} | custom-call | tf_op jit(solution)/shard_map/merge/pallas_call | solution.py:307
  313.2 3.4 %all-to-all-start.3 = ((bf16[8,16,1024]{2,1,0:T(8,128)(2,1)}), bf16[8,16,1024]{2,1,0:T(8,128)(2,1)S(1)}, u32[]{:S(2)}, u32[]{:S(2)}) async-start(bf16[8,16,1024]{2,1,0:T(8,128)(2,1)} %get-tuple-element.18), calls=%async_computation.3 | async-start | bytes 524288 | tf_op jit(solution)/shard_map/all_to_all | solution.py:305
  317.2 7.8 %all-to-all-done.3 = bf16[8,16,1024]{2,1,0:T(8,128)(2,1)S(1)} async-done(((bf16[8,16,1024]{2,1,0:T(8,128)(2,1)}), bf16[8,16,1024]{2,1,0:T(8,128)(2,1)S(1)}, u32[]{:S(2)}, u32[]{:S(2)}) %all-to-all-start.3) | async-done | bytes 262176 | tf_op jit(solution)/shard_map/all_to_all | solution.py:305
  (71 shorter events, 10.2 us)
Async XLA Ops:
  0.6 10.4 %copy-start.3 = (bf16[1,256,4096]{2,1,0:T(8,128)(2,1)S(1)}, bf16[1,256,4096]{2,1,0:T(8,128)(2,1)}, u32[]{:S(2)}) copy-start(bf16[1,256,4096]{2,1,0:T(8,128)(2,1)} %param.20) | copy-start | bytes 6291460
  0.6 18.2 %collective-permute-start = (s32[4]{0:T(128)}, s32[4]{0:T(128)S(1)}, u32[]{:S(2)}, u32[]{:S(2)}) collective-permute-start(s32[4]{0:T(128)} %bitcast.75), channel_id=1, source_target_pairs={{0,1},{1,0},{2,3},{3,2},{4,5},{5,4},{6,7},{7,6},{8,9},{9,8},{10,11... | collective-permute-start | bytes 56 | tf_op jit(solution)/shard_map/ppermute | solution.py:204
  2.8 17.2 %all-to-all-start = ((bf16[8,16,1024]{2,1,0:T(8,128)(2,1)}), bf16[8,16,1024]{2,1,0:T(8,128)(2,1)S(1)}, u32[]{:S(2)}, u32[]{:S(2)}) async-start(bf16[8,16,1024]{2,1,0:T(8,128)(2,1)} %bitcast.58), calls=%async_computation | async-start | bytes 524288 | tf_op jit(solution)/shard_map/all_to_all | solution.py:242
  11.3 7.5 %copy-start.6 = (s32[1,4]{1,0:T(1,128)S(1)}, s32[1,4]{1,0:T(1,128)}, u32[]{:S(2)}) copy-start(s32[1,4]{1,0:T(1,128)} %param.18) | copy-start | bytes 52
  12.4 36.3 %collective-permute-start.2 = (bf16[2,4,64,1024]{3,2,1,0:T(8,128)(2,1)}, bf16[2,4,64,1024]{3,2,1,0:T(8,128)(2,1)S(1)}, u32[]{:S(2)}, u32[]{:S(2)}) collective-permute-start(bf16[2,4,64,1024]{3,2,1,0:T(8,128)(2,1)} %bitcast.55), channel_id=1, source_target_pairs={{0,8},{1,9},{30,22},{31,23},{32,40},{33,41},{62,54},{63,55},{64,72... | collective-permute-start | bytes 3145736 | tf_op jit(solution)/shard_map/ppermute | solution.py:217
  17.4 42.0 %collective-permute-start.1 = (bf16[2,4,64,1024]{3,2,1,0:T(8,128)(2,1)}, bf16[2,4,64,1024]{3,2,1,0:T(8,128)(2,1)S(1)}, u32[]{:S(2)}, u32[]{:S(2)}) collective-permute-start(bf16[2,4,64,1024]{3,2,1,0:T(8,128)(2,1)} %bitcast.57), channel_id=1, source_target_pairs={{0,2},{1,3},{30,28},{31,29},{32,34},{33,35},{62,60},{63,61},{64,66... | collective-permute-start | bytes 3145736 | tf_op jit(solution)/shard_map/ppermute | solution.py:217
  23.3 51.8 %all-to-all-start.1 = ((bf16[32,2,16,1024]{3,2,1,0:T(8,128)(2,1)}), bf16[32,2,16,1024]{3,2,1,0:T(8,128)(2,1)}, u32[]{:S(2)}, u32[]{:S(2)}) async-start(bf16[32,2,16,1024]{3,2,1,0:T(8,128)(2,1)} %spread.1), calls=%async_computation.1 | async-start | bytes 4194304 | tf_op jit(solution)/shard_map/all_to_all | solution.py:250
  32.2 42.8 %collective-permute-start.3 = (bf16[2,4,64,1024]{3,2,1,0:T(8,128)(2,1)}, bf16[2,4,64,1024]{3,2,1,0:T(8,128)(2,1)S(1)}, u32[]{:S(2)}, u32[]{:S(2)}) collective-permute-start(bf16[2,4,64,1024]{3,2,1,0:T(8,128)(2,1)} %bitcast.53), channel_id=1, source_target_pairs={{0,6},{1,7},{30,24},{31,25},{32,38},{33,39},{62,56},{63,57},{64,70... | collective-permute-start | bytes 3145736 | tf_op jit(solution)/shard_map/ppermute | solution.py:217
  37.1 3.6 %copy-start.12 = (s32[32]{0:T(128)S(1)}, s32[32]{0:T(128)}, u32[]{:S(2)}) copy-start(s32[32]{0:T(128)} %constant.61.clone) | copy-start | bytes 388
  37.1 4.2 %copy-start.11 = (s32[32]{0:T(128)S(1)}, s32[32]{0:T(128)}, u32[]{:S(2)}) copy-start(s32[32]{0:T(128)} %constant.60.clone) | copy-start | bytes 388
  37.1 4.7 %copy-start.10 = (pred[32]{0:T(512)(128)(4,1)S(1)}, pred[32]{0:T(512)(128)(4,1)}, u32[]{:S(2)}) copy-start(pred[32]{0:T(512)(128)(4,1)} %constant.59.clone) | copy-start | bytes 100
  37.1 5.3 %copy-start.9 = (pred[32]{0:T(512)(128)(4,1)S(1)}, pred[32]{0:T(512)(128)(4,1)}, u32[]{:S(2)}) copy-start(pred[32]{0:T(512)(128)(4,1)} %constant.58.clone) | copy-start | bytes 100
  37.1 5.9 %copy-start.8 = (s32[32]{0:T(128)S(1)}, s32[32]{0:T(128)}, u32[]{:S(2)}) copy-start(s32[32]{0:T(128)} %constant.57.clone) | copy-start | bytes 388
  37.2 6.5 %copy-start.7 = (f32[32]{0:T(128)S(1)}, f32[32]{0:T(128)}, u32[]{:S(2)}) copy-start(f32[32]{0:T(128)} %param.19) | copy-start | bytes 388
  37.2 6.5 %copy-start.5 = (s32[4]{0:T(128)S(1)}, s32[4]{0:T(128)}, u32[]{:S(2)}) copy-start(s32[4]{0:T(128)} %constant.62.clone) | copy-start | bytes 52
  38.4 36.7 %collective-permute-start.4 = (bf16[2,4,64,1024]{3,2,1,0:T(8,128)(2,1)}, bf16[2,4,64,1024]{3,2,1,0:T(8,128)(2,1)}, u32[]{:S(2)}, u32[]{:S(2)}) collective-permute-start(bf16[2,4,64,1024]{3,2,1,0:T(8,128)(2,1)} %bitcast.51), channel_id=1, source_target_pairs={{0,24},{1,25},{30,6},{31,7},{32,56},{33,57},{62,38},{63,39},{64,88... | collective-permute-start | bytes 3145736 | tf_op jit(solution)/shard_map/ppermute | solution.py:217
  48.7 40.9 %copy-start = (s32[16]{0:T(128)}, s32[16]{0:T(128)S(1)}, u32[]{:S(2)}) copy-start(s32[16]{0:T(128)S(1)} %concatenate.3.flags) | copy-start | bytes 196
  89.6 1.0 copy-start.1
  90.6 22.9 %copy-start.2 = (bf16[2,64,4096]{2,1,0:T(8,128)(2,1)S(1)}, bf16[2,64,4096]{2,1,0:T(8,128)(2,1)}, u32[]{:S(2)}) copy-start(bf16[2,64,4096]{2,1,0:T(8,128)(2,1)} %copy-done.1) | copy-start | bytes 3145732
  90.6 54.8 %all-to-all-start.2 = ((bf16[32,32,1152]{2,1,0:T(8,128)(2,1)}), bf16[32,32,1152]{2,1,0:T(8,128)(2,1)S(1)}, u32[]{:S(2)}, u32[]{:S(2)}) async-start(bf16[32,32,1152]{2,1,0:T(8,128)(2,1)} %bitcast.68), calls=%async_computation.2 | async-start | bytes 4718592 | tf_op jit(solution)/shard_map/all_to_all | solution.py:290
  113.5 52.0 %collective-permute-start.8 = (bf16[2,64,4096]{2,1,0:T(8,128)(2,1)S(1)}, bf16[2,64,4096]{2,1,0:T(8,128)(2,1)}, u32[]{:S(2)}, u32[]{:S(2)}) collective-permute-start(bf16[2,64,4096]{2,1,0:T(8,128)(2,1)S(1)} %copy-done.2), channel_id=1, source_target_pairs={{24,0},{25,1},{6,30},{7,31},{56,32},{57,33},{38,62},{39,63},{88,64... | collective-permute-start | bytes 3145736 | tf_op jit(solution)/shard_map/ppermute | solution.py:289
  114.8 50.7 %collective-permute-start.7 = (bf16[2,64,4096]{2,1,0:T(8,128)(2,1)S(1)}, bf16[2,64,4096]{2,1,0:T(8,128)(2,1)}, u32[]{:S(2)}, u32[]{:S(2)}) collective-permute-start(bf16[2,64,4096]{2,1,0:T(8,128)(2,1)S(1)} %copy-done.2), channel_id=1, source_target_pairs={{6,0},{7,1},{24,30},{25,31},{38,32},{39,33},{56,62},{57,63},{70,64... | collective-permute-start | bytes 3145736 | tf_op jit(solution)/shard_map/ppermute | solution.py:289
  116.1 55.8 %collective-permute-start.6 = (bf16[2,64,4096]{2,1,0:T(8,128)(2,1)S(1)}, bf16[2,64,4096]{2,1,0:T(8,128)(2,1)}, u32[]{:S(2)}, u32[]{:S(2)}) collective-permute-start(bf16[2,64,4096]{2,1,0:T(8,128)(2,1)S(1)} %copy-done.2), channel_id=1, source_target_pairs={{8,0},{9,1},{22,30},{23,31},{40,32},{41,33},{54,62},{55,63},{72,64... | collective-permute-start | bytes 3145736 | tf_op jit(solution)/shard_map/ppermute | solution.py:289
  117.4 55.0 %collective-permute-start.5 = (bf16[2,64,4096]{2,1,0:T(8,128)(2,1)S(1)}, bf16[2,64,4096]{2,1,0:T(8,128)(2,1)}, u32[]{:S(2)}, u32[]{:S(2)}) collective-permute-start(bf16[2,64,4096]{2,1,0:T(8,128)(2,1)S(1)} %copy-done.2), channel_id=1, source_target_pairs={{2,0},{3,1},{28,30},{29,31},{34,32},{35,33},{60,62},{61,63},{66,64... | collective-permute-start | bytes 3145736 | tf_op jit(solution)/shard_map/ppermute | solution.py:289
  146.3 31.1 %collective-permute-start.15 = (f32[1,128]{1,0:T(1,128)S(1)}, f32[1,128]{1,0:T(1,128)S(1)}, u32[]{:S(2)}, u32[]{:S(2)}) collective-permute-start(f32[1,128]{1,0:T(1,128)S(1)} %get-tuple-element.19), channel_id=1, source_target_pairs={{0,224},{32,0},{64,32},{96,64},{128,96},{160,128},{192,160},{224,1... | collective-permute-start | bytes 1544 | tf_op jit(solution)/shard_map/ppermute | solution.py:304
  165.5 13.4 %collective-permute-start.14 = (f32[1,128]{1,0:T(1,128)S(1)}, f32[1,128]{1,0:T(1,128)S(1)}, u32[]{:S(2)}, u32[]{:S(2)}) collective-permute-start(f32[1,128]{1,0:T(1,128)S(1)} %get-tuple-element.19), channel_id=1, source_target_pairs={{0,192},{32,224},{64,0},{96,32},{128,64},{160,96},{192,128},{224,1... | collective-permute-start | bytes 1544 | tf_op jit(solution)/shard_map/ppermute | solution.py:304
  165.5 151.1 %collective-permute-start.13 = (f32[1,128]{1,0:T(1,128)S(1)}, f32[1,128]{1,0:T(1,128)S(1)}, u32[]{:S(2)}, u32[]{:S(2)}) collective-permute-start(f32[1,128]{1,0:T(1,128)S(1)} %get-tuple-element.19), channel_id=1, source_target_pairs={{0,160},{32,192},{64,224},{96,0},{128,32},{160,64},{192,96},{224,1... | collective-permute-start | bytes 1544 | tf_op jit(solution)/shard_map/ppermute | solution.py:304
  171.9 144.7 %collective-permute-start.12 = (f32[1,128]{1,0:T(1,128)S(1)}, f32[1,128]{1,0:T(1,128)S(1)}, u32[]{:S(2)}, u32[]{:S(2)}) collective-permute-start(f32[1,128]{1,0:T(1,128)S(1)} %get-tuple-element.19), channel_id=1, source_target_pairs={{0,128},{32,160},{64,192},{96,224},{128,0},{160,32},{192,64},{224,... | collective-permute-start | bytes 1544 | tf_op jit(solution)/shard_map/ppermute | solution.py:304
  172.4 144.2 %collective-permute-start.11 = (f32[1,128]{1,0:T(1,128)S(1)}, f32[1,128]{1,0:T(1,128)S(1)}, u32[]{:S(2)}, u32[]{:S(2)}) collective-permute-start(f32[1,128]{1,0:T(1,128)S(1)} %get-tuple-element.19), channel_id=1, source_target_pairs={{0,96},{32,128},{64,160},{96,192},{128,224},{160,0},{192,32},{224,... | collective-permute-start | bytes 1544 | tf_op jit(solution)/shard_map/ppermute | solution.py:304
  177.4 139.2 %collective-permute-start.10 = (f32[1,128]{1,0:T(1,128)S(1)}, f32[1,128]{1,0:T(1,128)S(1)}, u32[]{:S(2)}, u32[]{:S(2)}) collective-permute-start(f32[1,128]{1,0:T(1,128)S(1)} %get-tuple-element.19), channel_id=1, source_target_pairs={{0,64},{32,96},{64,128},{96,160},{128,192},{160,224},{192,0},{224,... | collective-permute-start | bytes 1544 | tf_op jit(solution)/shard_map/ppermute | solution.py:304
  178.9 137.8 %collective-permute-start.9 = (f32[1,128]{1,0:T(1,128)S(1)}, f32[1,128]{1,0:T(1,128)S(1)}, u32[]{:S(2)}, u32[]{:S(2)}) collective-permute-start(f32[1,128]{1,0:T(1,128)S(1)} %get-tuple-element.19), channel_id=1, source_target_pairs={{0,32},{32,64},{64,96},{96,128},{128,160},{160,192},{192,224},{224... | collective-permute-start | bytes 1544 | tf_op jit(solution)/shard_map/ppermute | solution.py:304
  313.2 11.8 %all-to-all-start.3 = ((bf16[8,16,1024]{2,1,0:T(8,128)(2,1)}), bf16[8,16,1024]{2,1,0:T(8,128)(2,1)S(1)}, u32[]{:S(2)}, u32[]{:S(2)}) async-start(bf16[8,16,1024]{2,1,0:T(8,128)(2,1)} %get-tuple-element.18), calls=%async_computation.3 | async-start | bytes 524288 | tf_op jit(solution)/shard_map/all_to_all | solution.py:305
  (1 other events, 0.7 us)

commit v2 on v0

v2 whole, which is shorter than its diff:
```python
import jax
import jax.numpy as jnp
from jax import lax
from jax.experimental import pallas as pl
from jax.experimental.pallas import tpu as pltpu
from jax.sharding import Mesh
from jax.sharding import PartitionSpec as P

CTX = ("x", "yh", "yl", "c")
CHIP = ("x", "yh", "yl")
IMG = ("x", "yh")
NLAT = 64
HEADS = 32
HS = 128
GRP = 8
BATCH = 4
COLS = GRP * HS
WIDE = COLS + 128
QUART = 16
SCALE = HS**-0.5
BF = jnp.bfloat16
F32 = jnp.float32

NEAR0 = (2, 8, 6, 24)
NEAR1 = (28, 22, 6, 24)
WORKER0 = [NEAR0[j % 4] + j // 4 for j in range(8)]
WORKER1 = [NEAR1[j % 4] + j // 4 for j in range(8)]
STEP0 = (0, 1, 2, 3)
STEP1 = (0, 1, 3, 2)


def block_pairs(s):
    a, b = NEAR0[STEP0[s]], NEAR1[STEP1[s]]
    return [(0, a), (1, a + 1), (30, b), (31, b + 1)]


def latent_pairs(s):
    first = [(4 * j + s, WORKER0[j]) for j in range(8)]
    second = [(4 * j + (s + 1) % 4, WORKER1[j]) for j in range(8) if WORKER1[j] != WORKER0[j]]
    return first + second


def back(pairs):
    return [(b, a) for a, b in pairs]


def nt(a, b):
    return lax.dot_general(a, b, (((1,), (1,)), ((), ())), preferred_element_type=F32)


def tn(a, b):
    return lax.dot_general(a, b, (((0,), (0,)), ((), ())), preferred_element_type=F32)


def nn(a, b):
    return lax.dot_general(a, b, (((1,), (0,)), ((), ())), preferred_element_type=F32)


def pick(cases, default):
    out = jnp.int32(default)
    for cond, value in cases:
        out = jnp.where(cond, jnp.int32(value), out)
    return out


def step_block(ctx, s):
    return jnp.where(ctx >= 16, jnp.int32(STEP1[s]), jnp.int32(STEP0[s]))


def chunk_kernel(src, dst):
    for i in range(8):
        dst[i] = src[:, i * COLS : (i + 1) * COLS]


def pack_kernel(ctx_ref, q, g, d0, d1, d2, d3, buf, sems):
    ctx = ctx_ref[0]

    @pl.when((ctx < 2) | (ctx >= 30))
    def _():
        loads = []
        for s in range(4):
            rows = pl.ds(pl.multiple_of(step_block(ctx, s) * NLAT, NLAT), NLAT)
            for a, ref in enumerate((q, g)):
                copy = pltpu.make_async_copy(ref.at[rows], buf.at[s, a], sems.at[0, s, a])
                copy.start()
                loads.append(copy)
        stores = []
        for s, d in enumerate((d0, d1, d2, d3)):
            for a in range(2):
                loads[2 * s + a].wait()
                copy = pltpu.make_async_copy(buf.at[s, a], d.at[a], sems.at[1, s, a])
                copy.start()
                stores.append(copy)
        for copy in stores:
            copy.wait()


def spread_kernel(ids, got, dst):
    sel = got[ids[1]]
    for p in range(16):
        dst[p] = sel


def heads_side_by_side(items):
    s = [nt(k, q) for q, g, k, v, t, keep in items]
    gf = [g.astype(F32) for q, g, k, v, t, keep in items]
    dm = [(it[4] * f).astype(BF) for it, f in zip(items, gf)]
    dp = [nt(it[3], d) for it, d in zip(items, dm)]
    e = [jnp.exp((x - jnp.max(x, axis=0, keepdims=True)) * SCALE) for x in s]
    p = [x * (it[5] / jnp.sum(x, axis=0, keepdims=True)) for it, x in zip(items, e)]
    pb = [x.astype(BF) for x in p]
    mix = [tn(x, it[3]) for it, x in zip(items, pb)]
    inner = [jnp.sum(a * b, axis=0, keepdims=True) for a, b in zip(p, dp)]
    ds = [(a * (b - c)).astype(BF) for a, b, c in zip(p, dp, inner)]
    dv = [nn(a, b) for a, b in zip(pb, dm)]
    dq = [tn(a, it[2]) * SCALE for it, a in zip(items, ds)]
    dk = [nn(a, it[0]) * SCALE for it, a in zip(items, ds)]
    gs = [jnp.sum(a * b, axis=0, keepdims=True) for a, b in zip(gf, mix)]
    out = [(it[4] * m).astype(BF) for it, m in zip(items, mix)]
    return list(zip(out, [x.astype(BF) for x in dq], dk, dv, gs))


def split3(x):
    hi = x.astype(BF).astype(F32)
    mid = (x - hi).astype(BF).astype(F32)
    lo = x - hi - mid
    row = lax.broadcasted_iota(jnp.int32, (16, x.shape[1]), 0)
    val = jnp.where(row == 0, hi, jnp.where(row == 1, mid, jnp.where(row == 2, lo, 0.0)))
    return val.astype(BF)


def attention_kernel(
    ids, tg, q, g, mine, other, l0, l1, l2, l3, x0, x1, x2, x3,
    o, dq, xo, pay, opay, y0, y1, y2, y3, gate, xbuf, gacc, sem,
):
    c = pl.program_id(0)
    tokens = q.shape[0]
    width = o.shape[1] * 4
    ctx, lead = ids[0], ids[1]
    latents = (l0, l1, l2, l3)
    grads = (y0, y1, y2, y3)
    from0 = [(ctx == WORKER0[j]) & (lead > j) for j in range(8)]
    from1 = [(ctx == WORKER1[j]) & (lead < j) for j in range(8)]
    cases = [(from0[j], STEP0.index(j % 4)) for j in range(8)]
    cases += [(from1[j], STEP1.index(j % 4)) for j in range(8)]
    source = pick(cases, -1)

    @pl.when(c == 0)
    def _():
        gacc[...] = jnp.zeros_like(gacc)
        for n, x in enumerate((x0, x1, x2, x3)):

            @pl.when(source == n)
            def _():
                copy = pltpu.make_async_copy(x, xbuf, sem)
                copy.start()
                copy.wait()

    block = lax.broadcasted_iota(jnp.int32, (1, tokens), 1) // (tokens // 4)
    keep = jnp.zeros((1, tokens), F32)
    for b in range(4):
        keep = jnp.where((block == b) & (ids[2 + b] == lead), 1.0, keep)
    ones = jnp.ones((1, NLAT), F32)

    def work(extra):
        for first in range(0, GRP, BATCH):
            items, heads = [], range(first, first + BATCH)
            for n in heads:
                cols = slice(n * HS, n * HS + HS)
                t = tg[c * GRP + n]
                k = [ref[0, 0, y, :, cols] for ref in (mine, other) for y in range(2)]
                v = [ref[1, 0, y, :, cols] for ref in (mine, other) for y in range(2)]
                k, v = jnp.concatenate(k, axis=0), jnp.concatenate(v, axis=0)
                items.append((q[:, cols], g[:, cols], k, v, t, keep))
                if extra:
                    wk = pl.ds(pl.multiple_of(c * COLS + n * HS, HS), HS)
                    wv = pl.ds(pl.multiple_of(width + c * COLS + n * HS, HS), HS)
                    k = jnp.concatenate([ref[:, wk] for ref in latents], axis=0)
                    v = jnp.concatenate([ref[:, wv] for ref in latents], axis=0)
                    items.append((xbuf[0, :, wk], xbuf[1, :, wk], k, v, t, ones))
            done = heads_side_by_side(items)
            for n in heads:
                cols = slice(n * HS, n * HS + HS)
                ob, dqb, dk, dv, gs = done.pop(0)
                o[:, cols] = ob
                dq[:, cols] = dqb
                for kv, d in enumerate((dk, dv)):
                    for y in range(2):
                        at = kv * 8 + c * 2 + y
                        pay[at, :, cols] = d[y * QUART : (y + 1) * QUART]
                        opay[at, :, cols] = d[(2 + y) * QUART : (3 + y) * QUART].astype(BF)
                if extra:
                    wk = pl.ds(pl.multiple_of(c * COLS + n * HS, HS), HS)
                    wv = pl.ds(pl.multiple_of(width + c * COLS + n * HS, HS), HS)
                    ob, dqb, dk, dv, gx = done.pop(0)
                    xo[0, :, cols] = ob
                    xo[1, :, cols] = dqb
                    for s in range(4):
                        grads[s][:, wk] = dk[s * QUART : (s + 1) * QUART].astype(BF)
                        grads[s][:, wv] = dv[s * QUART : (s + 1) * QUART].astype(BF)
                    gs = gs + gx
                gacc[pl.ds(c * GRP + n, 1), :] = gs

    @pl.when(source >= 0)
    def _():
        work(True)

    @pl.when(source < 0)
    def _():
        work(False)

    @pl.when(c == pl.num_programs(0) - 1)
    def _():
        gs = jnp.sum(gacc[...].T, axis=0, keepdims=True)
        gate[...] = gs
        opay[16] = jnp.zeros((QUART, COLS), BF)
        opay[16, :, 0:HS] = split3(gs)


def pair_kernel(pay, got, gate, dst):
    for d in range(16):
        dst[d, :, 0:COLS] = (pay[d] + got[d].astype(F32)).astype(BF)
    other = jnp.sum(got[16, :, 0:HS].astype(F32), axis=0, keepdims=True)
    val = split3(gate[...] + other)
    for d in range(16):
        dst[d, :, COLS:WIDE] = val


def collect_kernel(got, dst, gate):
    total = got[0].astype(F32)
    for p in range(1, 16):
        total += got[p].astype(F32)
    gate[...] = jnp.sum(total[:, COLS:WIDE], axis=0, keepdims=True)
    val = total[:, 0:COLS].astype(BF)
    for j in range(8):
        dst[j] = val


def assemble_kernel(ids, got, y0, y1, y2, y3, dst):
    ctx, lead = ids[0], ids[1]
    image, quarter = ctx // 4, ctx % 4
    shared = (image % 4) >= 2
    step = jnp.where((image < lead) | shared, quarter, (quarter + 3) % 4)

    @pl.when(image == lead)
    def _():
        for i in range(8):
            dst[:, i * COLS : (i + 1) * COLS] = got[i]

    for s, y in enumerate((y0, y1, y2, y3)):

        @pl.when((image != lead) & (step == s))
        def _():
            dst[...] = y[...]


def merge_kernel(ids, o_in, dq_in, r0, r1, r2, r3, o, dq, buf, sems):
    del o_in, dq_in
    ctx, lead = ids[0], ids[1]

    @pl.when((ctx < 2) | (ctx >= 30))
    def _():
        for s, r in enumerate((r0, r1, r2, r3)):
            odd = ids[2 + step_block(ctx, s)] != lead

            @pl.when(odd)
            def _():
                pltpu.make_async_copy(r, buf.at[s], sems.at[s, 0]).start()

        for s, r in enumerate((r0, r1, r2, r3)):
            k = step_block(ctx, s)
            odd = ids[2 + k] != lead
            rows = pl.ds(pl.multiple_of(k * NLAT, NLAT), NLAT)

            @pl.when(odd)
            def _():
                pltpu.make_async_copy(r, buf.at[s], sems.at[s, 0]).wait()
                pltpu.make_async_copy(buf.at[s, 0], o.at[rows], sems.at[s, 1]).start()
                pltpu.make_async_copy(buf.at[s, 1], dq.at[rows], sems.at[s, 2]).start()

        for s in range(4):
            k = step_block(ctx, s)
            odd = ids[2 + k] != lead
            rows = pl.ds(pl.multiple_of(k * NLAT, NLAT), NLAT)

            @pl.when(odd)
            def _():
                pltpu.make_async_copy(buf.at[s, 0], o.at[rows], sems.at[s, 1]).wait()
                pltpu.make_async_copy(buf.at[s, 1], dq.at[rows], sems.at[s, 2]).wait()


VM = pl.BlockSpec(memory_space=pltpu.VMEM)
SM = pl.BlockSpec(memory_space=pltpu.SMEM)
ANY = pl.BlockSpec(memory_space=pl.ANY)
LIMIT = 48 * 1024 * 1024


def shape(*dims, dtype=BF):
    return jax.ShapeDtypeStruct(dims, dtype)


def call(kernel, name, out_shape, in_specs, out_specs, **more):
    params = pltpu.CompilerParams(vmem_limit_bytes=LIMIT)
    return pl.pallas_call(
        kernel,
        name=name,
        out_shape=out_shape,
        in_specs=in_specs,
        out_specs=out_specs,
        compiler_params=params,
        **more,
    )


def body(queries, latent_kv, media, gate, grad_out):
    q, g, kv_rows = queries[0], grad_out[0], latent_kv[0]
    tokens, width = q.shape
    ctx = lax.axis_index(CTX)
    core = lax.axis_index("c")
    images = media[0]
    partner = lax.ppermute(images, "c", [(0, 1), (1, 0)])
    last = jnp.where(core == 0, partner, images)[3]
    first = jnp.where(core == 0, images, partner)[0]
    lead = jnp.where(ctx < 2, last, first)
    ids = jnp.concatenate([ctx[None], lead[None], images]).astype(jnp.int32)

    chunks = call(chunk_kernel, "chunk", shape(8, QUART, COLS), [VM], VM)(kv_rows)
    mixed = lax.all_to_all(chunks, IMG, 0, 0, tiled=True)
    packed = call(
        pack_kernel,
        "pack",
        [shape(2, NLAT, width)] * 4,
        [SM, ANY, ANY],
        [ANY] * 4,
        scratch_shapes=[
            pltpu.VMEM((4, 2, NLAT, width), BF),
            pltpu.SemaphoreType.DMA((2, 4, 2)),
        ],
    )(ctx[None].astype(jnp.int32), q, g)
    sent = [lax.ppermute(packed[s], CTX, block_pairs(s)) for s in range(4)]
    lent = [lax.ppermute(kv_rows, CTX, latent_pairs(s)) for s in range(4)]

    spread = call(spread_kernel, "spread", shape(16, QUART, COLS), [SM, VM], VM)(ids, mixed)
    mine = lax.all_to_all(spread, CHIP, 0, 0, tiled=True).reshape(2, 4, 2, QUART, COLS)
    other = lax.ppermute(mine, "c", [(0, 1), (1, 0)])

    tanh_gate = jnp.tanh(gate)
    wide = pl.BlockSpec((tokens, COLS), lambda c: (0, c))
    half = pl.BlockSpec((2, 1, 2, QUART, COLS), lambda c: (0, c, 0, 0, 0))
    o, dq, xo, pay, opay, y0, y1, y2, y3, gpart = call(
        attention_kernel,
        "attention",
        [
            shape(tokens, width),
            shape(tokens, width),
            shape(2, NLAT, width),
            shape(16, QUART, COLS, dtype=F32),
            shape(17, QUART, COLS),
            *[shape(QUART, 2 * width)] * 4,
            shape(1, HS, dtype=F32),
        ],
        [SM, SM, wide, wide, half, half, *[VM] * 4, *[ANY] * 4],
        [wide, wide, pl.BlockSpec((2, NLAT, COLS), lambda c: (0, 0, c)), *[VM] * 7],
        grid=(4,),
        scratch_shapes=[
            pltpu.VMEM((2, NLAT, width), BF),
            pltpu.VMEM((HS, HS), F32),
            pltpu.SemaphoreType.DMA,
        ],
    )(ids, tanh_gate, q, g, mine, other, *lent, *sent)

    theirs = lax.ppermute(opay, "c", [(0, 1), (1, 0)])
    paired = call(pair_kernel, "pair", shape(16, QUART, WIDE), [VM, VM, VM], VM)(
        pay, theirs, gpart
    )
    parts = lax.all_to_all(paired, CHIP, 0, 0, tiled=True)
    ready = [lax.ppermute(xo, CTX, back(block_pairs(s))) for s in range(4)]
    owned = [
        lax.ppermute(y, CTX, back(latent_pairs(s))) for s, y in enumerate((y0, y1, y2, y3))
    ]
    summed, gates = call(
        collect_kernel,
        "collect",
        [shape(8, QUART, COLS), shape(1, HS, dtype=F32)],
        [VM],
        [VM, VM],
    )(parts)
    final = lax.all_to_all(summed, IMG, 0, 0, tiled=True)
    for n in (1, 2, 4):
        gates = gates + lax.ppermute(gates, "dp", [(s, s ^ n) for s in range(8)])
    latent_grad = call(
        assemble_kernel, "assemble", shape(QUART, 2 * width), [SM, *[VM] * 5], VM
    )(ids, final, *owned)
    o, dq = call(
        merge_kernel,
        "merge",
        [shape(tokens, width)] * 2,
        [SM, *[ANY] * 6],
        [ANY, ANY],
        scratch_shapes=[
            pltpu.VMEM((4, 2, NLAT, width), BF),
            pltpu.SemaphoreType.DMA((4, 3)),
        ],
        input_output_aliases={1: 0, 2: 1},
    )(ids, o, dq, *ready)
    gate_grad = (1.0 - tanh_gate * tanh_gate) * gates[0, :HEADS]
    return o[None], dq[None], latent_grad[None], gate_grad


def solution(mesh):
    fine = Mesh(mesh.devices.reshape(8, 4, 2, 2, 2), ("dp", "x", "yh", "yl", "c"))
    wide = P("dp", CTX, None)
    return jax.shard_map(
        body,
        mesh=fine,
        in_specs=(wide, wide, P("dp", CTX), P(), wide),
        out_specs=(wide, wide, wide, P()),
        check_vma=False,
    )
```

time: 364 us -> 150 us (0.41)
  waiting for transfers between devices: 162 us -> 33.3 us
  starting transfers between devices: 0.08 us -> 64.4 us
  local copies, waits for them, and re-layouts: 61.8 us -> 3.55 us
  blocking collectives: 76.3 us -> 30.1 us
  matrix products: 27.2 us -> 0 us
  other arithmetic: 21.2 us -> 0.61 us
  Pallas kernels: 0 us -> 15.4 us
  between operations: 14.2 us -> 1.53 us
    reduce_scatter x1 -> x0, waiting for transfers between devices: 104 us -> none  [body(): lax.psum_scatter(every, 'ctx', scatter_dimension=0, tiled=True)]
    psum x1 -> x0, blocking collectives: 76.3 us -> none  [body(): gate_sum = lax.psum(gate_part, ('dp', 'ctx'))]
    all_gather x1 -> x0, waiting for transfers between devices: 57.8 us -> none  [body(): gathered = lax.all_gather(latent_kv, 'ctx', axis=1, tiled=True)[0]]
    ppermute x0 -> x22, starting transfers between devices: none -> 39.3 us  [the longest x3 10.8 us: body(): gates = gates + lax.ppermute(gates, 'dp', [(s, s ^ n) for s in range(8)])]
    all_to_all x0 -> x1, blocking collectives: none -> 30.1 us  [body(): parts = lax.all_to_all(paired, CHIP, 0, 0, tiled=True)]
    dot_general x7 -> x0, matrix products: 27.2 us -> none  [the longest x1 12.8 us: image_terms(): jnp.einsum('ib,bjc->ijc', onehot, terms, precision=lax.Precision.HIGHEST)]
    reshape x6 -> x0, local copies, waits for them, and re-layouts: 25.8 us -> none  [the longest x2 9.65 us: body(): key_part.reshape(blocks, NLAT, width)]
    all_to_all x0 -> x3, starting transfers between devices: none -> 25.1 us  [the longest x1 12.2 us: body(): final = lax.all_to_all(summed, IMG, 0, 0, tiled=True)]
  transfers between devices with their start and end apart: 2 -> 25, of which waited for: 2 -> 6; matrix products, arithmetic and copies ran while one was open for 6% -> 1% of each run, Pallas kernels for 0% -> 2%
where the time goes in v2:
time: 150 us; the launch traced here: 149 us
  starting transfers between devices  64.4 us (43%)
  waiting for transfers between devices  33.3 us (22%)
  blocking collectives  30.1 us (20%)
  Pallas kernels  15.4 us (10%)
  local copies, waits for them, and re-layouts  3.55 us (2%)
  between operations  1.53 us (1%)
    all_to_all x1, blocking collectives, body(): parts = lax.all_to_all(paired, CHIP, 0, 0, tiled=True)  30.1 us
    ppermute x4, waiting for transfers between devices, body(): lent = [lax.ppermute(kv_rows, CTX, latent_pairs(s)) for s in range(4)]  12.3 us
    all_to_all x1, starting transfers between devices, body(): final = lax.all_to_all(summed, IMG, 0, 0, tiled=True)  12.2 us
    ppermute x3, starting transfers between devices, body(): gates = gates + lax.ppermute(gates, 'dp', [(s, s ^ n) for s in range(8)])  10.8 us
    all_to_all x1, waiting for transfers between devices, body(): lax.all_to_all(spread, CHIP, 0, 0, tiled=True).reshape(2, 4, 2, QUART, COLS)  10.6 us
    pallas_call x1, Pallas kernels, body(): call(attention_kernel, 'attention', [shape(tokens, width), shape(tokens,...  10.3 us
    ppermute x4, starting transfers between devices, body(): lent = [lax.ppermute(kv_rows, CTX, latent_pairs(s)) for s in range(4)]  9.44 us
    all_to_all x1, starting transfers between devices, body(): lax.all_to_all(spread, CHIP, 0, 0, tiled=True).reshape(2, 4, 2, QUART, COLS)  8.08 us
  transfers between devices with their start and end apart: 25, of which 6 were waited for; matrix products, arithmetic and copies ran while one was open for 1% of the time, Pallas kernels for 2%

profile of v2, /device:TPU:24, one launch (start us, length us, event | category | flops | bytes accessed | tf_op | source)
XLA Modules:
  0.0 148.9 jit_solution(10594734297619132530)
XLA Ops:
  0.6 1.3 collective-permute-start.5
  1.9 3.1 %collective-permute-start.4 = (bf16[16,8192]{1,0:T(8,128)(2,1)}, bf16[16,8192]{1,0:T(8,128)(2,1)S(1)}, u32[]{:S(2)}, u32[]{:S(2)}) collective-permute-start(bf16[16,8192]{1,0:T(8,128)(2,1)} %bitcast.20), channel_id=1, source_target_pairs={{2,2},{6,8},{10,6},{14,24},{18,3},{22,9},{26,7},{30,25},{3,28},{7,... | collective-permute-start | bytes 786440 | tf_op jit(solution)/shard_map/ppermute | solution.py:341
  5.0 3.8 %collective-permute-start.3 = (bf16[16,8192]{1,0:T(8,128)(2,1)}, bf16[16,8192]{1,0:T(8,128)(2,1)S(1)}, u32[]{:S(2)}, u32[]{:S(2)}) collective-permute-start(bf16[16,8192]{1,0:T(8,128)(2,1)} %bitcast.21), channel_id=1, source_target_pairs={{1,2},{5,8},{9,6},{13,24},{17,3},{21,9},{25,7},{29,25},{2,28},{6,2... | collective-permute-start | bytes 786440 | tf_op jit(solution)/shard_map/ppermute | solution.py:341
  10.6 4.8 %all-to-all-start = ((bf16[8,16,1024]{2,1,0:T(8,128)(2,1)}), bf16[8,16,1024]{2,1,0:T(8,128)(2,1)S(1)}, u32[]{:S(2)}, u32[]{:S(2)}) async-start(bf16[8,16,1024]{2,1,0:T(8,128)(2,1)} %chunk.1), calls=%async_computation | async-start | bytes 524288 | tf_op jit(solution)/shard_map/all_to_all | solution.py:328
  15.6 1.0 copy-done.3
  17.5 1.6 %collective-permute-start.6 = (bf16[2,64,4096]{2,1,0:T(8,128)(2,1)}, bf16[2,64,4096]{2,1,0:T(8,128)(2,1)}, u32[]{:S(2)}, u32[]{:S(2)}) collective-permute-start(bf16[2,64,4096]{2,1,0:T(8,128)(2,1)} %get-tuple-element.22), channel_id=1, source_target_pairs={{0,2},{1,3},{30,28},{31,29},{32,34},{33,35},{62,60},{63,61},{64,66... | collective-permute-start | bytes 3145736 | tf_op jit(solution)/shard_map/ppermute | solution.py:340
  19.1 1.6 %collective-permute-start.7 = (bf16[2,64,4096]{2,1,0:T(8,128)(2,1)}, bf16[2,64,4096]{2,1,0:T(8,128)(2,1)}, u32[]{:S(2)}, u32[]{:S(2)}) collective-permute-start(bf16[2,64,4096]{2,1,0:T(8,128)(2,1)} %copy-done.4), channel_id=1, source_target_pairs={{0,8},{1,9},{30,22},{31,23},{32,40},{33,41},{62,54},{63,55},{64,72... | collective-permute-start | bytes 3145736 | tf_op jit(solution)/shard_map/ppermute | solution.py:340
  22.1 1.3 collective-permute-start.8
  23.4 1.3 collective-permute-start.9
  24.8 5.5 %all-to-all-done.got = bf16[8,16,1024]{2,1,0:T(8,128)(2,1)S(1)} async-done(((bf16[8,16,1024]{2,1,0:T(8,128)(2,1)}), bf16[8,16,1024]{2,1,0:T(8,128)(2,1)S(1)}, u32[]{:S(2)}, u32[]{:S(2)}) %all-to-all-start) | async-done | bytes 262176 | tf_op jit(solution)/shard_map/all_to_all | solution.py:328
  30.2 1.4 spread.1
  31.6 8.1 %all-to-all-start.1 = ((bf16[16,16,1024]{2,1,0:T(8,128)(2,1)}), bf16[16,16,1024]{2,1,0:T(8,128)(2,1)S(1)}, u32[]{:S(2)}, u32[]{:S(2)}) async-start(bf16[16,16,1024]{2,1,0:T(8,128)(2,1)} %spread.1), calls=%async_computation.1 | async-start | bytes 1048576 | tf_op jit(solution)/shard_map/all_to_all | solution.py:344
  39.7 1.3 collective-permute-start.2
  41.0 12.3 %collective-permute-done.2.l0 = bf16[16,8192]{1,0:T(8,128)(2,1)S(1)} collective-permute-done((bf16[16,8192]{1,0:T(8,128)(2,1)S(1)}, bf16[16,8192]{1,0:T(8,128)(2,1)S(1)}, u32[]{:S(2)}, u32[]{:S(2)}) %collective-permute-start.2) | collective-permute-done | bytes 262176 | tf_op jit(solution)/shard_map/ppermute | solution.py:341
  53.3 10.6 %all-to-all-done.1 = bf16[16,16,1024]{2,1,0:T(8,128)(2,1)S(1)} async-done(((bf16[16,16,1024]{2,1,0:T(8,128)(2,1)}), bf16[16,16,1024]{2,1,0:T(8,128)(2,1)S(1)}, u32[]{:S(2)}, u32[]{:S(2)}) %all-to-all-start.1) | async-done | bytes 524320 | tf_op jit(solution)/shard_map/all_to_all | solution.py:344
  64.0 1.9 %collective-permute-done.1.other = bf16[2,4,2,16,1024]{4,3,2,1,0:T(8,128)(2,1)S(1)} collective-permute-done((bf16[2,4,2,16,1024]{4,3,2,1,0:T(8,128)(2,1)S(1)}, bf16[2,4,2,16,1024]{4,3,2,1,0:T(8,128)(2,1)S(1)}, u32[]{:S(2)}, u32[]{:S(2)}) %collective-permute-start.1) | collective-permute-done | bytes 524320 | tf_op jit(solution)/shard_map/ppermute | solution.py:345
  65.8 10.3 %attention.1 = (bf16[256,4096]{1,0:T(8,128)(2,1)}, bf16[256,4096]{1,0:T(8,128)(2,1)}, bf16[2,64,4096]{2,1,0:T(8,128)(2,1)}, f32[16,16,1024]{2,1,0:T(8,128)S(1)},...) custom-call(s32[6]{0:T(128)S(1)} %pad_add_fusion.ids, ...), custom_call_target="tpu_custom_call" | custom-call | tf_op jit(solution)/shard_map/attention/pallas_call | solution.py:350
  76.4 1.3 collective-permute-start.13
  77.8 1.4 collective-permute-start.12
  79.9 1.6 %collective-permute-start.10 = (bf16[2,64,4096]{2,1,0:T(8,128)(2,1)}, bf16[2,64,4096]{2,1,0:T(8,128)(2,1)}, u32[]{:S(2)}, u32[]{:S(2)}) collective-permute-start(bf16[2,64,4096]{2,1,0:T(8,128)(2,1)} %get-tuple-element.28), channel_id=1, source_target_pairs={{2,0},{3,1},{28,30},{29,31},{34,32},{35,33},{60,62},{61,63},{66,64... | collective-permute-start | bytes 3145736 | tf_op jit(solution)/shard_map/ppermute | solution.py:377
  81.6 30.1 %all_to_all.20.got = bf16[16,16,1152]{2,1,0:T(8,128)(2,1)S(1)} all-to-all(bf16[16,16,1152]{2,1,0:T(8,128)(2,1)S(1)} %pair.1), channel_id=1, replica_groups=mesh['dp'=8,'x'=4,'yh'=2,'yl'=2,'c'=2] {'x','yh','yl'}, dimensions={0} | all-to-all | bytes 1179648 | tf_op jit(solution)/shard_map/all_to_all | solution.py:376
  111.8 2.0 %collective-permute-start.19 = (f32[1,128]{1,0:T(1,128)S(1)}, f32[1,128]{1,0:T(1,128)S(1)}, u32[]{:S(2)}, u32[]{:S(2)}) collective-permute-start(f32[1,128]{1,0:T(1,128)S(1)} %get-tuple-element.39), channel_id=1, source_target_pairs={{0,32},{32,0},{64,96},{96,64},{128,160},{160,128},{192,224},{224,1... | collective-permute-start | bytes 1544 | tf_op jit(solution)/shard_map/ppermute | solution.py:390
  113.8 1.6 %collective-permute-done.19 = f32[1,128]{1,0:T(1,128)S(1)} collective-permute-done((f32[1,128]{1,0:T(1,128)S(1)}, f32[1,128]{1,0:T(1,128)S(1)}, u32[]{:S(2)}, u32[]{:S(2)}) %collective-permute-start.19) | collective-permute-done | bytes 544 | tf_op jit(solution)/shard_map/ppermute | solution.py:390
  115.4 3.3 %collective-permute-start.20 = (f32[1,128]{1,0:T(1,128)S(1)}, f32[1,128]{1,0:T(1,128)S(1)}, u32[]{:S(2)}, u32[]{:S(2)}) collective-permute-start(f32[1,128]{1,0:T(1,128)S(1)} %add.21), channel_id=1, source_target_pairs={{0,64},{32,96},{64,0},{96,32},{128,192},{160,224},{192,128},{224,1... | collective-permute-start | bytes 1544 | tf_op jit(solution)/shard_map/ppermute | solution.py:390
  118.7 2.0 %collective-permute-start.15 = (bf16[16,8192]{1,0:T(8,128)(2,1)}, bf16[16,8192]{1,0:T(8,128)(2,1)}, u32[]{:S(2)}, u32[]{:S(2)}) collective-permute-start(bf16[16,8192]{1,0:T(8,128)(2,1)} %get-tuple-element.35), channel_id=1, source_target_pairs={{2,0},{8,4},{6,8},{24,12},{3,16},{9,20},{7,24},{25,28},{28,1},{22,... | collective-permute-start | bytes 786440 | tf_op jit(solution)/shard_map/ppermute | solution.py:379
  120.7 1.9 %collective-permute-start.16 = (bf16[16,8192]{1,0:T(8,128)(2,1)}, bf16[16,8192]{1,0:T(8,128)(2,1)}, u32[]{:S(2)}, u32[]{:S(2)}) collective-permute-start(bf16[16,8192]{1,0:T(8,128)(2,1)} %get-tuple-element.36), channel_id=1, source_target_pairs={{2,1},{8,5},{6,9},{24,13},{3,17},{9,21},{7,25},{25,29},{28,2},{22,... | collective-permute-start | bytes 786440 | tf_op jit(solution)/shard_map/ppermute | solution.py:379
  122.6 1.9 %collective-permute-start.17 = (bf16[16,8192]{1,0:T(8,128)(2,1)}, bf16[16,8192]{1,0:T(8,128)(2,1)}, u32[]{:S(2)}, u32[]{:S(2)}) collective-permute-start(bf16[16,8192]{1,0:T(8,128)(2,1)} %get-tuple-element.37), channel_id=1, source_target_pairs={{2,2},{8,6},{6,10},{24,14},{3,18},{9,22},{7,26},{25,30},{28,3},{22... | collective-permute-start | bytes 786440 | tf_op jit(solution)/shard_map/ppermute | solution.py:379
  124.6 2.0 %collective-permute-start.18 = (bf16[16,8192]{1,0:T(8,128)(2,1)}, bf16[16,8192]{1,0:T(8,128)(2,1)}, u32[]{:S(2)}, u32[]{:S(2)}) collective-permute-start(bf16[16,8192]{1,0:T(8,128)(2,1)} %get-tuple-element.38), channel_id=1, source_target_pairs={{2,3},{8,7},{6,11},{24,15},{3,19},{9,23},{7,27},{25,31},{28,0},{22... | collective-permute-start | bytes 786440 | tf_op jit(solution)/shard_map/ppermute | solution.py:379
  126.6 12.2 %all-to-all-start.3 = ((bf16[8,16,1024]{2,1,0:T(8,128)(2,1)}), bf16[8,16,1024]{2,1,0:T(8,128)(2,1)S(1)}, u32[]{:S(2)}, u32[]{:S(2)}) async-start(bf16[8,16,1024]{2,1,0:T(8,128)(2,1)} %copy-done.2), calls=%async_computation.3 | async-start | bytes 524288 | tf_op jit(solution)/shard_map/all_to_all | solution.py:388
  138.8 5.5 %collective-permute-start.21 = (f32[1,128]{1,0:T(1,128)S(1)}, f32[1,128]{1,0:T(1,128)S(1)}, u32[]{:S(2)}, u32[]{:S(2)}) collective-permute-start(f32[1,128]{1,0:T(1,128)S(1)} %add.22), channel_id=1, source_target_pairs={{0,128},{32,160},{64,192},{96,224},{128,0},{160,32},{192,64},{224,... | collective-permute-start | bytes 1544 | tf_op jit(solution)/shard_map/ppermute | solution.py:390
  145.0 1.4 collective-permute-done.21
  146.9 2.0 %assemble.1 = bf16[16,8192]{1,0:T(8,128)(2,1)} custom-call(s32[6]{0:T(128)S(1)} %pad_add_fusion.ids, bf16[8,16,1024]{2,1,0:T(8,128)(2,1)S(1)} %all-to-all-done.3.got, bf16[16,8192]{1,0:T(8,128)(2,1)} %collective-permute-done.15.y0, bf16[16,8192]{1,0:T(8,128)(2,1)} %collective-permute-done.16.y1, bf16[16,8192]{1,0:T(8,128)(2,1)} %collective-permute-done.17.y2, ...), custom_call_target="tpu_custom_call" | custom-call | tf_op jit(solution)/shard_map/assemble/pallas_call | solution.py:391
  (49 shorter events, 6.0 us)
Async XLA Ops:
  0.6 21.4 %collective-permute-start.5 = (bf16[16,8192]{1,0:T(8,128)(2,1)}, bf16[16,8192]{1,0:T(8,128)(2,1)S(1)}, u32[]{:S(2)}, u32[]{:S(2)}) collective-permute-start(bf16[16,8192]{1,0:T(8,128)(2,1)} %bitcast.19), channel_id=1, source_target_pairs={{3,2},{7,8},{11,6},{15,24},{19,3},{23,9},{27,7},{31,25},{0,28},{4,... | collective-permute-start | bytes 786440 | tf_op jit(solution)/shard_map/ppermute | solution.py:341
  1.9 21.4 %collective-permute-start.4 = (bf16[16,8192]{1,0:T(8,128)(2,1)}, bf16[16,8192]{1,0:T(8,128)(2,1)S(1)}, u32[]{:S(2)}, u32[]{:S(2)}) collective-permute-start(bf16[16,8192]{1,0:T(8,128)(2,1)} %bitcast.20), channel_id=1, source_target_pairs={{2,2},{6,8},{10,6},{14,24},{18,3},{22,9},{26,7},{30,25},{3,28},{7,... | collective-permute-start | bytes 786440 | tf_op jit(solution)/shard_map/ppermute | solution.py:341
  5.0 34.7 %collective-permute-start.3 = (bf16[16,8192]{1,0:T(8,128)(2,1)}, bf16[16,8192]{1,0:T(8,128)(2,1)S(1)}, u32[]{:S(2)}, u32[]{:S(2)}) collective-permute-start(bf16[16,8192]{1,0:T(8,128)(2,1)} %bitcast.21), channel_id=1, source_target_pairs={{1,2},{5,8},{9,6},{13,24},{17,3},{21,9},{25,7},{29,25},{2,28},{6,2... | collective-permute-start | bytes 786440 | tf_op jit(solution)/shard_map/ppermute | solution.py:341
  8.8 10.3 %collective-permute-start = (s32[4]{0:T(128)}, s32[4]{0:T(128)S(1)}, u32[]{:S(2)}, u32[]{:S(2)}) collective-permute-start(s32[4]{0:T(128)} %bitcast.31), channel_id=1, source_target_pairs={{0,1},{1,0},{2,3},{3,2},{4,5},{5,4},{6,7},{7,6},{8,9},{9,8},{10,11... | collective-permute-start | bytes 56 | tf_op jit(solution)/shard_map/ppermute | solution.py:321
  8.9 1.0 copy-start
  10.6 19.6 %all-to-all-start = ((bf16[8,16,1024]{2,1,0:T(8,128)(2,1)}), bf16[8,16,1024]{2,1,0:T(8,128)(2,1)S(1)}, u32[]{:S(2)}, u32[]{:S(2)}) async-start(bf16[8,16,1024]{2,1,0:T(8,128)(2,1)} %chunk.1), calls=%async_computation | async-start | bytes 524288 | tf_op jit(solution)/shard_map/all_to_all | solution.py:328
  15.4 5.4 %copy-start.5 = (s32[1,4]{1,0:T(1,128)S(1)}, s32[1,4]{1,0:T(1,128)}, u32[]{:S(2)}) copy-start(s32[1,4]{1,0:T(1,128)} %param.7) | copy-start | bytes 52
  15.4 24.3 %copy-start.1 = (bf16[1,16,8192]{2,1,0:T(8,128)(2,1)S(1)}, bf16[1,16,8192]{2,1,0:T(8,128)(2,1)}, u32[]{:S(2)}) copy-start(bf16[1,16,8192]{2,1,0:T(8,128)(2,1)} %param.6) | copy-start | bytes 786436
  15.4 48.6 %copy-start.6 = (f32[32]{0:T(128)S(1)}, f32[32]{0:T(128)}, u32[]{:S(2)}) copy-start(f32[32]{0:T(128)} %param.8) | copy-start | bytes 388
  15.6 1.0 copy-start.3
  16.5 1.0 copy-start.4
  17.5 46.4 %collective-permute-start.6 = (bf16[2,64,4096]{2,1,0:T(8,128)(2,1)}, bf16[2,64,4096]{2,1,0:T(8,128)(2,1)}, u32[]{:S(2)}, u32[]{:S(2)}) collective-permute-start(bf16[2,64,4096]{2,1,0:T(8,128)(2,1)} %get-tuple-element.22), channel_id=1, source_target_pairs={{0,2},{1,3},{30,28},{31,29},{32,34},{33,35},{62,60},{63,61},{64,66... | collective-permute-start | bytes 3145736 | tf_op jit(solution)/shard_map/ppermute | solution.py:340
  19.1 44.8 %collective-permute-start.7 = (bf16[2,64,4096]{2,1,0:T(8,128)(2,1)}, bf16[2,64,4096]{2,1,0:T(8,128)(2,1)}, u32[]{:S(2)}, u32[]{:S(2)}) collective-permute-start(bf16[2,64,4096]{2,1,0:T(8,128)(2,1)} %copy-done.4), channel_id=1, source_target_pairs={{0,8},{1,9},{30,22},{31,23},{32,40},{33,41},{62,54},{63,55},{64,72... | collective-permute-start | bytes 3145736 | tf_op jit(solution)/shard_map/ppermute | solution.py:340
  22.1 41.9 %collective-permute-start.8 = (bf16[2,64,4096]{2,1,0:T(8,128)(2,1)}, bf16[2,64,4096]{2,1,0:T(8,128)(2,1)}, u32[]{:S(2)}, u32[]{:S(2)}) collective-permute-start(bf16[2,64,4096]{2,1,0:T(8,128)(2,1)} %copy-done.3), channel_id=1, source_target_pairs={{0,6},{1,7},{30,24},{31,25},{32,38},{33,39},{62,56},{63,57},{64,70... | collective-permute-start | bytes 3145736 | tf_op jit(solution)/shard_map/ppermute | solution.py:340
  23.4 40.6 %collective-permute-start.9 = (bf16[2,64,4096]{2,1,0:T(8,128)(2,1)S(1)}, bf16[2,64,4096]{2,1,0:T(8,128)(2,1)}, u32[]{:S(2)}, u32[]{:S(2)}) collective-permute-start(bf16[2,64,4096]{2,1,0:T(8,128)(2,1)S(1)} %get-tuple-element.25), channel_id=1, source_target_pairs={{0,24},{1,25},{30,6},{31,7},{32,56},{33,57},{62,38},{63,39},{64,88... | collective-permute-start | bytes 3145736 | tf_op jit(solution)/shard_map/ppermute | solution.py:340
  31.6 32.3 %all-to-all-start.1 = ((bf16[16,16,1024]{2,1,0:T(8,128)(2,1)}), bf16[16,16,1024]{2,1,0:T(8,128)(2,1)S(1)}, u32[]{:S(2)}, u32[]{:S(2)}) async-start(bf16[16,16,1024]{2,1,0:T(8,128)(2,1)} %spread.1), calls=%async_computation.1 | async-start | bytes 1048576 | tf_op jit(solution)/shard_map/all_to_all | solution.py:344
  39.7 13.6 %collective-permute-start.2 = (bf16[16,8192]{1,0:T(8,128)(2,1)S(1)}, bf16[16,8192]{1,0:T(8,128)(2,1)S(1)}, u32[]{:S(2)}, u32[]{:S(2)}) collective-permute-start(bf16[16,8192]{1,0:T(8,128)(2,1)S(1)} %bitcast.23), channel_id=1, source_target_pairs={{0,2},{4,8},{8,6},{12,24},{16,3},{20,9},{24,7},{28,25},{1,28},{5,2... | collective-permute-start | bytes 786440 | tf_op jit(solution)/shard_map/ppermute | solution.py:341
  63.9 1.9 %collective-permute-start.1 = (bf16[2,4,2,16,1024]{4,3,2,1,0:T(8,128)(2,1)S(1)}, bf16[2,4,2,16,1024]{4,3,2,1,0:T(8,128)(2,1)S(1)}, u32[]{:S(2)}, u32[]{:S(2)}) collective-permute-start(bf16[2,4,2,16,1024]{4,3,2,1,0:T(8,128)(2,1)S(1)} %bitcast.17), channel_id=1, source_target_pairs={{0,1},{1,0},{2,3},{3,2},{4,5},{5,4},{6,7},{7,6},{8,9},{9,8},{10,11... | collective-permute-start | bytes 1572872 | tf_op jit(solution)/shard_map/ppermute | solution.py:345
  76.2 5.3 %collective-permute-start.14 = (bf16[17,16,1024]{2,1,0:T(8,128)(2,1)S(1)}, bf16[17,16,1024]{2,1,0:T(8,128)(2,1)S(1)}, u32[]{:S(2)}, u32[]{:S(2)}) collective-permute-start(bf16[17,16,1024]{2,1,0:T(8,128)(2,1)S(1)} %get-tuple-element.32), channel_id=1, source_target_pairs={{0,1},{1,0},{2,3},{3,2},{4,5},{5,4},{6,7},{7,6},{8,9},{9,8},{10,11... | collective-permute-start | bytes 1671176 | tf_op jit(solution)/shard_map/ppermute | solution.py:372
  76.4 42.3 %collective-permute-start.13 = (bf16[2,64,4096]{2,1,0:T(8,128)(2,1)}, bf16[2,64,4096]{2,1,0:T(8,128)(2,1)S(1)}, u32[]{:S(2)}, u32[]{:S(2)}) collective-permute-start(bf16[2,64,4096]{2,1,0:T(8,128)(2,1)} %get-tuple-element.28), channel_id=1, source_target_pairs={{24,0},{25,1},{6,30},{7,31},{56,32},{57,33},{38,62},{39,63},{88,64... | collective-permute-start | bytes 3145736 | tf_op jit(solution)/shard_map/ppermute | solution.py:377
  77.8 42.9 %collective-permute-start.12 = (bf16[2,64,4096]{2,1,0:T(8,128)(2,1)}, bf16[2,64,4096]{2,1,0:T(8,128)(2,1)S(1)}, u32[]{:S(2)}, u32[]{:S(2)}) collective-permute-start(bf16[2,64,4096]{2,1,0:T(8,128)(2,1)} %get-tuple-element.28), channel_id=1, source_target_pairs={{6,0},{7,1},{24,30},{25,31},{38,32},{39,33},{56,62},{57,63},{70,64... | collective-permute-start | bytes 3145736 | tf_op jit(solution)/shard_map/ppermute | solution.py:377
  79.1 43.5 %collective-permute-start.11 = (bf16[2,64,4096]{2,1,0:T(8,128)(2,1)}, bf16[2,64,4096]{2,1,0:T(8,128)(2,1)S(1)}, u32[]{:S(2)}, u32[]{:S(2)}) collective-permute-start(bf16[2,64,4096]{2,1,0:T(8,128)(2,1)} %get-tuple-element.28), channel_id=1, source_target_pairs={{8,0},{9,1},{22,30},{23,31},{40,32},{41,33},{54,62},{55,63},{72,64... | collective-permute-start | bytes 3145736 | tf_op jit(solution)/shard_map/ppermute | solution.py:377
  79.9 58.9 %collective-permute-start.10 = (bf16[2,64,4096]{2,1,0:T(8,128)(2,1)}, bf16[2,64,4096]{2,1,0:T(8,128)(2,1)}, u32[]{:S(2)}, u32[]{:S(2)}) collective-permute-start(bf16[2,64,4096]{2,1,0:T(8,128)(2,1)} %get-tuple-element.28), channel_id=1, source_target_pairs={{2,0},{3,1},{28,30},{29,31},{34,32},{35,33},{60,62},{61,63},{66,64... | collective-permute-start | bytes 3145736 | tf_op jit(solution)/shard_map/ppermute | solution.py:377
  111.8 14.8 %copy-start.2 = (bf16[8,16,1024]{2,1,0:T(8,128)(2,1)}, bf16[8,16,1024]{2,1,0:T(8,128)(2,1)S(1)}, u32[]{:S(2)}) copy-start(bf16[8,16,1024]{2,1,0:T(8,128)(2,1)S(1)} %get-tuple-element.34) | copy-start | bytes 786436
  111.8 3.6 %collective-permute-start.19 = (f32[1,128]{1,0:T(1,128)S(1)}, f32[1,128]{1,0:T(1,128)S(1)}, u32[]{:S(2)}, u32[]{:S(2)}) collective-permute-start(f32[1,128]{1,0:T(1,128)S(1)} %get-tuple-element.39), channel_id=1, source_target_pairs={{0,32},{32,0},{64,96},{96,64},{128,160},{160,128},{192,224},{224,1... | collective-permute-start | bytes 1544 | tf_op jit(solution)/shard_map/ppermute | solution.py:390
  115.4 9.1 %collective-permute-start.20 = (f32[1,128]{1,0:T(1,128)S(1)}, f32[1,128]{1,0:T(1,128)S(1)}, u32[]{:S(2)}, u32[]{:S(2)}) collective-permute-start(f32[1,128]{1,0:T(1,128)S(1)} %add.21), channel_id=1, source_target_pairs={{0,64},{32,96},{64,0},{96,32},{128,192},{160,224},{192,128},{224,1... | collective-permute-start | bytes 1544 | tf_op jit(solution)/shard_map/ppermute | solution.py:390
  118.7 28.2 %collective-permute-start.15 = (bf16[16,8192]{1,0:T(8,128)(2,1)}, bf16[16,8192]{1,0:T(8,128)(2,1)}, u32[]{:S(2)}, u32[]{:S(2)}) collective-permute-start(bf16[16,8192]{1,0:T(8,128)(2,1)} %get-tuple-element.35), channel_id=1, source_target_pairs={{2,0},{8,4},{6,8},{24,12},{3,16},{9,20},{7,24},{25,28},{28,1},{22,... | collective-permute-start | bytes 786440 | tf_op jit(solution)/shard_map/ppermute | solution.py:379
  120.7 26.2 %collective-permute-start.16 = (bf16[16,8192]{1,0:T(8,128)(2,1)}, bf16[16,8192]{1,0:T(8,128)(2,1)}, u32[]{:S(2)}, u32[]{:S(2)}) collective-permute-start(bf16[16,8192]{1,0:T(8,128)(2,1)} %get-tuple-element.36), channel_id=1, source_target_pairs={{2,1},{8,5},{6,9},{24,13},{3,17},{9,21},{7,25},{25,29},{28,2},{22,... | collective-permute-start | bytes 786440 | tf_op jit(solution)/shard_map/ppermute | solution.py:379
  122.6 24.2 %collective-permute-start.17 = (bf16[16,8192]{1,0:T(8,128)(2,1)}, bf16[16,8192]{1,0:T(8,128)(2,1)}, u32[]{:S(2)}, u32[]{:S(2)}) collective-permute-start(bf16[16,8192]{1,0:T(8,128)(2,1)} %get-tuple-element.37), channel_id=1, source_target_pairs={{2,2},{8,6},{6,10},{24,14},{3,18},{9,22},{7,26},{25,30},{28,3},{22... | collective-permute-start | bytes 786440 | tf_op jit(solution)/shard_map/ppermute | solution.py:379
  124.6 22.3 %collective-permute-start.18 = (bf16[16,8192]{1,0:T(8,128)(2,1)}, bf16[16,8192]{1,0:T(8,128)(2,1)}, u32[]{:S(2)}, u32[]{:S(2)}) collective-permute-start(bf16[16,8192]{1,0:T(8,128)(2,1)} %get-tuple-element.38), channel_id=1, source_target_pairs={{2,3},{8,7},{6,11},{24,15},{3,19},{9,23},{7,27},{25,31},{28,0},{22... | collective-permute-start | bytes 786440 | tf_op jit(solution)/shard_map/ppermute | solution.py:379
  126.6 20.3 %all-to-all-start.3 = ((bf16[8,16,1024]{2,1,0:T(8,128)(2,1)}), bf16[8,16,1024]{2,1,0:T(8,128)(2,1)S(1)}, u32[]{:S(2)}, u32[]{:S(2)}) async-start(bf16[8,16,1024]{2,1,0:T(8,128)(2,1)} %copy-done.2), calls=%async_computation.3 | async-start | bytes 524288 | tf_op jit(solution)/shard_map/all_to_all | solution.py:388
  138.8 7.5 %collective-permute-start.21 = (f32[1,128]{1,0:T(1,128)S(1)}, f32[1,128]{1,0:T(1,128)S(1)}, u32[]{:S(2)}, u32[]{:S(2)}) collective-permute-start(f32[1,128]{1,0:T(1,128)S(1)} %add.22), channel_id=1, source_target_pairs={{0,128},{32,160},{64,192},{96,224},{128,0},{160,32},{192,64},{224,... | collective-permute-start | bytes 1544 | tf_op jit(solution)/shard_map/ppermute | solution.py:390

commit v3 on v2

v3 whole, which is shorter than its diff:
```python
import jax
import jax.numpy as jnp
from jax import lax
from jax.experimental import pallas as pl
from jax.experimental.pallas import tpu as pltpu
from jax.sharding import Mesh
from jax.sharding import PartitionSpec as P

CTX = ("x", "yh", "yl", "c")
CHIP = ("x", "yh", "yl")
IMG = ("x", "yh")
NLAT = 64
HEADS = 32
HS = 128
GRP = 8
BATCH = 4
COLS = GRP * HS
WIDE = COLS + 128
QUART = 16
SCALE = HS**-0.5
DEP_CHUNK = 1
DEP_SPREAD = 0
DEP_LENT = 0
GATE_FIRST = 0
BF = jnp.bfloat16
F32 = jnp.float32

BLOCK_PAIRS = (
    [(0, 2), (1, 7), (31, 25)],
    [(0, 8), (1, 25), (30, 22), (31, 7)],
)
WORK = (
    (2, 0, True, 0),
    (8, 1, True, 1),
    (22, 1, False, 1),
    (7, 4, True, 0),
    (7, 4, False, 1),
    (25, 5, True, 1),
    (25, 5, False, 0),
)


def latent_pairs(s):
    pairs = [(2 * (4 + s), 0), (2 * (4 + s) + 1, 30), (2 * (12 + s) + 1, 31)]
    if s < 2:
        pairs.append((2 * (12 + s), 1))
        pairs += [(2 * s, 2), (2 * (2 + s), 8), (2 * (2 + s) + 1, 22)]
        pairs += [(2 * (8 + s), 7), (2 * (10 + s), 25)]
    return pairs


def back(pairs):
    return [(b, a) for a, b in pairs]


def nt(a, b):
    return lax.dot_general(a, b, (((1,), (1,)), ((), ())), preferred_element_type=F32)


def tn(a, b):
    return lax.dot_general(a, b, (((0,), (0,)), ((), ())), preferred_element_type=F32)


def nn(a, b):
    return lax.dot_general(a, b, (((1,), (0,)), ((), ())), preferred_element_type=F32)


def pick(cases, default):
    out = jnp.int32(default)
    for cond, value in cases:
        out = jnp.where(cond, jnp.int32(value), out)
    return out


def step_block(ctx, s):
    return jnp.where(ctx == 31, jnp.int32(1 - s), jnp.int32(s))


def place(here, images, partner):
    ctx = here[0]
    low = ctx % 2 == 0
    last = jnp.where(low, partner[3], images[3])
    first = jnp.where(low, images[0], partner[0])
    return ctx, jnp.where(ctx < 2, last, first)


def chunk_kernel(src, *rest):
    dst, sems = rest[-2:]
    copies = [
        pltpu.make_async_copy(src.at[:, pl.ds(i * COLS, COLS)], dst.at[i], sems.at[i])
        for i in range(8)
    ]
    for copy in copies:
        copy.start()
    for copy in copies:
        copy.wait()


def pack_kernel(here, q, g, d0, d1, buf, sems):
    ctx = here[0]

    @pl.when((ctx < 2) | (ctx >= 30))
    def _():
        loads = []
        for s in range(2):
            rows = pl.ds(pl.multiple_of(step_block(ctx, s) * NLAT, NLAT), NLAT)
            for a, ref in enumerate((q, g)):
                copy = pltpu.make_async_copy(ref.at[rows], buf.at[s, a], sems.at[0, s, a])
                copy.start()
                loads.append(copy)
        stores = []
        for s, d in enumerate((d0, d1)):
            for a in range(2):
                loads[2 * s + a].wait()
                copy = pltpu.make_async_copy(buf.at[s, a], d.at[a], sems.at[1, s, a])
                copy.start()
                stores.append(copy)
        for copy in stores:
            copy.wait()


def half_kernel(own, other, dst):
    dst[0:QUART] = own[...]
    dst[QUART : 2 * QUART] = other[...]


def spread_kernel(here, images, partner, got, *rest):
    dst = rest[-1]
    _, lead = place(here, images, partner)
    sel = got[lead]
    for p in range(16):
        dst[p] = sel


def heads_side_by_side(items):
    s = [nt(k, q) for q, g, k, v, t, keep in items]
    gf = [g.astype(F32) for q, g, k, v, t, keep in items]
    dm = [(it[4] * f).astype(BF) for it, f in zip(items, gf)]
    dp = [nt(it[3], d) for it, d in zip(items, dm)]
    e = [jnp.exp((x - jnp.max(x, axis=0, keepdims=True)) * SCALE) for x in s]
    p = [x * (it[5] / jnp.sum(x, axis=0, keepdims=True)) for it, x in zip(items, e)]
    pb = [x.astype(BF) for x in p]
    mix = [tn(x, it[3]) for it, x in zip(items, pb)]
    inner = [jnp.sum(a * b, axis=0, keepdims=True) for a, b in zip(p, dp)]
    ds = [(a * (b - c)).astype(BF) for a, b, c in zip(p, dp, inner)]
    dv = [nn(a, b) for a, b in zip(pb, dm)]
    dq = [tn(a, it[2]) * SCALE for it, a in zip(items, ds)]
    dk = [nn(a, it[0]) * SCALE for it, a in zip(items, ds)]
    gs = [jnp.sum(a * b, axis=0, keepdims=True) for a, b in zip(gf, mix)]
    out = [(it[4] * m).astype(BF) for it, m in zip(items, mix)]
    return list(zip(out, [x.astype(BF) for x in dq], dk, dv, gs))


def split3(x):
    hi = x.astype(BF).astype(F32)
    mid = (x - hi).astype(BF).astype(F32)
    lo = x - hi - mid
    row = lax.broadcasted_iota(jnp.int32, (16, x.shape[1]), 0)
    val = jnp.where(row == 0, hi, jnp.where(row == 1, mid, jnp.where(row == 2, lo, 0.0)))
    return val.astype(BF)


def attention_kernel(
    here, images, partner, tg, q, g, mine, other, l0, l1, l2, l3, x0, x1,
    o, dq, xo, pay, opay, y0, y1, y2, y3, gate, xbuf, gacc, sem,
):
    c = pl.program_id(0)
    tokens = q.shape[0]
    width = o.shape[1] * 4
    ctx, lead = place(here, images, partner)
    latents = (l0, l1, l2, l3)
    grads = (y0, y1, y2, y3)
    source = pick(
        [((ctx == w) & ((lead > j) if low else (lead < j)), s) for w, j, low, s in WORK], -1
    )
    hot = (ctx < 2) | (ctx >= 30)

    @pl.when(c == 0)
    def _():
        gacc[...] = jnp.zeros_like(gacc)
        for n, x in enumerate((x0, x1)):

            @pl.when(source == n)
            def _():
                copy = pltpu.make_async_copy(x, xbuf, sem)
                copy.start()
                copy.wait()

    block = lax.broadcasted_iota(jnp.int32, (1, tokens), 1) // (tokens // 4)
    keep = jnp.zeros((1, tokens), F32)
    for b in range(4):
        keep = jnp.where((block == b) & (images[b] == lead), 1.0, keep)
    ones = jnp.ones((1, NLAT), F32)
    stays = [jnp.where(images[k] == lead, 0.0, ones) for k in (2, 3)]

    def work(slots):
        for first in range(0, GRP, BATCH):
            items, heads = [], range(first, first + BATCH)
            for n in heads:
                cols = slice(n * HS, n * HS + HS)
                t = tg[c * GRP + n]
                k = [ref[0, 0, y, :, cols] for ref in (mine, other) for y in range(2)]
                v = [ref[1, 0, y, :, cols] for ref in (mine, other) for y in range(2)]
                k, v = jnp.concatenate(k, axis=0), jnp.concatenate(v, axis=0)
                items.append((q[:, cols], g[:, cols], k, v, t, keep))
                wk = pl.ds(pl.multiple_of(c * COLS + n * HS, HS), HS)
                wv = pl.ds(pl.multiple_of(width + c * COLS + n * HS, HS), HS)
                for z in range(slots):
                    k = jnp.concatenate([ref[:, wk] for ref in latents[2 * z : 2 * z + 2]], axis=0)
                    v = jnp.concatenate([ref[:, wv] for ref in latents[2 * z : 2 * z + 2]], axis=0)
                    if slots == 1:
                        items.append((xbuf[0, :, wk], xbuf[1, :, wk], k, v, t, ones))
                    else:
                        rows = slice((2 + z) * NLAT, (3 + z) * NLAT)
                        items.append((q[rows, cols], g[rows, cols], k, v, t, stays[z]))
            done = heads_side_by_side(items)
            for n in heads:
                cols = slice(n * HS, n * HS + HS)
                wk = pl.ds(pl.multiple_of(c * COLS + n * HS, HS), HS)
                wv = pl.ds(pl.multiple_of(width + c * COLS + n * HS, HS), HS)
                ob, dqb, dk, dv, gs = done.pop(0)
                for kv, d in enumerate((dk, dv)):
                    for y in range(2):
                        at = kv * 8 + c * 2 + y
                        pay[at, :, cols] = d[y * QUART : (y + 1) * QUART]
                        opay[at, :, cols] = d[(2 + y) * QUART : (3 + y) * QUART].astype(BF)
                if slots < 2:
                    o[:, cols] = ob
                    dq[:, cols] = dqb
                else:
                    o[0 : 2 * NLAT, cols] = ob[0 : 2 * NLAT]
                    dq[0 : 2 * NLAT, cols] = dqb[0 : 2 * NLAT]
                for z in range(slots):
                    ox, dqx, dk, dv, gx = done.pop(0)
                    if slots == 1:
                        xo[0, :, cols] = ox
                        xo[1, :, cols] = dqx
                    else:
                        rows = slice((2 + z) * NLAT, (3 + z) * NLAT)
                        o[rows, cols] = ob[rows] + ox
                        dq[rows, cols] = dqb[rows] + dqx
                    for h in range(2):
                        rows = slice(h * 2 * QUART, (h + 1) * 2 * QUART)
                        grads[2 * z + h][:, wk] = dk[rows].astype(BF)
                        grads[2 * z + h][:, wv] = dv[rows].astype(BF)
                    gs = gs + gx
                gacc[pl.ds(c * GRP + n, 1), :] = gs

    @pl.when(source >= 0)
    def _():
        work(1)

    @pl.when(hot)
    def _():
        work(2)

    @pl.when((source < 0) & jnp.logical_not(hot))
    def _():
        work(0)

    @pl.when(c == pl.num_programs(0) - 1)
    def _():
        gate[...] = jnp.sum(gacc[...].T, axis=0, keepdims=True)


def pair_kernel(pay, got, gate, dst):
    for d in range(16):
        dst[d, :, 0:COLS] = (pay[d] + got[d].astype(F32)).astype(BF)
    val = split3(gate[...])
    for d in range(16):
        dst[d, :, COLS:WIDE] = val


def collect_kernel(got, dst, gate):
    total = got[0].astype(F32)
    for p in range(1, 16):
        total += got[p].astype(F32)
    gate[...] = jnp.sum(total[:, COLS:WIDE], axis=0, keepdims=True)
    val = total[:, 0:COLS].astype(BF)
    for j in range(8):
        dst[j] = val


def sort_kernel(here, r0, r1, r2, r3, own, give):
    chip = here[0] // 2
    step = jnp.where(chip // 4 % 2 == 0, chip % 2, chip % 4)
    for s, r in enumerate((r0, r1, r2, r3)):

        @pl.when(step == s)
        def _():
            own[...] = r[0:QUART]
            give[...] = r[QUART : 2 * QUART]


def assemble_kernel(here, images, partner, got, own, given, dst):
    ctx, lead = place(here, images, partner)
    image = ctx // 4
    low = (image > 3) & (image < 6) | (image < lead)
    held = low == (ctx % 2 == 0)

    @pl.when(image == lead)
    def _():
        for i in range(8):
            dst[:, i * COLS : (i + 1) * COLS] = got[i]

    @pl.when((image != lead) & held)
    def _():
        dst[...] = own[...]

    @pl.when((image != lead) & jnp.logical_not(held))
    def _():
        dst[...] = given[...]


def merge_kernel(here, images, partner, o_in, dq_in, r0, r1, o, dq, buf, sems):
    del o_in, dq_in
    ctx, lead = place(here, images, partner)

    @pl.when((ctx < 2) | (ctx >= 30))
    def _():
        for s, r in enumerate((r0, r1)):
            odd = images[step_block(ctx, s)] != lead

            @pl.when(odd)
            def _():
                pltpu.make_async_copy(r, buf.at[s], sems.at[s, 0]).start()

        for s, r in enumerate((r0, r1)):
            k = step_block(ctx, s)
            odd = images[k] != lead
            rows = pl.ds(pl.multiple_of(k * NLAT, NLAT), NLAT)

            @pl.when(odd)
            def _():
                pltpu.make_async_copy(r, buf.at[s], sems.at[s, 0]).wait()
                pltpu.make_async_copy(buf.at[s, 0], o.at[rows], sems.at[s, 1]).start()
                pltpu.make_async_copy(buf.at[s, 1], dq.at[rows], sems.at[s, 2]).start()

        for s in range(2):
            k = step_block(ctx, s)
            odd = images[k] != lead
            rows = pl.ds(pl.multiple_of(k * NLAT, NLAT), NLAT)

            @pl.when(odd)
            def _():
                pltpu.make_async_copy(buf.at[s, 0], o.at[rows], sems.at[s, 1]).wait()
                pltpu.make_async_copy(buf.at[s, 1], dq.at[rows], sems.at[s, 2]).wait()


VM = pl.BlockSpec(memory_space=pltpu.VMEM)
SM = pl.BlockSpec(memory_space=pltpu.SMEM)
HBM = pl.BlockSpec(memory_space=pltpu.HBM)
ANY = pl.BlockSpec(memory_space=pl.ANY)
LIMIT = 48 * 1024 * 1024


def shape(*dims, dtype=BF):
    return jax.ShapeDtypeStruct(dims, dtype)


def call(kernel, name, out_shape, in_specs, out_specs, cost=(0, 0), **more):
    estimate = pl.CostEstimate(flops=cost[0], bytes_accessed=cost[1], transcendentals=0)
    params = pltpu.CompilerParams(vmem_limit_bytes=LIMIT)
    return pl.pallas_call(
        kernel,
        name=name,
        out_shape=out_shape,
        in_specs=in_specs,
        out_specs=out_specs,
        compiler_params=params,
        cost_estimate=estimate,
        **more,
    )


def over_dp(x):
    for far in (1, 2, 4):
        x = x + lax.ppermute(x, "dp", [(s, s ^ far) for s in range(8)])
    return x


def body(queries, latent_kv, media, gate, grad_out):
    q, g, kv_rows = queries[0], grad_out[0], latent_kv[0]
    tokens, width = q.shape
    here = lax.axis_index(CTX).astype(jnp.int32)[None]
    images = media[0]
    partner = lax.ppermute(images, "c", [(0, 1), (1, 0)])
    where = (here, images, partner)

    packed = call(
        pack_kernel,
        "pack",
        [shape(2, NLAT, width)] * 2,
        [SM, HBM, HBM],
        [HBM] * 2,
        scratch_shapes=[
            pltpu.VMEM((2, 2, NLAT, width), BF),
            pltpu.SemaphoreType.DMA((2, 2, 2)),
        ],
    )(here, q, g)
    after = packed[:1] if DEP_CHUNK else []
    chunks = call(
        chunk_kernel,
        "chunk",
        shape(8, QUART, COLS),
        [HBM] * (1 + len(after)),
        VM,
        scratch_shapes=[pltpu.SemaphoreType.DMA((8,))],
    )(kv_rows, *after)
    mixed = lax.all_to_all(chunks, IMG, 0, 0, tiled=True)
    sent = [lax.ppermute(packed[s], CTX, BLOCK_PAIRS[s]) for s in range(2)]
    chip_rows = call(half_kernel, "half", shape(2 * QUART, 2 * width), [VM, VM], VM)(
        kv_rows, lax.ppermute(kv_rows, "c", [(0, 1), (1, 0)])
    )
    lent = [lax.ppermute(chip_rows, CTX, latent_pairs(s)) for s in range(4)]

    after = sent[:DEP_SPREAD] + lent[:DEP_LENT]
    spread = call(
        spread_kernel, "spread", shape(16, QUART, COLS), [SM, SM, SM, VM, *[HBM] * len(after)], VM
    )(*where, mixed, *after)
    mine = lax.all_to_all(spread, CHIP, 0, 0, tiled=True).reshape(2, 4, 2, QUART, COLS)
    other = lax.ppermute(mine, "c", [(0, 1), (1, 0)])

    tanh_gate = jnp.tanh(gate)
    wide = pl.BlockSpec((tokens, COLS), lambda c: (0, c))
    half = pl.BlockSpec((2, 1, 2, QUART, COLS), lambda c: (0, c, 0, 0, 0))
    o, dq, xo, pay, opay, y0, y1, y2, y3, gpart = call(
        attention_kernel,
        "attention",
        [
            shape(tokens, width),
            shape(tokens, width),
            shape(2, NLAT, width),
            shape(16, QUART, COLS, dtype=F32),
            shape(16, QUART, COLS),
            *[shape(2 * QUART, 2 * width)] * 4,
            shape(1, HS, dtype=F32),
        ],
        [SM, SM, SM, SM, wide, wide, half, half, *[VM] * 4, *[HBM] * 2],
        [wide, wide, pl.BlockSpec((2, NLAT, COLS), lambda c: (0, 0, c)), *[VM] * 7],
        grid=(4,),
        scratch_shapes=[
            pltpu.VMEM((2, NLAT, width), BF),
            pltpu.VMEM((HS, HS), F32),
            pltpu.SemaphoreType.DMA,
        ],
    )(*where, tanh_gate, q, g, mine, other, *lent, *sent)

    gsum = gpart + lax.ppermute(gpart, "c", [(0, 1), (1, 0)])
    if GATE_FIRST:
        gsum = over_dp(gsum)
    theirs = lax.ppermute(opay, "c", [(0, 1), (1, 0)])
    paired = call(pair_kernel, "pair", shape(16, QUART, WIDE), [VM, VM, VM], VM)(
        pay, theirs, gsum
    )
    parts = lax.all_to_all(paired, CHIP, 0, 0, tiled=True)
    owned = [
        lax.ppermute(y, CTX, back(latent_pairs(s))) for s, y in enumerate((y0, y1, y2, y3))
    ]
    own, give = call(
        sort_kernel, "sort", [shape(QUART, 2 * width)] * 2, [SM, *[VM] * 4], [VM, VM]
    )(here, *owned)
    given = lax.ppermute(give, "c", [(0, 1), (1, 0)])
    ready = [lax.ppermute(xo, CTX, back(BLOCK_PAIRS[s])) for s in range(2)]
    summed, gates = call(
        collect_kernel,
        "collect",
        [shape(8, QUART, COLS), shape(1, HS, dtype=F32)],
        [VM],
        [VM, VM],
    )(parts)
    if not GATE_FIRST:
        gates = over_dp(gates)
    final = lax.all_to_all(summed, IMG, 0, 0, tiled=True)
    latent_grad = call(
        assemble_kernel, "assemble", shape(QUART, 2 * width), [SM, SM, SM, VM, VM, VM], VM
    )(*where, final, own, given)
    o, dq = call(
        merge_kernel,
        "merge",
        [shape(tokens, width)] * 2,
        [SM, SM, SM, *[ANY] * 4],
        [ANY, ANY],
        scratch_shapes=[
            pltpu.VMEM((2, 2, NLAT, width), BF),
            pltpu.SemaphoreType.DMA((2, 3)),
        ],
        input_output_aliases={3: 0, 4: 1},
    )(*where, o, dq, *ready)
    gate_grad = (1.0 - tanh_gate * tanh_gate) * gates[0, :HEADS]
    return o[None], dq[None], latent_grad[None], gate_grad


def solution(mesh):
    fine = Mesh(mesh.devices.reshape(8, 4, 2, 2, 2), ("dp", "x", "yh", "yl", "c"))
    wide = P("dp", CTX, None)
    return jax.shard_map(
        body,
        mesh=fine,
        in_specs=(wide, wide, P("dp", CTX), P(), wide),
        out_specs=(wide, wide, wide, P()),
        check_vma=False,
    )
```

time: 150 us -> 135 us (0.900)
  blocking collectives: 30.1 us -> 0 us
  starting transfers between devices: 64.4 us -> 86 us
  waiting for transfers between devices: 33.3 us -> 24.4 us
  Pallas kernels: 15.4 us -> 18.2 us
    all_to_all x1 -> x0, blocking collectives: 30.1 us -> none  [body(): parts = lax.all_to_all(paired, CHIP, 0, 0, tiled=True)]
    all_to_all x0 -> x1, starting transfers between devices: none -> 8.02 us  [body(): parts = lax.all_to_all(paired, CHIP, 0, 0, tiled=True)]
    ppermute x15 -> x14, starting transfers between devices: 31.1 us -> 38.8 us  [the longest x1 12.8 us: body(): gsum = gpart + lax.ppermute(gpart, 'c', [(0, 1), (1, 0)])]
    ppermute x1, starting transfers between devices: 0.22 us -> 7.15 us  [body(): theirs = lax.ppermute(opay, 'c', [(0, 1), (1, 0)])]
    all_to_all x1, waiting for transfers between devices: 10.6 us -> 4.55 us  [body(): lax.all_to_all(spread, CHIP, 0, 0, tiled=True).reshape(2, 4, 2, QUART, COLS)]
    all_to_all x0 -> x1, waiting for transfers between devices: none -> 5.55 us  [body(): parts = lax.all_to_all(paired, CHIP, 0, 0, tiled=True)]
    all_to_all x1, waiting for transfers between devices: 5.47 us -> 0.11 us  [body(): mixed = lax.all_to_all(chunks, IMG, 0, 0, tiled=True)]
    all_to_all x1, starting transfers between devices: 4.8 us -> 8.29 us  [body(): mixed = lax.all_to_all(chunks, IMG, 0, 0, tiled=True)]
  transfers between devices with their start and end apart: 25 -> 25, of which waited for: 6 -> 9; matrix products, arithmetic and copies ran while one was open for 1% -> 0% of each run, Pallas kernels for 2% -> 6%
where the time goes in v3:
time: 135 us; the launch traced here: 134 us
  starting transfers between devices  86 us (64%)
  waiting for transfers between devices  24.4 us (18%)
  Pallas kernels  18.2 us (13%)
  local copies, waits for them, and re-layouts  3.68 us (3%)
    ppermute x1, starting transfers between devices, body(): gsum = gpart + lax.ppermute(gpart, 'c', [(0, 1), (1, 0)])  12.8 us
    ppermute x3, starting transfers between devices, over_dp(): x = x + lax.ppermute(x, 'dp', [(s, s ^ far) for s in range(8)])  12 us
    all_to_all x1, starting transfers between devices, body(): lax.all_to_all(spread, CHIP, 0, 0, tiled=True).reshape(2, 4, 2, QUART, COLS)  9.94 us
    pallas_call x1, Pallas kernels, body(): call(attention_kernel, 'attention', [shape(tokens, width), shape(tokens,...  9.24 us
    all_to_all x1, starting transfers between devices, body(): final = lax.all_to_all(summed, IMG, 0, 0, tiled=True)  8.9 us
    all_to_all x1, starting transfers between devices, body(): mixed = lax.all_to_all(chunks, IMG, 0, 0, tiled=True)  8.29 us
    ppermute x4, waiting for transfers between devices, body(): lent = [lax.ppermute(chip_rows, CTX, latent_pairs(s)) for s in range(4)]  8.18 us
    all_to_all x1, starting transfers between devices, body(): parts = lax.all_to_all(paired, CHIP, 0, 0, tiled=True)  8.02 us
  transfers between devices with their start and end apart: 25, of which 9 were waited for; matrix products, arithmetic and copies ran while one was open for 0% of the time, Pallas kernels for 6%

profile of v3, /device:TPU:24, one launch (start us, length us, event | category | flops | bytes accessed | tf_op | source)
XLA Modules:
  0.0 133.7 jit_solution(10405883453073270224)
XLA Ops:
  0.8 1.6 %copy-done = bf16[1,256,4096]{2,1,0:T(8,128)(2,1)S(1)} copy-done((bf16[1,256,4096]{2,1,0:T(8,128)(2,1)S(1)}, bf16[1,256,4096]{2,1,0:T(8,128)(2,1)}, u32[]{:S(2)}) %copy-start) | copy-done | bytes 2097176
  3.3 0.9 chunk.1
  4.2 8.3 %all-to-all-start = ((bf16[8,16,1024]{2,1,0:T(8,128)(2,1)}), bf16[8,16,1024]{2,1,0:T(8,128)(2,1)S(1)}, u32[]{:S(2)}, u32[]{:S(2)}) async-start(bf16[8,16,1024]{2,1,0:T(8,128)(2,1)} %chunk.1), calls=%async_computation | async-start | bytes 524288 | tf_op jit(solution)/shard_map/all_to_all | solution.py:410
  14.8 1.7 %collective-permute-start.8 = (bf16[2,64,4096]{2,1,0:T(8,128)(2,1)}, bf16[2,64,4096]{2,1,0:T(8,128)(2,1)}, u32[]{:S(2)}, u32[]{:S(2)}) collective-permute-start(bf16[2,64,4096]{2,1,0:T(8,128)(2,1)} %get-tuple-element.23), channel_id=1, source_target_pairs={{0,8},{1,25},{30,22},{31,7},{32,40},{33,57},{62,54},{63,39},{64,72... | collective-permute-start | bytes 3145736 | tf_op jit(solution)/shard_map/ppermute | solution.py:411
  16.4 1.6 %collective-permute-start.7 = (bf16[2,64,4096]{2,1,0:T(8,128)(2,1)S(1)}, bf16[2,64,4096]{2,1,0:T(8,128)(2,1)}, u32[]{:S(2)}, u32[]{:S(2)}) collective-permute-start(bf16[2,64,4096]{2,1,0:T(8,128)(2,1)S(1)} %get-tuple-element.22.rest_0_), channel_id=1, source_target_pairs={{0,2},{1,7},{31,25},{32,34},{33,39},{63,57},{64,66},{65,71},{95,89... | collective-permute-start | bytes 3145736 | tf_op jit(solution)/shard_map/ppermute | solution.py:411
  18.1 1.1 collective-permute-done.partner
  19.3 1.4 %spread.1 = bf16[16,16,1024]{2,1,0:T(8,128)(2,1)} custom-call(s32[1]{0:T(128)} %bitcast.here, s32[4]{0:T(128)S(1)} %bitcast.19, s32[4]{0:T(128)S(1)} %collective-permute-done.partner, bf16[8,16,1024]{2,1,0:T(8,128)(2,1)S(1)} %all-to-all-done.got), custom_call_target="tpu_custom_call" | custom-call | tf_op jit(solution)/shard_map/spread/pallas_call | solution.py:418
  20.7 9.9 %all-to-all-start.1 = ((bf16[16,16,1024]{2,1,0:T(8,128)(2,1)}), bf16[16,16,1024]{2,1,0:T(8,128)(2,1)S(1)}, u32[]{:S(2)}, u32[]{:S(2)}) async-start(bf16[16,16,1024]{2,1,0:T(8,128)(2,1)} %spread.1), calls=%async_computation.1 | async-start | bytes 1048576 | tf_op jit(solution)/shard_map/all_to_all | solution.py:421
  30.6 3.4 %collective-permute-start.4 = (bf16[32,8192]{1,0:T(8,128)(2,1)}, bf16[32,8192]{1,0:T(8,128)(2,1)S(1)}, u32[]{:S(2)}, u32[]{:S(2)}) collective-permute-start(bf16[32,8192]{1,0:T(8,128)(2,1)} %half.1), channel_id=1, source_target_pairs={{10,0},{11,30},{27,31},{26,1},{2,2},{6,8},{7,22},{18,7},{22,25},{4... | collective-permute-start | bytes 1572872 | tf_op jit(solution)/shard_map/ppermute | solution.py:415
  34.0 1.5 %collective-permute-start.3 = (bf16[32,8192]{1,0:T(8,128)(2,1)}, bf16[32,8192]{1,0:T(8,128)(2,1)}, u32[]{:S(2)}, u32[]{:S(2)}) collective-permute-start(bf16[32,8192]{1,0:T(8,128)(2,1)} %half.1), channel_id=1, source_target_pairs={{8,0},{9,30},{25,31},{24,1},{0,2},{4,8},{5,22},{16,7},{20,25},{40,... | collective-permute-start | bytes 1572872 | tf_op jit(solution)/shard_map/ppermute | solution.py:415
  35.5 4.5 %all-to-all-done.1 = bf16[16,16,1024]{2,1,0:T(8,128)(2,1)S(1)} async-done(((bf16[16,16,1024]{2,1,0:T(8,128)(2,1)}), bf16[16,16,1024]{2,1,0:T(8,128)(2,1)S(1)}, u32[]{:S(2)}, u32[]{:S(2)}) %all-to-all-start.1) | async-done | bytes 524320 | tf_op jit(solution)/shard_map/all_to_all | solution.py:421
  40.1 8.2 %collective-permute-done.4.l1 = bf16[32,8192]{1,0:T(8,128)(2,1)S(1)} collective-permute-done((bf16[32,8192]{1,0:T(8,128)(2,1)}, bf16[32,8192]{1,0:T(8,128)(2,1)S(1)}, u32[]{:S(2)}, u32[]{:S(2)}) %collective-permute-start.4) | collective-permute-done | bytes 524320 | tf_op jit(solution)/shard_map/ppermute | solution.py:415
  48.3 9.2 %attention.1 = (bf16[256,4096]{1,0:T(8,128)(2,1)}, bf16[256,4096]{1,0:T(8,128)(2,1)}, bf16[2,64,4096]{2,1,0:T(8,128)(2,1)}, f32[16,16,1024]{2,1,0:T(8,128)}, bf1...) custom-call(s32[1]{0:T(128)} %bitcast.here, ...), custom_call_target="tpu_custom_call" | custom-call | tf_op jit(solution)/shard_map/attention/pallas_call | solution.py:427
  57.5 7.2 %collective-permute-start.11 = (bf16[16,16,1024]{2,1,0:T(8,128)(2,1)S(1)}, bf16[16,16,1024]{2,1,0:T(8,128)(2,1)S(1)}, u32[]{:S(2)}, u32[]{:S(2)}) collective-permute-start(bf16[16,16,1024]{2,1,0:T(8,128)(2,1)S(1)} %get-tuple-element.30), channel_id=1, source_target_pairs={{0,1},{1,0},{2,3},{3,2},{4,5},{5,4},{6,7},{7,6},{8,9},{9,8},{10,11... | collective-permute-start | bytes 1572872 | tf_op jit(solution)/shard_map/ppermute | solution.py:452
  66.9 12.8 %collective-permute-start.12 = (f32[1,128]{1,0:T(1,128)S(1)}, f32[1,128]{1,0:T(1,128)S(1)}, u32[]{:S(2)}, u32[]{:S(2)}) collective-permute-start(f32[1,128]{1,0:T(1,128)S(1)} %get-tuple-element.31), channel_id=1, source_target_pairs={{0,1},{1,0},{2,3},{3,2},{4,5},{5,4},{6,7},{7,6},{8,9},{9,8},{10,11... | collective-permute-start | bytes 1544 | tf_op jit(solution)/shard_map/ppermute | solution.py:449
  80.5 1.3 collective-permute-start.14
  81.8 1.5 %collective-permute-start.15 = (bf16[32,8192]{1,0:T(8,128)(2,1)}, bf16[32,8192]{1,0:T(8,128)(2,1)}, u32[]{:S(2)}, u32[]{:S(2)}) collective-permute-start(bf16[32,8192]{1,0:T(8,128)(2,1)} %get-tuple-element.35), channel_id=1, source_target_pairs={{0,12},{30,13},{31,29},{32,44},{62,45},{63,61},{64,76},{94,77},{95... | collective-permute-start | bytes 1572872 | tf_op jit(solution)/shard_map/ppermute | solution.py:458
  83.2 1.5 %collective-permute-start.16 = (bf16[32,8192]{1,0:T(8,128)(2,1)}, bf16[32,8192]{1,0:T(8,128)(2,1)}, u32[]{:S(2)}, u32[]{:S(2)}) collective-permute-start(bf16[32,8192]{1,0:T(8,128)(2,1)} %get-tuple-element.36), channel_id=1, source_target_pairs={{0,14},{30,15},{31,31},{32,46},{62,47},{63,63},{64,78},{94,79},{95... | collective-permute-start | bytes 1572872 | tf_op jit(solution)/shard_map/ppermute | solution.py:458
  84.7 1.2 copy-done.1
  85.9 0.9 pair.1
  86.8 8.0 %all-to-all-start.2 = ((bf16[16,16,1152]{2,1,0:T(8,128)(2,1)}), bf16[16,16,1152]{2,1,0:T(8,128)(2,1)S(1)}, u32[]{:S(2)}, u32[]{:S(2)}) async-start(bf16[16,16,1152]{2,1,0:T(8,128)(2,1)} %pair.1), calls=%async_computation.2 | async-start | bytes 1179648 | tf_op jit(solution)/shard_map/all_to_all | solution.py:456
  94.9 2.1 %sort.1 = (bf16[16,8192]{1,0:T(8,128)(2,1)S(1)}, bf16[16,8192]{1,0:T(8,128)(2,1)}) custom-call(s32[1]{0:T(128)} %bitcast.here, bf16[32,8192]{1,0:T(8,128)(2,1)S(1)} %collective-permute-done.13.r0, bf16[32,8192]{1,0:T(8,128)(2,1)} %collective-permute-done.14.r1, bf16[32,8192]{1,0:T(8,128)(2,1)} %collective-permute-done.15.r2, ...), custom_call_target="tpu_custom_call" | custom-call | tf_op jit(solution)/shard_map/sort/pallas_call | solution.py:460
  97.0 2.9 %collective-permute-start.17 = (bf16[16,8192]{1,0:T(8,128)(2,1)}, bf16[16,8192]{1,0:T(8,128)(2,1)S(1)}, u32[]{:S(2)}, u32[]{:S(2)}) collective-permute-start(bf16[16,8192]{1,0:T(8,128)(2,1)} %get-tuple-element.38), channel_id=1, source_target_pairs={{0,1},{1,0},{2,3},{3,2},{4,5},{5,4},{6,7},{7,6},{8,9},{9,8},{10,11... | collective-permute-start | bytes 786440 | tf_op jit(solution)/shard_map/ppermute | solution.py:463
  99.9 5.6 %all-to-all-done.2.got = bf16[16,16,1152]{2,1,0:T(8,128)(2,1)S(1)} async-done(((bf16[16,16,1152]{2,1,0:T(8,128)(2,1)}), bf16[16,16,1152]{2,1,0:T(8,128)(2,1)S(1)}, u32[]{:S(2)}, u32[]{:S(2)}) %all-to-all-start.2) | async-done | bytes 589856 | tf_op jit(solution)/shard_map/all_to_all | solution.py:456
  106.2 8.9 %all-to-all-start.3 = ((bf16[8,16,1024]{2,1,0:T(8,128)(2,1)}), bf16[8,16,1024]{2,1,0:T(8,128)(2,1)S(1)}, u32[]{:S(2)}, u32[]{:S(2)}) async-start(bf16[8,16,1024]{2,1,0:T(8,128)(2,1)} %get-tuple-element.32), calls=%async_computation.3 | async-start | bytes 524288 | tf_op jit(solution)/shard_map/all_to_all | solution.py:474
  115.2 1.9 %collective-permute-start.18 = (f32[1,128]{1,0:T(1,128)S(1)}, f32[1,128]{1,0:T(1,128)S(1)}, u32[]{:S(2)}, u32[]{:S(2)}) collective-permute-start(f32[1,128]{1,0:T(1,128)S(1)} %get-tuple-element.39), channel_id=1, source_target_pairs={{0,32},{32,0},{64,96},{96,64},{128,160},{160,128},{192,224},{224,1... | collective-permute-start | bytes 1544 | tf_op jit(solution)/shard_map/ppermute | solution.py:378
  117.1 1.6 %collective-permute-done.18 = f32[1,128]{1,0:T(1,128)S(1)} collective-permute-done((f32[1,128]{1,0:T(1,128)S(1)}, f32[1,128]{1,0:T(1,128)S(1)}, u32[]{:S(2)}, u32[]{:S(2)}) %collective-permute-start.18) | collective-permute-done | bytes 544 | tf_op jit(solution)/shard_map/ppermute | solution.py:378
  118.7 3.2 %collective-permute-start.19 = (f32[1,128]{1,0:T(1,128)S(1)}, f32[1,128]{1,0:T(1,128)S(1)}, u32[]{:S(2)}, u32[]{:S(2)}) collective-permute-start(f32[1,128]{1,0:T(1,128)S(1)} %add.25), channel_id=1, source_target_pairs={{0,64},{32,96},{64,0},{96,32},{128,192},{160,224},{192,128},{224,1... | collective-permute-start | bytes 1544 | tf_op jit(solution)/shard_map/ppermute | solution.py:378
  121.9 1.5 %collective-permute-done.19 = f32[1,128]{1,0:T(1,128)S(1)} collective-permute-done((f32[1,128]{1,0:T(1,128)S(1)}, f32[1,128]{1,0:T(1,128)S(1)}, u32[]{:S(2)}, u32[]{:S(2)}) %collective-permute-start.19) | collective-permute-done | bytes 544 | tf_op jit(solution)/shard_map/ppermute | solution.py:378
  123.4 6.9 %collective-permute-start.20 = (f32[1,128]{1,0:T(1,128)S(1)}, f32[1,128]{1,0:T(1,128)S(1)}, u32[]{:S(2)}, u32[]{:S(2)}) collective-permute-start(f32[1,128]{1,0:T(1,128)S(1)} %add.26), channel_id=1, source_target_pairs={{0,128},{32,160},{64,192},{96,224},{128,0},{160,32},{192,64},{224,... | collective-permute-start | bytes 1544 | tf_op jit(solution)/shard_map/ppermute | solution.py:378
  131.0 0.9 collective-permute-done.20
  132.4 1.3 assemble.1
  (44 shorter events, 8.3 us)
Async XLA Ops:
  0.6 11.9 %collective-permute-start.2 = (bf16[16,8192]{1,0:T(8,128)(2,1)}, bf16[16,8192]{1,0:T(8,128)(2,1)S(1)}, u32[]{:S(2)}, u32[]{:S(2)}) collective-permute-start(bf16[16,8192]{1,0:T(8,128)(2,1)} %bitcast.15), channel_id=1, source_target_pairs={{0,1},{1,0},{2,3},{3,2},{4,5},{5,4},{6,7},{7,6},{8,9},{9,8},{10,11... | collective-permute-start | bytes 786440 | tf_op jit(solution)/shard_map/ppermute | solution.py:413
  0.7 1.6 %copy-start = (bf16[1,256,4096]{2,1,0:T(8,128)(2,1)S(1)}, bf16[1,256,4096]{2,1,0:T(8,128)(2,1)}, u32[]{:S(2)}) copy-start(bf16[1,256,4096]{2,1,0:T(8,128)(2,1)} %param.5) | copy-start | bytes 6291460
  2.3 0.9 copy-start.2
  2.4 15.6 %copy-start.3 = (s32[1,4]{1,0:T(1,128)S(1)}, s32[1,4]{1,0:T(1,128)}, u32[]{:S(2)}) copy-start(s32[1,4]{1,0:T(1,128)} %param.7) | copy-start | bytes 52
  4.2 35.9 %copy-start.4 = (f32[32]{0:T(128)S(1)}, f32[32]{0:T(128)}, u32[]{:S(2)}) copy-start(f32[32]{0:T(128)} %param.8) | copy-start | bytes 388
  4.2 15.1 %all-to-all-start = ((bf16[8,16,1024]{2,1,0:T(8,128)(2,1)}), bf16[8,16,1024]{2,1,0:T(8,128)(2,1)S(1)}, u32[]{:S(2)}, u32[]{:S(2)}) async-start(bf16[8,16,1024]{2,1,0:T(8,128)(2,1)} %chunk.1), calls=%async_computation | async-start | bytes 524288 | tf_op jit(solution)/shard_map/all_to_all | solution.py:410
  13.4 20.7 %collective-permute-start.6 = (bf16[32,8192]{1,0:T(8,128)(2,1)}, bf16[32,8192]{1,0:T(8,128)(2,1)S(1)}, u32[]{:S(2)}, u32[]{:S(2)}) collective-permute-start(bf16[32,8192]{1,0:T(8,128)(2,1)} %half.1), channel_id=1, source_target_pairs={{14,0},{15,30},{31,31},{46,32},{47,62},{63,63},{78,64},{79,94},{95... | collective-permute-start | bytes 1572872 | tf_op jit(solution)/shard_map/ppermute | solution.py:415
  14.1 26.0 %collective-permute-start.5 = (bf16[32,8192]{1,0:T(8,128)(2,1)}, bf16[32,8192]{1,0:T(8,128)(2,1)S(1)}, u32[]{:S(2)}, u32[]{:S(2)}) collective-permute-start(bf16[32,8192]{1,0:T(8,128)(2,1)} %half.1), channel_id=1, source_target_pairs={{12,0},{13,30},{29,31},{44,32},{45,62},{61,63},{76,64},{77,94},{93... | collective-permute-start | bytes 1572872 | tf_op jit(solution)/shard_map/ppermute | solution.py:415
  14.8 33.5 %collective-permute-start.8 = (bf16[2,64,4096]{2,1,0:T(8,128)(2,1)}, bf16[2,64,4096]{2,1,0:T(8,128)(2,1)}, u32[]{:S(2)}, u32[]{:S(2)}) collective-permute-start(bf16[2,64,4096]{2,1,0:T(8,128)(2,1)} %get-tuple-element.23), channel_id=1, source_target_pairs={{0,8},{1,25},{30,22},{31,7},{32,40},{33,57},{62,54},{63,39},{64,72... | collective-permute-start | bytes 3145736 | tf_op jit(solution)/shard_map/ppermute | solution.py:411
  16.4 31.9 %collective-permute-start.7 = (bf16[2,64,4096]{2,1,0:T(8,128)(2,1)S(1)}, bf16[2,64,4096]{2,1,0:T(8,128)(2,1)}, u32[]{:S(2)}, u32[]{:S(2)}) collective-permute-start(bf16[2,64,4096]{2,1,0:T(8,128)(2,1)S(1)} %get-tuple-element.22.rest_0_), channel_id=1, source_target_pairs={{0,2},{1,7},{31,25},{32,34},{33,39},{63,57},{64,66},{65,71},{95,89... | collective-permute-start | bytes 3145736 | tf_op jit(solution)/shard_map/ppermute | solution.py:411
  18.1 1.1 collective-permute-start
  20.7 19.4 %all-to-all-start.1 = ((bf16[16,16,1024]{2,1,0:T(8,128)(2,1)}), bf16[16,16,1024]{2,1,0:T(8,128)(2,1)S(1)}, u32[]{:S(2)}, u32[]{:S(2)}) async-start(bf16[16,16,1024]{2,1,0:T(8,128)(2,1)} %spread.1), calls=%async_computation.1 | async-start | bytes 1048576 | tf_op jit(solution)/shard_map/all_to_all | solution.py:421
  30.6 17.6 %collective-permute-start.4 = (bf16[32,8192]{1,0:T(8,128)(2,1)}, bf16[32,8192]{1,0:T(8,128)(2,1)S(1)}, u32[]{:S(2)}, u32[]{:S(2)}) collective-permute-start(bf16[32,8192]{1,0:T(8,128)(2,1)} %half.1), channel_id=1, source_target_pairs={{10,0},{11,30},{27,31},{26,1},{2,2},{6,8},{7,22},{18,7},{22,25},{4... | collective-permute-start | bytes 1572872 | tf_op jit(solution)/shard_map/ppermute | solution.py:415
  34.0 14.2 %collective-permute-start.3 = (bf16[32,8192]{1,0:T(8,128)(2,1)}, bf16[32,8192]{1,0:T(8,128)(2,1)}, u32[]{:S(2)}, u32[]{:S(2)}) collective-permute-start(bf16[32,8192]{1,0:T(8,128)(2,1)} %half.1), channel_id=1, source_target_pairs={{8,0},{9,30},{25,31},{24,1},{0,2},{4,8},{5,22},{16,7},{20,25},{40,... | collective-permute-start | bytes 1572872 | tf_op jit(solution)/shard_map/ppermute | solution.py:415
  40.1 8.2 %collective-permute-start.1 = (bf16[2,4,2,16,1024]{4,3,2,1,0:T(8,128)(2,1)S(1)}, bf16[2,4,2,16,1024]{4,3,2,1,0:T(8,128)(2,1)S(1)}, u32[]{:S(2)}, u32[]{:S(2)}) collective-permute-start(bf16[2,4,2,16,1024]{4,3,2,1,0:T(8,128)(2,1)S(1)} %bitcast.13), channel_id=1, source_target_pairs={{0,1},{1,0},{2,3},{3,2},{4,5},{5,4},{6,7},{7,6},{8,9},{9,8},{10,11... | collective-permute-start | bytes 1572872 | tf_op jit(solution)/shard_map/ppermute | solution.py:422
  57.5 24.2 %collective-permute-start.11 = (bf16[16,16,1024]{2,1,0:T(8,128)(2,1)S(1)}, bf16[16,16,1024]{2,1,0:T(8,128)(2,1)S(1)}, u32[]{:S(2)}, u32[]{:S(2)}) collective-permute-start(bf16[16,16,1024]{2,1,0:T(8,128)(2,1)S(1)} %get-tuple-element.30), channel_id=1, source_target_pairs={{0,1},{1,0},{2,3},{3,2},{4,5},{5,4},{6,7},{7,6},{8,9},{9,8},{10,11... | collective-permute-start | bytes 1572872 | tf_op jit(solution)/shard_map/ppermute | solution.py:452
  64.7 18.5 %collective-permute-start.13 = (bf16[32,8192]{1,0:T(8,128)(2,1)S(1)}, bf16[32,8192]{1,0:T(8,128)(2,1)S(1)}, u32[]{:S(2)}, u32[]{:S(2)}) collective-permute-start(bf16[32,8192]{1,0:T(8,128)(2,1)S(1)} %get-tuple-element.33), channel_id=1, source_target_pairs={{0,8},{30,9},{31,25},{1,24},{2,0},{8,4},{22,5},{7,16},{25,20},{32,... | collective-permute-start | bytes 1572872 | tf_op jit(solution)/shard_map/ppermute | solution.py:458
  65.4 64.9 %collective-permute-start.10 = (bf16[2,64,4096]{2,1,0:T(8,128)(2,1)}, bf16[2,64,4096]{2,1,0:T(8,128)(2,1)S(1)}, u32[]{:S(2)}, u32[]{:S(2)}) collective-permute-start(bf16[2,64,4096]{2,1,0:T(8,128)(2,1)} %get-tuple-element.26), channel_id=1, source_target_pairs={{8,0},{25,1},{22,30},{7,31},{40,32},{57,33},{54,62},{39,63},{72,64... | collective-permute-start | bytes 3145736 | tf_op jit(solution)/shard_map/ppermute | solution.py:464
  66.1 64.2 %collective-permute-start.9 = (bf16[2,64,4096]{2,1,0:T(8,128)(2,1)}, bf16[2,64,4096]{2,1,0:T(8,128)(2,1)S(1)}, u32[]{:S(2)}, u32[]{:S(2)}) collective-permute-start(bf16[2,64,4096]{2,1,0:T(8,128)(2,1)} %get-tuple-element.26), channel_id=1, source_target_pairs={{2,0},{7,1},{25,31},{34,32},{39,33},{57,63},{66,64},{71,65},{89,95... | collective-permute-start | bytes 3145736 | tf_op jit(solution)/shard_map/ppermute | solution.py:464
  66.9 13.6 %collective-permute-start.12 = (f32[1,128]{1,0:T(1,128)S(1)}, f32[1,128]{1,0:T(1,128)S(1)}, u32[]{:S(2)}, u32[]{:S(2)}) collective-permute-start(f32[1,128]{1,0:T(1,128)S(1)} %get-tuple-element.31), channel_id=1, source_target_pairs={{0,1},{1,0},{2,3},{3,2},{4,5},{5,4},{6,7},{7,6},{8,9},{9,8},{10,11... | collective-permute-start | bytes 1544 | tf_op jit(solution)/shard_map/ppermute | solution.py:449
  80.5 14.4 %collective-permute-start.14 = (bf16[32,8192]{1,0:T(8,128)(2,1)}, bf16[32,8192]{1,0:T(8,128)(2,1)}, u32[]{:S(2)}, u32[]{:S(2)}) collective-permute-start(bf16[32,8192]{1,0:T(8,128)(2,1)} %get-tuple-element.34), channel_id=1, source_target_pairs={{0,10},{30,11},{31,27},{1,26},{2,2},{8,6},{22,7},{7,18},{25,22},{3... | collective-permute-start | bytes 1572872 | tf_op jit(solution)/shard_map/ppermute | solution.py:458
  81.8 13.1 %collective-permute-start.15 = (bf16[32,8192]{1,0:T(8,128)(2,1)}, bf16[32,8192]{1,0:T(8,128)(2,1)}, u32[]{:S(2)}, u32[]{:S(2)}) collective-permute-start(bf16[32,8192]{1,0:T(8,128)(2,1)} %get-tuple-element.35), channel_id=1, source_target_pairs={{0,12},{30,13},{31,29},{32,44},{62,45},{63,61},{64,76},{94,77},{95... | collective-permute-start | bytes 1572872 | tf_op jit(solution)/shard_map/ppermute | solution.py:458
  83.2 11.6 %collective-permute-start.16 = (bf16[32,8192]{1,0:T(8,128)(2,1)}, bf16[32,8192]{1,0:T(8,128)(2,1)}, u32[]{:S(2)}, u32[]{:S(2)}) collective-permute-start(bf16[32,8192]{1,0:T(8,128)(2,1)} %get-tuple-element.36), channel_id=1, source_target_pairs={{0,14},{30,15},{31,31},{32,46},{62,47},{63,63},{64,78},{94,79},{95... | collective-permute-start | bytes 1572872 | tf_op jit(solution)/shard_map/ppermute | solution.py:458
  84.7 1.2 copy-start.1
  86.8 18.6 %all-to-all-start.2 = ((bf16[16,16,1152]{2,1,0:T(8,128)(2,1)}), bf16[16,16,1152]{2,1,0:T(8,128)(2,1)S(1)}, u32[]{:S(2)}, u32[]{:S(2)}) async-start(bf16[16,16,1152]{2,1,0:T(8,128)(2,1)} %pair.1), calls=%async_computation.2 | async-start | bytes 1179648 | tf_op jit(solution)/shard_map/all_to_all | solution.py:456
  97.0 35.4 %collective-permute-start.17 = (bf16[16,8192]{1,0:T(8,128)(2,1)}, bf16[16,8192]{1,0:T(8,128)(2,1)S(1)}, u32[]{:S(2)}, u32[]{:S(2)}) collective-permute-start(bf16[16,8192]{1,0:T(8,128)(2,1)} %get-tuple-element.38), channel_id=1, source_target_pairs={{0,1},{1,0},{2,3},{3,2},{4,5},{5,4},{6,7},{7,6},{8,9},{9,8},{10,11... | collective-permute-start | bytes 786440 | tf_op jit(solution)/shard_map/ppermute | solution.py:463
  106.2 26.1 %all-to-all-start.3 = ((bf16[8,16,1024]{2,1,0:T(8,128)(2,1)}), bf16[8,16,1024]{2,1,0:T(8,128)(2,1)S(1)}, u32[]{:S(2)}, u32[]{:S(2)}) async-start(bf16[8,16,1024]{2,1,0:T(8,128)(2,1)} %get-tuple-element.32), calls=%async_computation.3 | async-start | bytes 524288 | tf_op jit(solution)/shard_map/all_to_all | solution.py:474
  115.2 3.5 %collective-permute-start.18 = (f32[1,128]{1,0:T(1,128)S(1)}, f32[1,128]{1,0:T(1,128)S(1)}, u32[]{:S(2)}, u32[]{:S(2)}) collective-permute-start(f32[1,128]{1,0:T(1,128)S(1)} %get-tuple-element.39), channel_id=1, source_target_pairs={{0,32},{32,0},{64,96},{96,64},{128,160},{160,128},{192,224},{224,1... | collective-permute-start | bytes 1544 | tf_op jit(solution)/shard_map/ppermute | solution.py:378
  118.7 4.7 %collective-permute-start.19 = (f32[1,128]{1,0:T(1,128)S(1)}, f32[1,128]{1,0:T(1,128)S(1)}, u32[]{:S(2)}, u32[]{:S(2)}) collective-permute-start(f32[1,128]{1,0:T(1,128)S(1)} %add.25), channel_id=1, source_target_pairs={{0,64},{32,96},{64,0},{96,32},{128,192},{160,224},{192,128},{224,1... | collective-permute-start | bytes 1544 | tf_op jit(solution)/shard_map/ppermute | solution.py:378
  123.4 8.5 %collective-permute-start.20 = (f32[1,128]{1,0:T(1,128)S(1)}, f32[1,128]{1,0:T(1,128)S(1)}, u32[]{:S(2)}, u32[]{:S(2)}) collective-permute-start(f32[1,128]{1,0:T(1,128)S(1)} %add.26), channel_id=1, source_target_pairs={{0,128},{32,160},{64,192},{96,224},{128,0},{160,32},{192,64},{224,... | collective-permute-start | bytes 1544 | tf_op jit(solution)/shard_map/ppermute | solution.py:378

commit v4 on v3

--- a/solution.py
+++ b/solution.py
@@ -18,10 +18,6 @@
 WIDE = COLS + 128
 QUART = 16
 SCALE = HS**-0.5
-DEP_CHUNK = 1
-DEP_SPREAD = 0
-DEP_LENT = 0
-GATE_FIRST = 0
 BF = jnp.bfloat16
 F32 = jnp.float32
 
@@ -41,6 +37,7 @@
 
 
 def latent_pairs(s):
+    s = (s + 2) % 4
     pairs = [(2 * (4 + s), 0), (2 * (4 + s) + 1, 30), (2 * (12 + s) + 1, 31)]
     if s < 2:
         pairs.append((2 * (12 + s), 1))
@@ -76,22 +73,22 @@
     return jnp.where(ctx == 31, jnp.int32(1 - s), jnp.int32(s))
 
 
-def place(here, images, partner):
-    ctx = here[0]
-    low = ctx % 2 == 0
-    last = jnp.where(low, partner[3], images[3])
-    first = jnp.where(low, images[0], partner[0])
-    return ctx, jnp.where(ctx < 2, last, first)
-
-
-def chunk_kernel(src, *rest):
-    dst, sems = rest[-2:]
+def sends(ctx, s):
+    return (ctx < 2) | (ctx == 31) | ((ctx == 30) & (s == 1))
+
+
+def chunk_kernel(images, src, dst, sems):
     copies = [
-        pltpu.make_async_copy(src.at[:, pl.ds(i * COLS, COLS)], dst.at[i], sems.at[i])
+        pltpu.make_async_copy(
+            src.at[:, pl.ds(i * COLS, COLS)], dst.at[i, :, pl.ds(0, COLS)], sems.at[i]
+        )
         for i in range(8)
     ]
     for copy in copies:
         copy.start()
+    known = jnp.full((QUART, WIDE - COLS), images[0].astype(F32)).astype(BF)
+    for i in range(8):
+        dst[i, :, COLS:WIDE] = known
     for copy in copies:
         copy.wait()
 
@@ -99,24 +96,40 @@
 def pack_kernel(here, q, g, d0, d1, buf, sems):
     ctx = here[0]
 
-    @pl.when((ctx < 2) | (ctx >= 30))
-    def _():
-        loads = []
-        for s in range(2):
-            rows = pl.ds(pl.multiple_of(step_block(ctx, s) * NLAT, NLAT), NLAT)
-            for a, ref in enumerate((q, g)):
-                copy = pltpu.make_async_copy(ref.at[rows], buf.at[s, a], sems.at[0, s, a])
+    def loads(s):
+        rows = pl.ds(pl.multiple_of(step_block(ctx, s) * NLAT, NLAT), NLAT)
+        return [
+            pltpu.make_async_copy(ref.at[rows], buf.at[s, a], sems.at[0, s, a])
+            for a, ref in enumerate((q, g))
+        ]
+
+    def stores(s):
+        d = (d0, d1)[s]
+        return [
+            pltpu.make_async_copy(buf.at[s, a], d.at[a], sems.at[1, s, a]) for a in range(2)
+        ]
+
+    for s in range(2):
+
+        @pl.when(sends(ctx, s))
+        def _():
+            for copy in loads(s):
                 copy.start()
-                loads.append(copy)
-        stores = []
-        for s, d in enumerate((d0, d1)):
-            for a in range(2):
-                loads[2 * s + a].wait()
-                copy = pltpu.make_async_copy(buf.at[s, a], d.at[a], sems.at[1, s, a])
-                copy.start()
-                stores.append(copy)
-        for copy in stores:
-            copy.wait()
+
+    for s in range(2):
+
+        @pl.when(sends(ctx, s))
+        def _():
+            for load, store in zip(loads(s), stores(s)):
+                load.wait()
+                store.start()
+
+    for s in range(2):
+
+        @pl.when(sends(ctx, s))
+        def _():
+            for copy in stores(s):
+                copy.wait()
 
 
 def half_kernel(own, other, dst):
@@ -124,10 +137,10 @@
     dst[QUART : 2 * QUART] = other[...]
 
 
-def spread_kernel(here, images, partner, got, *rest):
-    dst = rest[-1]
-    _, lead = place(here, images, partner)
-    sel = got[lead]
+def spread_kernel(got, dst, lead):
+    first = jnp.max(got[3, :, COLS:WIDE].astype(F32)).astype(jnp.int32)
+    lead[0] = first
+    sel = got[first, :, 0:COLS]
     for p in range(16):
         dst[p] = sel
 
@@ -161,15 +174,15 @@
 
 
 def attention_kernel(
-    here, images, partner, tg, q, g, mine, other, l0, l1, l2, l3, x0, x1,
+    here, images, lead_ref, tg, q, g, mine, other, l0, l1, l2, l3, x0, x1,
     o, dq, xo, pay, opay, y0, y1, y2, y3, gate, xbuf, gacc, sem,
 ):
     c = pl.program_id(0)
     tokens = q.shape[0]
     width = o.shape[1] * 4
-    ctx, lead = place(here, images, partner)
-    latents = (l0, l1, l2, l3)
-    grads = (y0, y1, y2, y3)
+    ctx, lead = here[0], lead_ref[0]
+    latents = (l2, l3, l0, l1)
+    grads = (y2, y3, y0, y1)
     source = pick(
         [((ctx == w) & ((lead > j) if low else (lead < j)), s) for w, j, low, s in WORK], -1
     )
@@ -260,15 +273,19 @@
 
     @pl.when(c == pl.num_programs(0) - 1)
     def _():
-        gate[...] = jnp.sum(gacc[...].T, axis=0, keepdims=True)
+        gs = jnp.sum(gacc[...].T, axis=0, keepdims=True)
+        gate[...] = gs
+        opay[16] = jnp.zeros((QUART, COLS), BF)
+        opay[16, :, 0:HS] = split3(gs)
 
 
 def pair_kernel(pay, got, gate, dst):
     for d in range(16):
         dst[d, :, 0:COLS] = (pay[d] + got[d].astype(F32)).astype(BF)
-    val = split3(gate[...])
+    other = jnp.sum(got[16, :, 0:HS].astype(F32), axis=0, keepdims=True)
+    gates = split3(gate[...] + other)
     for d in range(16):
-        dst[d, :, COLS:WIDE] = val
+        dst[d, :, COLS:WIDE] = gates
 
 
 def collect_kernel(got, dst, gate):
@@ -284,7 +301,7 @@
 def sort_kernel(here, r0, r1, r2, r3, own, give):
     chip = here[0] // 2
     step = jnp.where(chip // 4 % 2 == 0, chip % 2, chip % 4)
-    for s, r in enumerate((r0, r1, r2, r3)):
+    for s, r in enumerate((r2, r3, r0, r1)):
 
         @pl.when(step == s)
         def _():
@@ -292,8 +309,8 @@
             give[...] = r[QUART : 2 * QUART]
 
 
-def assemble_kernel(here, images, partner, got, own, given, dst):
-    ctx, lead = place(here, images, partner)
+def assemble_kernel(here, lead_ref, got, own, given, dst):
+    ctx, lead = here[0], lead_ref[0]
     image = ctx // 4
     low = (image > 3) & (image < 6) | (image < lead)
     held = low == (ctx % 2 == 0)
@@ -312,39 +329,43 @@
         dst[...] = given[...]
 
 
-def merge_kernel(here, images, partner, o_in, dq_in, r0, r1, o, dq, buf, sems):
+def merge_kernel(here, images, lead_ref, o_in, dq_in, r0, r1, o, dq, buf, sems):
     del o_in, dq_in
-    ctx, lead = place(here, images, partner)
-
-    @pl.when((ctx < 2) | (ctx >= 30))
-    def _():
-        for s, r in enumerate((r0, r1)):
-            odd = images[step_block(ctx, s)] != lead
-
-            @pl.when(odd)
-            def _():
-                pltpu.make_async_copy(r, buf.at[s], sems.at[s, 0]).start()
-
-        for s, r in enumerate((r0, r1)):
-            k = step_block(ctx, s)
-            odd = images[k] != lead
-            rows = pl.ds(pl.multiple_of(k * NLAT, NLAT), NLAT)
-
-            @pl.when(odd)
-            def _():
-                pltpu.make_async_copy(r, buf.at[s], sems.at[s, 0]).wait()
-                pltpu.make_async_copy(buf.at[s, 0], o.at[rows], sems.at[s, 1]).start()
-                pltpu.make_async_copy(buf.at[s, 1], dq.at[rows], sems.at[s, 2]).start()
-
-        for s in range(2):
-            k = step_block(ctx, s)
-            odd = images[k] != lead
-            rows = pl.ds(pl.multiple_of(k * NLAT, NLAT), NLAT)
-
-            @pl.when(odd)
-            def _():
-                pltpu.make_async_copy(buf.at[s, 0], o.at[rows], sems.at[s, 1]).wait()
-                pltpu.make_async_copy(buf.at[s, 1], dq.at[rows], sems.at[s, 2]).wait()
+    ctx, lead = here[0], lead_ref[0]
+
+    def odd(s):
+        return sends(ctx, s) & (images[step_block(ctx, s)] != lead)
+
+    def load(s):
+        return pltpu.make_async_copy((r0, r1)[s], buf.at[s], sems.at[s, 0])
+
+    def stores(s):
+        rows = pl.ds(pl.multiple_of(step_block(ctx, s) * NLAT, NLAT), NLAT)
+        return (
+            pltpu.make_async_copy(buf.at[s, 0], o.at[rows], sems.at[s, 1]),
+            pltpu.make_async_copy(buf.at[s, 1], dq.at[rows], sems.at[s, 2]),
+        )
+
+    for s in range(2):
+
+        @pl.when(odd(s))
+        def _():
+            load(s).start()
+
+    for s in range(2):
+
+        @pl.when(odd(s))
+        def _():
+            load(s).wait()
+            for copy in stores(s):
+                copy.start()
+
+    for s in range(2):
+
+        @pl.when(odd(s))
+        def _():
+            for copy in stores(s):
+                copy.wait()
 
 
 VM = pl.BlockSpec(memory_space=pltpu.VMEM)
@@ -373,19 +394,12 @@
     )
 
 
-def over_dp(x):
-    for far in (1, 2, 4):
-        x = x + lax.ppermute(x, "dp", [(s, s ^ far) for s in range(8)])
-    return x
-
-
 def body(queries, latent_kv, media, gate, grad_out):
     q, g, kv_rows = queries[0], grad_out[0], latent_kv[0]
     tokens, width = q.shape
     here = lax.axis_index(CTX).astype(jnp.int32)[None]
     images = media[0]
-    partner = lax.ppermute(images, "c", [(0, 1), (1, 0)])
-    where = (here, images, partner)
+    swap = [(0, 1), (1, 0)]
 
     packed = call(
         pack_kernel,
@@ -398,28 +412,30 @@
             pltpu.SemaphoreType.DMA((2, 2, 2)),
         ],
     )(here, q, g)
-    after = packed[:1] if DEP_CHUNK else []
     chunks = call(
         chunk_kernel,
         "chunk",
-        shape(8, QUART, COLS),
-        [HBM] * (1 + len(after)),
+        shape(8, QUART, WIDE),
+        [SM, HBM],
         VM,
         scratch_shapes=[pltpu.SemaphoreType.DMA((8,))],
-    )(kv_rows, *after)
+    )(images, kv_rows)
     mixed = lax.all_to_all(chunks, IMG, 0, 0, tiled=True)
     sent = [lax.ppermute(packed[s], CTX, BLOCK_PAIRS[s]) for s in range(2)]
     chip_rows = call(half_kernel, "half", shape(2 * QUART, 2 * width), [VM, VM], VM)(
-        kv_rows, lax.ppermute(kv_rows, "c", [(0, 1), (1, 0)])
+        kv_rows, lax.ppermute(kv_rows, "c", swap)
     )
     lent = [lax.ppermute(chip_rows, CTX, latent_pairs(s)) for s in range(4)]
 
-    after = sent[:DEP_SPREAD] + lent[:DEP_LENT]
-    spread = call(
-        spread_kernel, "spread", shape(16, QUART, COLS), [SM, SM, SM, VM, *[HBM] * len(after)], VM
-    )(*where, mixed, *after)
+    spread, lead = call(
+        spread_kernel,
+        "spread",
+        [shape(16, QUART, COLS), shape(1, dtype=jnp.int32)],
+        [VM],
+        [VM, SM],
+    )(mixed)
     mine = lax.all_to_all(spread, CHIP, 0, 0, tiled=True).reshape(2, 4, 2, QUART, COLS)
-    other = lax.ppermute(mine, "c", [(0, 1), (1, 0)])
+    other = lax.ppermute(mine, "c", swap)
 
     tanh_gate = jnp.tanh(gate)
     wide = pl.BlockSpec((tokens, COLS), lambda c: (0, c))
@@ -432,11 +448,11 @@
             shape(tokens, width),
             shape(2, NLAT, width),
             shape(16, QUART, COLS, dtype=F32),
-            shape(16, QUART, COLS),
+            shape(17, QUART, COLS),
             *[shape(2 * QUART, 2 * width)] * 4,
             shape(1, HS, dtype=F32),
         ],
-        [SM, SM, SM, SM, wide, wide, half, half, *[VM] * 4, *[HBM] * 2],
+        [SM, SM, SM, SM, wide, wide, half, half, *[VM] * 4, HBM, HBM],
         [wide, wide, pl.BlockSpec((2, NLAT, COLS), lambda c: (0, 0, c)), *[VM] * 7],
         grid=(4,),
         scratch_shapes=[
@@ -444,23 +460,18 @@
             pltpu.VMEM((HS, HS), F32),
             pltpu.SemaphoreType.DMA,
         ],
-    )(*where, tanh_gate, q, g, mine, other, *lent, *sent)
-
-    gsum = gpart + lax.ppermute(gpart, "c", [(0, 1), (1, 0)])
-    if GATE_FIRST:
-        gsum = over_dp(gsum)
-    theirs = lax.ppermute(opay, "c", [(0, 1), (1, 0)])
+    )(here, images, lead, tanh_gate, q, g, mine, other, *lent, *sent)
+
+    theirs = lax.ppermute(opay, "c", swap)
     paired = call(pair_kernel, "pair", shape(16, QUART, WIDE), [VM, VM, VM], VM)(
-        pay, theirs, gsum
+        pay, theirs, gpart
     )
     parts = lax.all_to_all(paired, CHIP, 0, 0, tiled=True)
-    owned = [
-        lax.ppermute(y, CTX, back(latent_pairs(s))) for s, y in enumerate((y0, y1, y2, y3))
-    ]
+    owned = [lax.ppermute(y, CTX, back(latent_pairs(s))) for s, y in enumerate((y0, y1, y2, y3))]
     own, give = call(
         sort_kernel, "sort", [shape(QUART, 2 * width)] * 2, [SM, *[VM] * 4], [VM, VM]
     )(here, *owned)
-    given = lax.ppermute(give, "c", [(0, 1), (1, 0)])
+    given = lax.ppermute(give, "c", swap)
     ready = [lax.ppermute(xo, CTX, back(BLOCK_PAIRS[s])) for s in range(2)]
     summed, gates = call(
         collect_kernel,
@@ -469,12 +480,12 @@
         [VM],
         [VM, VM],
     )(parts)
-    if not GATE_FIRST:
-        gates = over_dp(gates)
+    for flip in (1, 2, 7):
+        gates = gates + lax.ppermute(gates, "dp", [(s, s ^ flip) for s in range(8)])
     final = lax.all_to_all(summed, IMG, 0, 0, tiled=True)
     latent_grad = call(
-        assemble_kernel, "assemble", shape(QUART, 2 * width), [SM, SM, SM, VM, VM, VM], VM
-    )(*where, final, own, given)
+        assemble_kernel, "assemble", shape(QUART, 2 * width), [SM, SM, VM, VM, VM], VM
+    )(here, lead, final, own, given)
     o, dq = call(
         merge_kernel,
         "merge",
@@ -486,7 +497,7 @@
             pltpu.SemaphoreType.DMA((2, 3)),
         ],
         input_output_aliases={3: 0, 4: 1},
-    )(*where, o, dq, *ready)
+    )(here, images, lead, o, dq, *ready)
     gate_grad = (1.0 - tanh_gate * tanh_gate) * gates[0, :HEADS]
     return o[None], dq[None], latent_grad[None], gate_grad
 

time: 135 us -> 131 us (0.970)
  starting transfers between devices: 86 us -> 74.6 us
  waiting for transfers between devices: 24.4 us -> 30 us
  local copies, waits for them, and re-layouts: 3.68 us -> 5.26 us
    ppermute x9 -> x7, starting transfers between devices: 35 us -> 19.3 us  [the longest x3 10.7 us: body(): gates = gates + lax.ppermute(gates, 'dp', [(s, s ^ flip) for s in range(8)])]
    ppermute x4, waiting for transfers between devices: 0.01 us -> 13.2 us  [body(): lax.ppermute(y, CTX, back(latent_pairs(s)))]
    ppermute x4, waiting for transfers between devices: 8.18 us -> 0.01 us  [body(): lent = [lax.ppermute(chip_rows, CTX, latent_pairs(s)) for s in range(4)]]
    all_to_all x1, starting transfers between devices: 8.02 us -> 15.7 us  [body(): parts = lax.all_to_all(paired, CHIP, 0, 0, tiled=True)]
    all_to_all x1, waiting for transfers between devices: 4.55 us -> 11 us  [body(): lax.all_to_all(spread, CHIP, 0, 0, tiled=True).reshape(2, 4, 2, QUART, COLS)]
    all_to_all x1, waiting for transfers between devices: 5.55 us -> 0.89 us  [body(): parts = lax.all_to_all(paired, CHIP, 0, 0, tiled=True)]
    all_to_all x1, starting transfers between devices: 8.9 us -> 6.12 us  [body(): final = lax.all_to_all(summed, IMG, 0, 0, tiled=True)]
    unnamed x10 -> x14, local copies, waits for them, and re-layouts: 3.68 us -> 5.25 us
  transfers between devices with their start and end apart: 25 -> 23, of which waited for: 9 -> 7; matrix products, arithmetic and copies ran while one was open for 0% -> 0% of each run, Pallas kernels for 6% -> 6%
where the time goes in v4:
time: 131 us; the launch traced here: 130 us
  starting transfers between devices  74.6 us (57%)
  waiting for transfers between devices  30 us (23%)
  Pallas kernels  18.7 us (14%)
  local copies, waits for them, and re-layouts  5.26 us (4%)
    all_to_all x1, starting transfers between devices, body(): parts = lax.all_to_all(paired, CHIP, 0, 0, tiled=True)  15.7 us
    ppermute x4, waiting for transfers between devices, body(): lax.ppermute(y, CTX, back(latent_pairs(s)))  13.2 us
    all_to_all x1, starting transfers between devices, body(): lax.all_to_all(spread, CHIP, 0, 0, tiled=True).reshape(2, 4, 2, QUART, COLS)  11.3 us
    all_to_all x1, waiting for transfers between devices, body(): lax.all_to_all(spread, CHIP, 0, 0, tiled=True).reshape(2, 4, 2, QUART, COLS)  11 us
    ppermute x3, starting transfers between devices, body(): gates = gates + lax.ppermute(gates, 'dp', [(s, s ^ flip) for s in range(8)])  10.7 us
    pallas_call x1, Pallas kernels, body(): call(attention_kernel, 'attention', [shape(tokens, width), shape(tokens,...  9.65 us
    all_to_all x1, starting transfers between devices, body(): mixed = lax.all_to_all(chunks, IMG, 0, 0, tiled=True)  7.27 us
    ppermute x1, starting transfers between devices, body(): other = lax.ppermute(mine, 'c', swap)  6.16 us
  transfers between devices with their start and end apart: 23, of which 7 were waited for; matrix products, arithmetic and copies ran while one was open for 0% of the time, Pallas kernels for 6%

profile of v4, /device:TPU:24, one launch (start us, length us, event | category | flops | bytes accessed | tf_op | source)
XLA Modules:
  0.0 130.0 jit_solution(7823156625626259871)
XLA Ops:
  0.7 0.9 copy-done.2
  2.3 1.5 %chunk.1 = bf16[8,16,1152]{2,1,0:T(8,128)(2,1)} custom-call(s32[4]{0:T(128)S(1)} %bitcast.18, bf16[16,8192]{1,0:T(8,128)(2,1)S(1)} %bitcast.16), custom_call_target="tpu_custom_call" | custom-call | tf_op jit(solution)/shard_map/chunk/pallas_call | solution.py:415
  3.9 7.3 %all-to-all-start = ((bf16[8,16,1152]{2,1,0:T(8,128)(2,1)}), bf16[8,16,1152]{2,1,0:T(8,128)(2,1)S(1)}, u32[]{:S(2)}, u32[]{:S(2)}) async-start(bf16[8,16,1152]{2,1,0:T(8,128)(2,1)} %chunk.1), calls=%async_computation | async-start | bytes 589824 | tf_op jit(solution)/shard_map/all_to_all | solution.py:423
  11.1 1.6 %copy-done = bf16[1,256,4096]{2,1,0:T(8,128)(2,1)S(1)} copy-done((bf16[1,256,4096]{2,1,0:T(8,128)(2,1)S(1)}, bf16[1,256,4096]{2,1,0:T(8,128)(2,1)}, u32[]{:S(2)}) %copy-start) | copy-done | bytes 2097176
  12.8 0.8 copy-done.3
  13.7 3.3 %collective-permute-start.5 = (bf16[32,8192]{1,0:T(8,128)(2,1)S(1)}, bf16[32,8192]{1,0:T(8,128)(2,1)S(1)}, u32[]{:S(2)}, u32[]{:S(2)}) collective-permute-start(bf16[32,8192]{1,0:T(8,128)(2,1)S(1)} %half.1), channel_id=1, source_target_pairs={{10,0},{11,30},{27,31},{26,1},{2,2},{6,8},{7,22},{18,7},{22,25},{4... | collective-permute-start | bytes 1572872 | tf_op jit(solution)/shard_map/ppermute | solution.py:428
  17.0 1.6 %collective-permute-start.6 = (bf16[2,64,4096]{2,1,0:T(8,128)(2,1)}, bf16[2,64,4096]{2,1,0:T(8,128)(2,1)}, u32[]{:S(2)}, u32[]{:S(2)}) collective-permute-start(bf16[2,64,4096]{2,1,0:T(8,128)(2,1)} %get-tuple-element.26), channel_id=1, source_target_pairs={{0,2},{1,7},{31,25},{32,34},{33,39},{63,57},{64,66},{65,71},{95,89... | collective-permute-start | bytes 3145736 | tf_op jit(solution)/shard_map/ppermute | solution.py:424
  19.3 1.7 %collective-permute-start.7 = (bf16[2,64,4096]{2,1,0:T(8,128)(2,1)}, bf16[2,64,4096]{2,1,0:T(8,128)(2,1)}, u32[]{:S(2)}, u32[]{:S(2)}) collective-permute-start(bf16[2,64,4096]{2,1,0:T(8,128)(2,1)} %get-tuple-element.27), channel_id=1, source_target_pairs={{0,8},{1,25},{30,22},{31,7},{32,40},{33,57},{62,54},{63,39},{64,72... | collective-permute-start | bytes 3145736 | tf_op jit(solution)/shard_map/ppermute | solution.py:424
  21.0 0.9 spread.1
  21.9 11.3 %all-to-all-start.1 = ((bf16[16,16,1024]{2,1,0:T(8,128)(2,1)}), bf16[16,16,1024]{2,1,0:T(8,128)(2,1)S(1)}, u32[]{:S(2)}, u32[]{:S(2)}) async-start(bf16[16,16,1024]{2,1,0:T(8,128)(2,1)} %get-tuple-element.25), calls=%async_computation.1 | async-start | bytes 1048576 | tf_op jit(solution)/shard_map/all_to_all | solution.py:437
  34.6 11.0 %all-to-all-done.1 = bf16[16,16,1024]{2,1,0:T(8,128)(2,1)S(1)} async-done(((bf16[16,16,1024]{2,1,0:T(8,128)(2,1)}), bf16[16,16,1024]{2,1,0:T(8,128)(2,1)S(1)}, u32[]{:S(2)}, u32[]{:S(2)}) %all-to-all-start.1) | async-done | bytes 524320 | tf_op jit(solution)/shard_map/all_to_all | solution.py:437
  45.7 6.2 %collective-permute-start = (bf16[2,4,2,16,1024]{4,3,2,1,0:T(8,128)(2,1)S(1)}, bf16[2,4,2,16,1024]{4,3,2,1,0:T(8,128)(2,1)S(1)}, u32[]{:S(2)}, u32[]{:S(2)}) collective-permute-start(bf16[2,4,2,16,1024]{4,3,2,1,0:T(8,128)(2,1)S(1)} %bitcast.13), channel_id=1, source_target_pairs={{0,1},{1,0},{2,3},{3,2},{4,5},{5,4},{6,7},{7,6},{8,9},{9,8},{10,11... | collective-permute-start | bytes 1572872 | tf_op jit(solution)/shard_map/ppermute | solution.py:438
  51.9 1.5 %collective-permute-done.other = bf16[2,4,2,16,1024]{4,3,2,1,0:T(8,128)(2,1)S(1)} collective-permute-done((bf16[2,4,2,16,1024]{4,3,2,1,0:T(8,128)(2,1)S(1)}, bf16[2,4,2,16,1024]{4,3,2,1,0:T(8,128)(2,1)S(1)}, u32[]{:S(2)}, u32[]{:S(2)}) %collective-permute-start) | collective-permute-done | bytes 524320 | tf_op jit(solution)/shard_map/ppermute | solution.py:438
  53.4 9.6 %attention.1 = (bf16[256,4096]{1,0:T(8,128)(2,1)}, bf16[256,4096]{1,0:T(8,128)(2,1)}, bf16[2,64,4096]{2,1,0:T(8,128)(2,1)}, f32[16,16,1024]{2,1,0:T(8,128)}, bf1...) custom-call(s32[1]{0:T(128)} %bitcast.here, ...), custom_call_target="tpu_custom_call" | custom-call | tf_op jit(solution)/shard_map/attention/pallas_call | solution.py:443
  63.0 2.3 %collective-permute-start.10 = (bf16[17,16,1024]{2,1,0:T(8,128)(2,1)S(1)}, bf16[17,16,1024]{2,1,0:T(8,128)(2,1)S(1)}, u32[]{:S(2)}, u32[]{:S(2)}) collective-permute-start(bf16[17,16,1024]{2,1,0:T(8,128)(2,1)S(1)} %get-tuple-element.34), channel_id=1, source_target_pairs={{0,1},{1,0},{2,3},{3,2},{4,5},{5,4},{6,7},{7,6},{8,9},{9,8},{10,11... | collective-permute-start | bytes 1671176 | tf_op jit(solution)/shard_map/ppermute | solution.py:465
  67.5 1.5 %collective-permute-start.12 = (bf16[32,8192]{1,0:T(8,128)(2,1)}, bf16[32,8192]{1,0:T(8,128)(2,1)}, u32[]{:S(2)}, u32[]{:S(2)}) collective-permute-start(bf16[32,8192]{1,0:T(8,128)(2,1)} %get-tuple-element.38), channel_id=1, source_target_pairs={{0,14},{30,15},{31,31},{32,46},{62,47},{63,63},{64,78},{94,79},{95... | collective-permute-start | bytes 1572872 | tf_op jit(solution)/shard_map/ppermute | solution.py:470
  69.0 1.5 %collective-permute-start.13 = (bf16[32,8192]{1,0:T(8,128)(2,1)}, bf16[32,8192]{1,0:T(8,128)(2,1)}, u32[]{:S(2)}, u32[]{:S(2)}) collective-permute-start(bf16[32,8192]{1,0:T(8,128)(2,1)} %get-tuple-element.39), channel_id=1, source_target_pairs={{0,8},{30,9},{31,25},{1,24},{2,0},{8,4},{22,5},{7,16},{25,20},{32,... | collective-permute-start | bytes 1572872 | tf_op jit(solution)/shard_map/ppermute | solution.py:470
  70.4 1.3 collective-permute-start.14
  71.7 1.2 copy-done.1
  72.9 1.0 pair.1
  74.0 15.7 %all-to-all-start.2 = ((bf16[16,16,1152]{2,1,0:T(8,128)(2,1)}), bf16[16,16,1152]{2,1,0:T(8,128)(2,1)S(1)}, u32[]{:S(2)}, u32[]{:S(2)}) async-start(bf16[16,16,1152]{2,1,0:T(8,128)(2,1)} %pair.1), calls=%async_computation.2 | async-start | bytes 1179648 | tf_op jit(solution)/shard_map/all_to_all | solution.py:469
  89.7 13.2 %collective-permute-done.14.r3 = bf16[32,8192]{1,0:T(8,128)(2,1)} collective-permute-done((bf16[32,8192]{1,0:T(8,128)(2,1)}, bf16[32,8192]{1,0:T(8,128)(2,1)}, u32[]{:S(2)}, u32[]{:S(2)}) %collective-permute-start.14) | collective-permute-done | bytes 524320 | tf_op jit(solution)/shard_map/ppermute | solution.py:470
  102.9 2.1 %sort.1 = (bf16[16,8192]{1,0:T(8,128)(2,1)S(1)}, bf16[16,8192]{1,0:T(8,128)(2,1)}) custom-call(s32[1]{0:T(128)} %bitcast.here, bf16[32,8192]{1,0:T(8,128)(2,1)S(1)} %collective-permute-done.11.r0, bf16[32,8192]{1,0:T(8,128)(2,1)} %collective-permute-done.12.r1, bf16[32,8192]{1,0:T(8,128)(2,1)} %collective-permute-done.13.r2, ...), custom_call_target="tpu_custom_call" | custom-call | tf_op jit(solution)/shard_map/sort/pallas_call | solution.py:471
  105.0 0.9 all-to-all-done.2.got
  106.6 6.1 %all-to-all-start.3 = ((bf16[8,16,1024]{2,1,0:T(8,128)(2,1)}), bf16[8,16,1024]{2,1,0:T(8,128)(2,1)S(1)}, u32[]{:S(2)}, u32[]{:S(2)}) async-start(bf16[8,16,1024]{2,1,0:T(8,128)(2,1)} %get-tuple-element.36), calls=%async_computation.3 | async-start | bytes 524288 | tf_op jit(solution)/shard_map/all_to_all | solution.py:485
  112.8 1.9 %collective-permute-start.16 = (f32[1,128]{1,0:T(1,128)S(1)}, f32[1,128]{1,0:T(1,128)S(1)}, u32[]{:S(2)}, u32[]{:S(2)}) collective-permute-start(f32[1,128]{1,0:T(1,128)S(1)} %get-tuple-element.43), channel_id=1, source_target_pairs={{0,32},{32,0},{64,96},{96,64},{128,160},{160,128},{192,224},{224,1... | collective-permute-start | bytes 1544 | tf_op jit(solution)/shard_map/ppermute | solution.py:484
  114.7 1.6 %collective-permute-done.16 = f32[1,128]{1,0:T(1,128)S(1)} collective-permute-done((f32[1,128]{1,0:T(1,128)S(1)}, f32[1,128]{1,0:T(1,128)S(1)}, u32[]{:S(2)}, u32[]{:S(2)}) %collective-permute-start.16) | collective-permute-done | bytes 544 | tf_op jit(solution)/shard_map/ppermute | solution.py:484
  116.3 3.3 %collective-permute-start.17 = (f32[1,128]{1,0:T(1,128)S(1)}, f32[1,128]{1,0:T(1,128)S(1)}, u32[]{:S(2)}, u32[]{:S(2)}) collective-permute-start(f32[1,128]{1,0:T(1,128)S(1)} %add.21), channel_id=1, source_target_pairs={{0,64},{32,96},{64,0},{96,32},{128,192},{160,224},{192,128},{224,1... | collective-permute-start | bytes 1544 | tf_op jit(solution)/shard_map/ppermute | solution.py:484
  119.6 1.5 %collective-permute-done.17 = f32[1,128]{1,0:T(1,128)S(1)} collective-permute-done((f32[1,128]{1,0:T(1,128)S(1)}, f32[1,128]{1,0:T(1,128)S(1)}, u32[]{:S(2)}, u32[]{:S(2)}) %collective-permute-start.17) | collective-permute-done | bytes 544 | tf_op jit(solution)/shard_map/ppermute | solution.py:484
  121.1 5.5 %collective-permute-start.18 = (f32[1,128]{1,0:T(1,128)S(1)}, f32[1,128]{1,0:T(1,128)S(1)}, u32[]{:S(2)}, u32[]{:S(2)}) collective-permute-start(f32[1,128]{1,0:T(1,128)S(1)} %add.22), channel_id=1, source_target_pairs={{0,224},{32,192},{64,160},{96,128},{128,96},{160,64},{192,32},{224... | collective-permute-start | bytes 1544 | tf_op jit(solution)/shard_map/ppermute | solution.py:484
  126.6 1.3 merge.1
  128.7 1.4 %assemble.1 = bf16[16,8192]{1,0:T(8,128)(2,1)} custom-call(s32[1]{0:T(128)} %bitcast.here, s32[1]{0:T(128)} %get-tuple-element.24.lead_ref, bf16[8,16,1024]{2,1,0:T(8,128)(2,1)S(1)} %all-to-all-done.3.got, bf16[16,8192]{1,0:T(8,128)(2,1)S(1)} %get-tuple-element.41.own, bf16[16,8192]{1,0:T(8,128)(2,1)S(1)} %collective-permute-done.15.given), custom_call_target="tpu_custom_call" | custom-call | tf_op jit(solution)/shard_map/assemble/pallas_call | solution.py:486
  (43 shorter events, 6.7 us)
Async XLA Ops:
  0.6 12.2 %collective-permute-start.1 = (bf16[16,8192]{1,0:T(8,128)(2,1)}, bf16[16,8192]{1,0:T(8,128)(2,1)S(1)}, u32[]{:S(2)}, u32[]{:S(2)}) collective-permute-start(bf16[16,8192]{1,0:T(8,128)(2,1)} %bitcast.15), channel_id=1, source_target_pairs={{0,1},{1,0},{2,3},{3,2},{4,5},{5,4},{6,7},{7,6},{8,9},{9,8},{10,11... | collective-permute-start | bytes 786440 | tf_op jit(solution)/shard_map/ppermute | solution.py:426
  0.7 1.0 copy-start.2
  1.7 0.7 copy-start.4
  3.9 17.1 %all-to-all-start = ((bf16[8,16,1152]{2,1,0:T(8,128)(2,1)}), bf16[8,16,1152]{2,1,0:T(8,128)(2,1)S(1)}, u32[]{:S(2)}, u32[]{:S(2)}) async-start(bf16[8,16,1152]{2,1,0:T(8,128)(2,1)} %chunk.1), calls=%async_computation | async-start | bytes 589824 | tf_op jit(solution)/shard_map/all_to_all | solution.py:423
  11.1 1.6 %copy-start = (bf16[1,256,4096]{2,1,0:T(8,128)(2,1)S(1)}, bf16[1,256,4096]{2,1,0:T(8,128)(2,1)}, u32[]{:S(2)}) copy-start(bf16[1,256,4096]{2,1,0:T(8,128)(2,1)} %param.5) | copy-start | bytes 6291460
  12.7 0.9 copy-start.3
  12.8 39.0 %copy-start.6 = (f32[32]{0:T(128)S(1)}, f32[32]{0:T(128)}, u32[]{:S(2)}) copy-start(f32[32]{0:T(128)} %param.8) | copy-start | bytes 388
  12.8 40.5 %copy-start.5 = (s32[1,4]{1,0:T(1,128)S(1)}, s32[1,4]{1,0:T(1,128)}, u32[]{:S(2)}) copy-start(s32[1,4]{1,0:T(1,128)} %param.7) | copy-start | bytes 52
  13.7 20.2 %collective-permute-start.5 = (bf16[32,8192]{1,0:T(8,128)(2,1)S(1)}, bf16[32,8192]{1,0:T(8,128)(2,1)S(1)}, u32[]{:S(2)}, u32[]{:S(2)}) collective-permute-start(bf16[32,8192]{1,0:T(8,128)(2,1)S(1)} %half.1), channel_id=1, source_target_pairs={{10,0},{11,30},{27,31},{26,1},{2,2},{6,8},{7,22},{18,7},{22,25},{4... | collective-permute-start | bytes 1572872 | tf_op jit(solution)/shard_map/ppermute | solution.py:428
  17.0 34.8 %collective-permute-start.6 = (bf16[2,64,4096]{2,1,0:T(8,128)(2,1)}, bf16[2,64,4096]{2,1,0:T(8,128)(2,1)}, u32[]{:S(2)}, u32[]{:S(2)}) collective-permute-start(bf16[2,64,4096]{2,1,0:T(8,128)(2,1)} %get-tuple-element.26), channel_id=1, source_target_pairs={{0,2},{1,7},{31,25},{32,34},{33,39},{63,57},{64,66},{65,71},{95,89... | collective-permute-start | bytes 3145736 | tf_op jit(solution)/shard_map/ppermute | solution.py:424
  18.6 27.0 %collective-permute-start.4 = (bf16[32,8192]{1,0:T(8,128)(2,1)S(1)}, bf16[32,8192]{1,0:T(8,128)(2,1)S(1)}, u32[]{:S(2)}, u32[]{:S(2)}) collective-permute-start(bf16[32,8192]{1,0:T(8,128)(2,1)S(1)} %half.1), channel_id=1, source_target_pairs={{8,0},{9,30},{25,31},{24,1},{0,2},{4,8},{5,22},{16,7},{20,25},{40,... | collective-permute-start | bytes 1572872 | tf_op jit(solution)/shard_map/ppermute | solution.py:428
  19.3 32.5 %collective-permute-start.7 = (bf16[2,64,4096]{2,1,0:T(8,128)(2,1)}, bf16[2,64,4096]{2,1,0:T(8,128)(2,1)}, u32[]{:S(2)}, u32[]{:S(2)}) collective-permute-start(bf16[2,64,4096]{2,1,0:T(8,128)(2,1)} %get-tuple-element.27), channel_id=1, source_target_pairs={{0,8},{1,25},{30,22},{31,7},{32,40},{33,57},{62,54},{63,39},{64,72... | collective-permute-start | bytes 3145736 | tf_op jit(solution)/shard_map/ppermute | solution.py:424
  21.9 23.7 %all-to-all-start.1 = ((bf16[16,16,1024]{2,1,0:T(8,128)(2,1)}), bf16[16,16,1024]{2,1,0:T(8,128)(2,1)S(1)}, u32[]{:S(2)}, u32[]{:S(2)}) async-start(bf16[16,16,1024]{2,1,0:T(8,128)(2,1)} %get-tuple-element.25), calls=%async_computation.1 | async-start | bytes 1048576 | tf_op jit(solution)/shard_map/all_to_all | solution.py:437
  33.2 18.6 %collective-permute-start.3 = (bf16[32,8192]{1,0:T(8,128)(2,1)S(1)}, bf16[32,8192]{1,0:T(8,128)(2,1)S(1)}, u32[]{:S(2)}, u32[]{:S(2)}) collective-permute-start(bf16[32,8192]{1,0:T(8,128)(2,1)S(1)} %half.1), channel_id=1, source_target_pairs={{14,0},{15,30},{31,31},{46,32},{47,62},{63,63},{78,64},{79,94},{95... | collective-permute-start | bytes 1572872 | tf_op jit(solution)/shard_map/ppermute | solution.py:428
  33.9 17.9 %collective-permute-start.2 = (bf16[32,8192]{1,0:T(8,128)(2,1)S(1)}, bf16[32,8192]{1,0:T(8,128)(2,1)S(1)}, u32[]{:S(2)}, u32[]{:S(2)}) collective-permute-start(bf16[32,8192]{1,0:T(8,128)(2,1)S(1)} %half.1), channel_id=1, source_target_pairs={{12,0},{13,30},{29,31},{44,32},{45,62},{61,63},{76,64},{77,94},{93... | collective-permute-start | bytes 1572872 | tf_op jit(solution)/shard_map/ppermute | solution.py:428
  45.7 7.7 %collective-permute-start = (bf16[2,4,2,16,1024]{4,3,2,1,0:T(8,128)(2,1)S(1)}, bf16[2,4,2,16,1024]{4,3,2,1,0:T(8,128)(2,1)S(1)}, u32[]{:S(2)}, u32[]{:S(2)}) collective-permute-start(bf16[2,4,2,16,1024]{4,3,2,1,0:T(8,128)(2,1)S(1)} %bitcast.13), channel_id=1, source_target_pairs={{0,1},{1,0},{2,3},{3,2},{4,5},{5,4},{6,7},{7,6},{8,9},{9,8},{10,11... | collective-permute-start | bytes 1572872 | tf_op jit(solution)/shard_map/ppermute | solution.py:438
  63.0 7.4 %collective-permute-start.10 = (bf16[17,16,1024]{2,1,0:T(8,128)(2,1)S(1)}, bf16[17,16,1024]{2,1,0:T(8,128)(2,1)S(1)}, u32[]{:S(2)}, u32[]{:S(2)}) collective-permute-start(bf16[17,16,1024]{2,1,0:T(8,128)(2,1)S(1)} %get-tuple-element.34), channel_id=1, source_target_pairs={{0,1},{1,0},{2,3},{3,2},{4,5},{5,4},{6,7},{7,6},{8,9},{9,8},{10,11... | collective-permute-start | bytes 1671176 | tf_op jit(solution)/shard_map/ppermute | solution.py:465
  65.3 3.6 %collective-permute-start.11 = (bf16[32,8192]{1,0:T(8,128)(2,1)S(1)}, bf16[32,8192]{1,0:T(8,128)(2,1)S(1)}, u32[]{:S(2)}, u32[]{:S(2)}) collective-permute-start(bf16[32,8192]{1,0:T(8,128)(2,1)S(1)} %get-tuple-element.37), channel_id=1, source_target_pairs={{0,12},{30,13},{31,29},{32,44},{62,45},{63,61},{64,76},{94,77},{95... | collective-permute-start | bytes 1572872 | tf_op jit(solution)/shard_map/ppermute | solution.py:470
  66.0 60.6 %collective-permute-start.9 = (bf16[2,64,4096]{2,1,0:T(8,128)(2,1)}, bf16[2,64,4096]{2,1,0:T(8,128)(2,1)S(1)}, u32[]{:S(2)}, u32[]{:S(2)}) collective-permute-start(bf16[2,64,4096]{2,1,0:T(8,128)(2,1)} %get-tuple-element.30), channel_id=1, source_target_pairs={{8,0},{25,1},{22,30},{7,31},{40,32},{57,33},{54,62},{39,63},{72,64... | collective-permute-start | bytes 3145736 | tf_op jit(solution)/shard_map/ppermute | solution.py:475
  66.8 59.8 %collective-permute-start.8 = (bf16[2,64,4096]{2,1,0:T(8,128)(2,1)}, bf16[2,64,4096]{2,1,0:T(8,128)(2,1)S(1)}, u32[]{:S(2)}, u32[]{:S(2)}) collective-permute-start(bf16[2,64,4096]{2,1,0:T(8,128)(2,1)} %get-tuple-element.30), channel_id=1, source_target_pairs={{2,0},{7,1},{25,31},{34,32},{39,33},{57,63},{66,64},{71,65},{89,95... | collective-permute-start | bytes 3145736 | tf_op jit(solution)/shard_map/ppermute | solution.py:475
  67.5 22.2 %collective-permute-start.12 = (bf16[32,8192]{1,0:T(8,128)(2,1)}, bf16[32,8192]{1,0:T(8,128)(2,1)}, u32[]{:S(2)}, u32[]{:S(2)}) collective-permute-start(bf16[32,8192]{1,0:T(8,128)(2,1)} %get-tuple-element.38), channel_id=1, source_target_pairs={{0,14},{30,15},{31,31},{32,46},{62,47},{63,63},{64,78},{94,79},{95... | collective-permute-start | bytes 1572872 | tf_op jit(solution)/shard_map/ppermute | solution.py:470
  69.0 20.7 %collective-permute-start.13 = (bf16[32,8192]{1,0:T(8,128)(2,1)}, bf16[32,8192]{1,0:T(8,128)(2,1)}, u32[]{:S(2)}, u32[]{:S(2)}) collective-permute-start(bf16[32,8192]{1,0:T(8,128)(2,1)} %get-tuple-element.39), channel_id=1, source_target_pairs={{0,8},{30,9},{31,25},{1,24},{2,0},{8,4},{22,5},{7,16},{25,20},{32,... | collective-permute-start | bytes 1572872 | tf_op jit(solution)/shard_map/ppermute | solution.py:470
  70.4 32.4 %collective-permute-start.14 = (bf16[32,8192]{1,0:T(8,128)(2,1)}, bf16[32,8192]{1,0:T(8,128)(2,1)}, u32[]{:S(2)}, u32[]{:S(2)}) collective-permute-start(bf16[32,8192]{1,0:T(8,128)(2,1)} %get-tuple-element.40), channel_id=1, source_target_pairs={{0,10},{30,11},{31,27},{1,26},{2,2},{8,6},{22,7},{7,18},{25,22},{3... | collective-permute-start | bytes 1572872 | tf_op jit(solution)/shard_map/ppermute | solution.py:470
  71.7 1.2 copy-start.1
  74.0 31.9 %all-to-all-start.2 = ((bf16[16,16,1152]{2,1,0:T(8,128)(2,1)}), bf16[16,16,1152]{2,1,0:T(8,128)(2,1)S(1)}, u32[]{:S(2)}, u32[]{:S(2)}) async-start(bf16[16,16,1152]{2,1,0:T(8,128)(2,1)} %pair.1), calls=%async_computation.2 | async-start | bytes 1179648 | tf_op jit(solution)/shard_map/all_to_all | solution.py:469
  105.0 23.7 %collective-permute-start.15 = (bf16[16,8192]{1,0:T(8,128)(2,1)}, bf16[16,8192]{1,0:T(8,128)(2,1)S(1)}, u32[]{:S(2)}, u32[]{:S(2)}) collective-permute-start(bf16[16,8192]{1,0:T(8,128)(2,1)} %get-tuple-element.42), channel_id=1, source_target_pairs={{0,1},{1,0},{2,3},{3,2},{4,5},{5,4},{6,7},{7,6},{8,9},{9,8},{10,11... | collective-permute-start | bytes 786440 | tf_op jit(solution)/shard_map/ppermute | solution.py:474
  106.6 22.0 %all-to-all-start.3 = ((bf16[8,16,1024]{2,1,0:T(8,128)(2,1)}), bf16[8,16,1024]{2,1,0:T(8,128)(2,1)S(1)}, u32[]{:S(2)}, u32[]{:S(2)}) async-start(bf16[8,16,1024]{2,1,0:T(8,128)(2,1)} %get-tuple-element.36), calls=%async_computation.3 | async-start | bytes 524288 | tf_op jit(solution)/shard_map/all_to_all | solution.py:485
  112.8 3.5 %collective-permute-start.16 = (f32[1,128]{1,0:T(1,128)S(1)}, f32[1,128]{1,0:T(1,128)S(1)}, u32[]{:S(2)}, u32[]{:S(2)}) collective-permute-start(f32[1,128]{1,0:T(1,128)S(1)} %get-tuple-element.43), channel_id=1, source_target_pairs={{0,32},{32,0},{64,96},{96,64},{128,160},{160,128},{192,224},{224,1... | collective-permute-start | bytes 1544 | tf_op jit(solution)/shard_map/ppermute | solution.py:484
  116.3 4.8 %collective-permute-start.17 = (f32[1,128]{1,0:T(1,128)S(1)}, f32[1,128]{1,0:T(1,128)S(1)}, u32[]{:S(2)}, u32[]{:S(2)}) collective-permute-start(f32[1,128]{1,0:T(1,128)S(1)} %add.21), channel_id=1, source_target_pairs={{0,64},{32,96},{64,0},{96,32},{128,192},{160,224},{192,128},{224,1... | collective-permute-start | bytes 1544 | tf_op jit(solution)/shard_map/ppermute | solution.py:484
  121.1 7.0 %collective-permute-start.18 = (f32[1,128]{1,0:T(1,128)S(1)}, f32[1,128]{1,0:T(1,128)S(1)}, u32[]{:S(2)}, u32[]{:S(2)}) collective-permute-start(f32[1,128]{1,0:T(1,128)S(1)} %add.22), channel_id=1, source_target_pairs={{0,224},{32,192},{64,160},{96,128},{128,96},{160,64},{192,32},{224... | collective-permute-start | bytes 1544 | tf_op jit(solution)/shard_map/ppermute | solution.py:484

commit v5 on v4

--- a/solution.py
+++ b/solution.py
@@ -77,20 +77,11 @@
     return (ctx < 2) | (ctx == 31) | ((ctx == 30) & (s == 1))
 
 
-def chunk_kernel(images, src, dst, sems):
-    copies = [
-        pltpu.make_async_copy(
-            src.at[:, pl.ds(i * COLS, COLS)], dst.at[i, :, pl.ds(0, COLS)], sems.at[i]
-        )
-        for i in range(8)
-    ]
-    for copy in copies:
-        copy.start()
+def chunk_kernel(images, src, dst):
     known = jnp.full((QUART, WIDE - COLS), images[0].astype(F32)).astype(BF)
     for i in range(8):
+        dst[i, :, 0:COLS] = src[:, i * COLS : (i + 1) * COLS]
         dst[i, :, COLS:WIDE] = known
-    for copy in copies:
-        copy.wait()
 
 
 def pack_kernel(here, q, g, d0, d1, buf, sems):
@@ -298,15 +289,19 @@
         dst[j] = val
 
 
-def sort_kernel(here, r0, r1, r2, r3, own, give):
+def sort_kernel(here, r0, r1, r2, r3, own, give, sems):
     chip = here[0] // 2
     step = jnp.where(chip // 4 % 2 == 0, chip % 2, chip % 4)
     for s, r in enumerate((r2, r3, r0, r1)):
 
         @pl.when(step == s)
         def _():
-            own[...] = r[0:QUART]
-            give[...] = r[QUART : 2 * QUART]
+            first = pltpu.make_async_copy(r.at[pl.ds(0, QUART)], own, sems.at[0])
+            second = pltpu.make_async_copy(r.at[pl.ds(QUART, QUART)], give, sems.at[1])
+            first.start()
+            second.start()
+            first.wait()
+            second.wait()
 
 
 def assemble_kernel(here, lead_ref, got, own, given, dst):
@@ -373,15 +368,16 @@
 HBM = pl.BlockSpec(memory_space=pltpu.HBM)
 ANY = pl.BlockSpec(memory_space=pl.ANY)
 LIMIT = 48 * 1024 * 1024
+SMALL = 16 * 1024 * 1024
 
 
 def shape(*dims, dtype=BF):
     return jax.ShapeDtypeStruct(dims, dtype)
 
 
-def call(kernel, name, out_shape, in_specs, out_specs, cost=(0, 0), **more):
+def call(kernel, name, out_shape, in_specs, out_specs, cost=(0, 0), limit=SMALL, **more):
     estimate = pl.CostEstimate(flops=cost[0], bytes_accessed=cost[1], transcendentals=0)
-    params = pltpu.CompilerParams(vmem_limit_bytes=LIMIT)
+    params = pltpu.CompilerParams(vmem_limit_bytes=limit)
     return pl.pallas_call(
         kernel,
         name=name,
@@ -407,19 +403,13 @@
         [shape(2, NLAT, width)] * 2,
         [SM, HBM, HBM],
         [HBM] * 2,
+        limit=62 * 1024 * 1024,
         scratch_shapes=[
             pltpu.VMEM((2, 2, NLAT, width), BF),
             pltpu.SemaphoreType.DMA((2, 2, 2)),
         ],
     )(here, q, g)
-    chunks = call(
-        chunk_kernel,
-        "chunk",
-        shape(8, QUART, WIDE),
-        [SM, HBM],
-        VM,
-        scratch_shapes=[pltpu.SemaphoreType.DMA((8,))],
-    )(images, kv_rows)
+    chunks = call(chunk_kernel, "chunk", shape(8, QUART, WIDE), [SM, VM], VM)(images, kv_rows)
     mixed = lax.all_to_all(chunks, IMG, 0, 0, tiled=True)
     sent = [lax.ppermute(packed[s], CTX, BLOCK_PAIRS[s]) for s in range(2)]
     chip_rows = call(half_kernel, "half", shape(2 * QUART, 2 * width), [VM, VM], VM)(
@@ -455,6 +445,7 @@
         [SM, SM, SM, SM, wide, wide, half, half, *[VM] * 4, HBM, HBM],
         [wide, wide, pl.BlockSpec((2, NLAT, COLS), lambda c: (0, 0, c)), *[VM] * 7],
         grid=(4,),
+        limit=LIMIT,
         scratch_shapes=[
             pltpu.VMEM((2, NLAT, width), BF),
             pltpu.VMEM((HS, HS), F32),
@@ -469,7 +460,12 @@
     parts = lax.all_to_all(paired, CHIP, 0, 0, tiled=True)
     owned = [lax.ppermute(y, CTX, back(latent_pairs(s))) for s, y in enumerate((y0, y1, y2, y3))]
     own, give = call(
-        sort_kernel, "sort", [shape(QUART, 2 * width)] * 2, [SM, *[VM] * 4], [VM, VM]
+        sort_kernel,
+        "sort",
+        [shape(QUART, 2 * width)] * 2,
+        [SM, *[ANY] * 4],
+        [VM, VM],
+        scratch_shapes=[pltpu.SemaphoreType.DMA((2,))],
     )(here, *owned)
     given = lax.ppermute(give, "c", swap)
     ready = [lax.ppermute(xo, CTX, back(BLOCK_PAIRS[s])) for s in range(2)]

time: 131 us -> 130 us (level)
  local copies, waits for them, and re-layouts: 5.26 us -> 3.67 us
    unnamed x14 -> x12, local copies, waits for them, and re-layouts: 5.25 us -> 3.66 us
where the time goes in v5:
time: 130 us; the launch traced here: 128 us
  starting transfers between devices  74.8 us (58%)
  waiting for transfers between devices  30.2 us (23%)
  Pallas kernels  18.2 us (14%)
  local copies, waits for them, and re-layouts  3.67 us (3%)
    all_to_all x1, starting transfers between devices, body(): parts = lax.all_to_all(paired, CHIP, 0, 0, tiled=True)  15.8 us
    ppermute x4, waiting for transfers between devices, body(): lax.ppermute(y, CTX, back(latent_pairs(s)))  13.2 us
    all_to_all x1, starting transfers between devices, body(): lax.all_to_all(spread, CHIP, 0, 0, tiled=True).reshape(2, 4, 2, QUART, COLS)  11.3 us
    all_to_all x1, waiting for transfers between devices, body(): lax.all_to_all(spread, CHIP, 0, 0, tiled=True).reshape(2, 4, 2, QUART, COLS)  11 us
    ppermute x3, starting transfers between devices, body(): gates = gates + lax.ppermute(gates, 'dp', [(s, s ^ flip) for s in range(8)])  10.7 us
    pallas_call x1, Pallas kernels, body(): call(attention_kernel, 'attention', [shape(tokens, width), shape(tokens,...  9.64 us
    all_to_all x1, starting transfers between devices, body(): mixed = lax.all_to_all(chunks, IMG, 0, 0, tiled=True)  7.26 us
    ppermute x1, starting transfers between devices, body(): other = lax.ppermute(mine, 'c', swap)  6.17 us
  transfers between devices with their start and end apart: 23, of which 7 were waited for; matrix products, arithmetic and copies ran while one was open for 0% of the time, Pallas kernels for 6%

profile of v5, /device:TPU:24, one launch (start us, length us, event | category | flops | bytes accessed | tf_op | source)
XLA Modules:
  0.0 128.2 jit_solution(9590483184670807370)
XLA Ops:
  0.7 0.9 copy-done.1
  2.3 1.3 chunk.1
  3.6 7.3 %all-to-all-start = ((bf16[8,16,1152]{2,1,0:T(8,128)(2,1)}), bf16[8,16,1152]{2,1,0:T(8,128)(2,1)S(1)}, u32[]{:S(2)}, u32[]{:S(2)}) async-start(bf16[8,16,1152]{2,1,0:T(8,128)(2,1)} %chunk.1), calls=%async_computation | async-start | bytes 589824 | tf_op jit(solution)/shard_map/all_to_all | solution.py:413
  11.0 0.8 copy-done.2
  11.9 3.3 %collective-permute-start.5 = (bf16[32,8192]{1,0:T(8,128)(2,1)S(1)}, bf16[32,8192]{1,0:T(8,128)(2,1)S(1)}, u32[]{:S(2)}, u32[]{:S(2)}) collective-permute-start(bf16[32,8192]{1,0:T(8,128)(2,1)S(1)} %half.1), channel_id=1, source_target_pairs={{10,0},{11,30},{27,31},{26,1},{2,2},{6,8},{7,22},{18,7},{22,25},{4... | collective-permute-start | bytes 1572872 | tf_op jit(solution)/shard_map/ppermute | solution.py:418
  15.2 1.6 %collective-permute-start.6 = (bf16[2,64,4096]{2,1,0:T(8,128)(2,1)}, bf16[2,64,4096]{2,1,0:T(8,128)(2,1)}, u32[]{:S(2)}, u32[]{:S(2)}) collective-permute-start(bf16[2,64,4096]{2,1,0:T(8,128)(2,1)} %get-tuple-element.26), channel_id=1, source_target_pairs={{0,2},{1,7},{31,25},{32,34},{33,39},{63,57},{64,66},{65,71},{95,89... | collective-permute-start | bytes 3145736 | tf_op jit(solution)/shard_map/ppermute | solution.py:414
  17.5 1.6 %collective-permute-start.7 = (bf16[2,64,4096]{2,1,0:T(8,128)(2,1)}, bf16[2,64,4096]{2,1,0:T(8,128)(2,1)}, u32[]{:S(2)}, u32[]{:S(2)}) collective-permute-start(bf16[2,64,4096]{2,1,0:T(8,128)(2,1)} %get-tuple-element.27), channel_id=1, source_target_pairs={{0,8},{1,25},{30,22},{31,7},{32,40},{33,57},{62,54},{63,39},{64,72... | collective-permute-start | bytes 3145736 | tf_op jit(solution)/shard_map/ppermute | solution.py:414
  19.1 1.0 spread.1
  20.1 11.3 %all-to-all-start.1 = ((bf16[16,16,1024]{2,1,0:T(8,128)(2,1)}), bf16[16,16,1024]{2,1,0:T(8,128)(2,1)S(1)}, u32[]{:S(2)}, u32[]{:S(2)}) async-start(bf16[16,16,1024]{2,1,0:T(8,128)(2,1)} %get-tuple-element.25), calls=%async_computation.1 | async-start | bytes 1048576 | tf_op jit(solution)/shard_map/all_to_all | solution.py:427
  32.8 11.0 %all-to-all-done.1 = bf16[16,16,1024]{2,1,0:T(8,128)(2,1)S(1)} async-done(((bf16[16,16,1024]{2,1,0:T(8,128)(2,1)}), bf16[16,16,1024]{2,1,0:T(8,128)(2,1)S(1)}, u32[]{:S(2)}, u32[]{:S(2)}) %all-to-all-start.1) | async-done | bytes 524320 | tf_op jit(solution)/shard_map/all_to_all | solution.py:427
  43.8 6.2 %collective-permute-start = (bf16[2,4,2,16,1024]{4,3,2,1,0:T(8,128)(2,1)S(1)}, bf16[2,4,2,16,1024]{4,3,2,1,0:T(8,128)(2,1)S(1)}, u32[]{:S(2)}, u32[]{:S(2)}) collective-permute-start(bf16[2,4,2,16,1024]{4,3,2,1,0:T(8,128)(2,1)S(1)} %bitcast.11), channel_id=1, source_target_pairs={{0,1},{1,0},{2,3},{3,2},{4,5},{5,4},{6,7},{7,6},{8,9},{9,8},{10,11... | collective-permute-start | bytes 1572872 | tf_op jit(solution)/shard_map/ppermute | solution.py:428
  50.0 1.5 %collective-permute-done.other = bf16[2,4,2,16,1024]{4,3,2,1,0:T(8,128)(2,1)S(1)} collective-permute-done((bf16[2,4,2,16,1024]{4,3,2,1,0:T(8,128)(2,1)S(1)}, bf16[2,4,2,16,1024]{4,3,2,1,0:T(8,128)(2,1)S(1)}, u32[]{:S(2)}, u32[]{:S(2)}) %collective-permute-start) | collective-permute-done | bytes 524320 | tf_op jit(solution)/shard_map/ppermute | solution.py:428
  51.5 9.6 %attention.1 = (bf16[256,4096]{1,0:T(8,128)(2,1)}, bf16[256,4096]{1,0:T(8,128)(2,1)}, bf16[2,64,4096]{2,1,0:T(8,128)(2,1)}, f32[16,16,1024]{2,1,0:T(8,128)}, bf1...) custom-call(s32[1]{0:T(128)} %bitcast.here, ...), custom_call_target="tpu_custom_call" | custom-call | tf_op jit(solution)/shard_map/attention/pallas_call | solution.py:433
  61.2 2.3 %collective-permute-start.10 = (bf16[17,16,1024]{2,1,0:T(8,128)(2,1)S(1)}, bf16[17,16,1024]{2,1,0:T(8,128)(2,1)S(1)}, u32[]{:S(2)}, u32[]{:S(2)}) collective-permute-start(bf16[17,16,1024]{2,1,0:T(8,128)(2,1)S(1)} %get-tuple-element.34), channel_id=1, source_target_pairs={{0,1},{1,0},{2,3},{3,2},{4,5},{5,4},{6,7},{7,6},{8,9},{9,8},{10,11... | collective-permute-start | bytes 1671176 | tf_op jit(solution)/shard_map/ppermute | solution.py:456
  65.7 1.5 %collective-permute-start.12 = (bf16[32,8192]{1,0:T(8,128)(2,1)}, bf16[32,8192]{1,0:T(8,128)(2,1)}, u32[]{:S(2)}, u32[]{:S(2)}) collective-permute-start(bf16[32,8192]{1,0:T(8,128)(2,1)} %get-tuple-element.38), channel_id=1, source_target_pairs={{0,14},{30,15},{31,31},{32,46},{62,47},{63,63},{64,78},{94,79},{95... | collective-permute-start | bytes 1572872 | tf_op jit(solution)/shard_map/ppermute | solution.py:461
  67.1 1.5 %collective-permute-start.13 = (bf16[32,8192]{1,0:T(8,128)(2,1)}, bf16[32,8192]{1,0:T(8,128)(2,1)}, u32[]{:S(2)}, u32[]{:S(2)}) collective-permute-start(bf16[32,8192]{1,0:T(8,128)(2,1)} %get-tuple-element.39), channel_id=1, source_target_pairs={{0,8},{30,9},{31,25},{1,24},{2,0},{8,4},{22,5},{7,16},{25,20},{32,... | collective-permute-start | bytes 1572872 | tf_op jit(solution)/shard_map/ppermute | solution.py:461
  68.6 1.3 collective-permute-start.14
  69.9 1.2 copy-done
  71.1 1.0 pair.1
  72.1 15.8 %all-to-all-start.2 = ((bf16[16,16,1152]{2,1,0:T(8,128)(2,1)}), bf16[16,16,1152]{2,1,0:T(8,128)(2,1)S(1)}, u32[]{:S(2)}, u32[]{:S(2)}) async-start(bf16[16,16,1152]{2,1,0:T(8,128)(2,1)} %pair.1), calls=%async_computation.2 | async-start | bytes 1179648 | tf_op jit(solution)/shard_map/all_to_all | solution.py:460
  87.9 13.2 %collective-permute-done.14.r3 = bf16[32,8192]{1,0:T(8,128)(2,1)} collective-permute-done((bf16[32,8192]{1,0:T(8,128)(2,1)}, bf16[32,8192]{1,0:T(8,128)(2,1)}, u32[]{:S(2)}, u32[]{:S(2)}) %collective-permute-start.14) | collective-permute-done | bytes 524320 | tf_op jit(solution)/shard_map/ppermute | solution.py:461
  101.1 1.8 %sort.1 = (bf16[16,8192]{1,0:T(8,128)(2,1)S(1)}, bf16[16,8192]{1,0:T(8,128)(2,1)}) custom-call(s32[1]{0:T(128)} %bitcast.here, bf16[32,8192]{1,0:T(8,128)(2,1)S(1)} %collective-permute-done.11.r0, bf16[32,8192]{1,0:T(8,128)(2,1)} %collective-permute-done.12.r1, bf16[32,8192]{1,0:T(8,128)(2,1)} %collective-permute-done.13.r2, ...), custom_call_target="tpu_custom_call" | custom-call | tf_op jit(solution)/shard_map/sort/pallas_call | solution.py:462
  102.9 1.1 all-to-all-done.2.got
  104.1 0.8 collect.1
  104.8 6.1 %all-to-all-start.3 = ((bf16[8,16,1024]{2,1,0:T(8,128)(2,1)}), bf16[8,16,1024]{2,1,0:T(8,128)(2,1)S(1)}, u32[]{:S(2)}, u32[]{:S(2)}) async-start(bf16[8,16,1024]{2,1,0:T(8,128)(2,1)} %get-tuple-element.36), calls=%async_computation.3 | async-start | bytes 524288 | tf_op jit(solution)/shard_map/all_to_all | solution.py:481
  111.0 1.9 %collective-permute-start.16 = (f32[1,128]{1,0:T(1,128)S(1)}, f32[1,128]{1,0:T(1,128)S(1)}, u32[]{:S(2)}, u32[]{:S(2)}) collective-permute-start(f32[1,128]{1,0:T(1,128)S(1)} %get-tuple-element.43), channel_id=1, source_target_pairs={{0,32},{32,0},{64,96},{96,64},{128,160},{160,128},{192,224},{224,1... | collective-permute-start | bytes 1544 | tf_op jit(solution)/shard_map/ppermute | solution.py:480
  112.9 1.6 %collective-permute-done.16 = f32[1,128]{1,0:T(1,128)S(1)} collective-permute-done((f32[1,128]{1,0:T(1,128)S(1)}, f32[1,128]{1,0:T(1,128)S(1)}, u32[]{:S(2)}, u32[]{:S(2)}) %collective-permute-start.16) | collective-permute-done | bytes 544 | tf_op jit(solution)/shard_map/ppermute | solution.py:480
  114.5 3.3 %collective-permute-start.17 = (f32[1,128]{1,0:T(1,128)S(1)}, f32[1,128]{1,0:T(1,128)S(1)}, u32[]{:S(2)}, u32[]{:S(2)}) collective-permute-start(f32[1,128]{1,0:T(1,128)S(1)} %add.21), channel_id=1, source_target_pairs={{0,64},{32,96},{64,0},{96,32},{128,192},{160,224},{192,128},{224,1... | collective-permute-start | bytes 1544 | tf_op jit(solution)/shard_map/ppermute | solution.py:480
  117.8 1.5 %collective-permute-done.17 = f32[1,128]{1,0:T(1,128)S(1)} collective-permute-done((f32[1,128]{1,0:T(1,128)S(1)}, f32[1,128]{1,0:T(1,128)S(1)}, u32[]{:S(2)}, u32[]{:S(2)}) %collective-permute-start.17) | collective-permute-done | bytes 544 | tf_op jit(solution)/shard_map/ppermute | solution.py:480
  119.3 5.5 %collective-permute-start.18 = (f32[1,128]{1,0:T(1,128)S(1)}, f32[1,128]{1,0:T(1,128)S(1)}, u32[]{:S(2)}, u32[]{:S(2)}) collective-permute-start(f32[1,128]{1,0:T(1,128)S(1)} %add.22), channel_id=1, source_target_pairs={{0,224},{32,192},{64,160},{96,128},{128,96},{160,64},{192,32},{224... | collective-permute-start | bytes 1544 | tf_op jit(solution)/shard_map/ppermute | solution.py:480
  124.8 1.3 merge.1
  126.9 1.4 %assemble.1 = bf16[16,8192]{1,0:T(8,128)(2,1)} custom-call(s32[1]{0:T(128)} %bitcast.here, s32[1]{0:T(128)} %get-tuple-element.24.lead_ref, bf16[8,16,1024]{2,1,0:T(8,128)(2,1)S(1)} %all-to-all-done.3.got, bf16[16,8192]{1,0:T(8,128)(2,1)S(1)} %get-tuple-element.41.own, bf16[16,8192]{1,0:T(8,128)(2,1)S(1)} %collective-permute-done.15.given), custom_call_target="tpu_custom_call" | custom-call | tf_op jit(solution)/shard_map/assemble/pallas_call | solution.py:482
  (41 shorter events, 6.0 us)
Async XLA Ops:
  0.6 10.4 %collective-permute-start.1 = (bf16[16,8192]{1,0:T(8,128)(2,1)}, bf16[16,8192]{1,0:T(8,128)(2,1)S(1)}, u32[]{:S(2)}, u32[]{:S(2)}) collective-permute-start(bf16[16,8192]{1,0:T(8,128)(2,1)} %bitcast.13), channel_id=1, source_target_pairs={{0,1},{1,0},{2,3},{3,2},{4,5},{5,4},{6,7},{7,6},{8,9},{9,8},{10,11... | collective-permute-start | bytes 786440 | tf_op jit(solution)/shard_map/ppermute | solution.py:416
  0.7 1.0 copy-start.1
  1.7 0.7 copy-start.3
  3.6 15.5 %all-to-all-start = ((bf16[8,16,1152]{2,1,0:T(8,128)(2,1)}), bf16[8,16,1152]{2,1,0:T(8,128)(2,1)S(1)}, u32[]{:S(2)}, u32[]{:S(2)}) async-start(bf16[8,16,1152]{2,1,0:T(8,128)(2,1)} %chunk.1), calls=%async_computation | async-start | bytes 589824 | tf_op jit(solution)/shard_map/all_to_all | solution.py:413
  10.9 0.9 copy-start.2
  11.0 39.0 %copy-start.5 = (f32[32]{0:T(128)S(1)}, f32[32]{0:T(128)}, u32[]{:S(2)}) copy-start(f32[32]{0:T(128)} %param.8) | copy-start | bytes 388
  11.0 40.5 %copy-start.4 = (s32[1,4]{1,0:T(1,128)S(1)}, s32[1,4]{1,0:T(1,128)}, u32[]{:S(2)}) copy-start(s32[1,4]{1,0:T(1,128)} %param.7) | copy-start | bytes 52
  11.9 20.2 %collective-permute-start.5 = (bf16[32,8192]{1,0:T(8,128)(2,1)S(1)}, bf16[32,8192]{1,0:T(8,128)(2,1)S(1)}, u32[]{:S(2)}, u32[]{:S(2)}) collective-permute-start(bf16[32,8192]{1,0:T(8,128)(2,1)S(1)} %half.1), channel_id=1, source_target_pairs={{10,0},{11,30},{27,31},{26,1},{2,2},{6,8},{7,22},{18,7},{22,25},{4... | collective-permute-start | bytes 1572872 | tf_op jit(solution)/shard_map/ppermute | solution.py:418
  15.2 34.8 %collective-permute-start.6 = (bf16[2,64,4096]{2,1,0:T(8,128)(2,1)}, bf16[2,64,4096]{2,1,0:T(8,128)(2,1)}, u32[]{:S(2)}, u32[]{:S(2)}) collective-permute-start(bf16[2,64,4096]{2,1,0:T(8,128)(2,1)} %get-tuple-element.26), channel_id=1, source_target_pairs={{0,2},{1,7},{31,25},{32,34},{33,39},{63,57},{64,66},{65,71},{95,89... | collective-permute-start | bytes 3145736 | tf_op jit(solution)/shard_map/ppermute | solution.py:414
  16.8 27.0 %collective-permute-start.4 = (bf16[32,8192]{1,0:T(8,128)(2,1)S(1)}, bf16[32,8192]{1,0:T(8,128)(2,1)S(1)}, u32[]{:S(2)}, u32[]{:S(2)}) collective-permute-start(bf16[32,8192]{1,0:T(8,128)(2,1)S(1)} %half.1), channel_id=1, source_target_pairs={{8,0},{9,30},{25,31},{24,1},{0,2},{4,8},{5,22},{16,7},{20,25},{40,... | collective-permute-start | bytes 1572872 | tf_op jit(solution)/shard_map/ppermute | solution.py:418
  17.5 32.5 %collective-permute-start.7 = (bf16[2,64,4096]{2,1,0:T(8,128)(2,1)}, bf16[2,64,4096]{2,1,0:T(8,128)(2,1)}, u32[]{:S(2)}, u32[]{:S(2)}) collective-permute-start(bf16[2,64,4096]{2,1,0:T(8,128)(2,1)} %get-tuple-element.27), channel_id=1, source_target_pairs={{0,8},{1,25},{30,22},{31,7},{32,40},{33,57},{62,54},{63,39},{64,72... | collective-permute-start | bytes 3145736 | tf_op jit(solution)/shard_map/ppermute | solution.py:414
  20.1 23.7 %all-to-all-start.1 = ((bf16[16,16,1024]{2,1,0:T(8,128)(2,1)}), bf16[16,16,1024]{2,1,0:T(8,128)(2,1)S(1)}, u32[]{:S(2)}, u32[]{:S(2)}) async-start(bf16[16,16,1024]{2,1,0:T(8,128)(2,1)} %get-tuple-element.25), calls=%async_computation.1 | async-start | bytes 1048576 | tf_op jit(solution)/shard_map/all_to_all | solution.py:427
  31.4 18.6 %collective-permute-start.3 = (bf16[32,8192]{1,0:T(8,128)(2,1)S(1)}, bf16[32,8192]{1,0:T(8,128)(2,1)S(1)}, u32[]{:S(2)}, u32[]{:S(2)}) collective-permute-start(bf16[32,8192]{1,0:T(8,128)(2,1)S(1)} %half.1), channel_id=1, source_target_pairs={{14,0},{15,30},{31,31},{46,32},{47,62},{63,63},{78,64},{79,94},{95... | collective-permute-start | bytes 1572872 | tf_op jit(solution)/shard_map/ppermute | solution.py:418
  32.1 17.9 %collective-permute-start.2 = (bf16[32,8192]{1,0:T(8,128)(2,1)S(1)}, bf16[32,8192]{1,0:T(8,128)(2,1)S(1)}, u32[]{:S(2)}, u32[]{:S(2)}) collective-permute-start(bf16[32,8192]{1,0:T(8,128)(2,1)S(1)} %half.1), channel_id=1, source_target_pairs={{12,0},{13,30},{29,31},{44,32},{45,62},{61,63},{76,64},{77,94},{93... | collective-permute-start | bytes 1572872 | tf_op jit(solution)/shard_map/ppermute | solution.py:418
  43.8 7.7 %collective-permute-start = (bf16[2,4,2,16,1024]{4,3,2,1,0:T(8,128)(2,1)S(1)}, bf16[2,4,2,16,1024]{4,3,2,1,0:T(8,128)(2,1)S(1)}, u32[]{:S(2)}, u32[]{:S(2)}) collective-permute-start(bf16[2,4,2,16,1024]{4,3,2,1,0:T(8,128)(2,1)S(1)} %bitcast.11), channel_id=1, source_target_pairs={{0,1},{1,0},{2,3},{3,2},{4,5},{5,4},{6,7},{7,6},{8,9},{9,8},{10,11... | collective-permute-start | bytes 1572872 | tf_op jit(solution)/shard_map/ppermute | solution.py:428
  61.2 7.4 %collective-permute-start.10 = (bf16[17,16,1024]{2,1,0:T(8,128)(2,1)S(1)}, bf16[17,16,1024]{2,1,0:T(8,128)(2,1)S(1)}, u32[]{:S(2)}, u32[]{:S(2)}) collective-permute-start(bf16[17,16,1024]{2,1,0:T(8,128)(2,1)S(1)} %get-tuple-element.34), channel_id=1, source_target_pairs={{0,1},{1,0},{2,3},{3,2},{4,5},{5,4},{6,7},{7,6},{8,9},{9,8},{10,11... | collective-permute-start | bytes 1671176 | tf_op jit(solution)/shard_map/ppermute | solution.py:456
  63.5 3.6 %collective-permute-start.11 = (bf16[32,8192]{1,0:T(8,128)(2,1)S(1)}, bf16[32,8192]{1,0:T(8,128)(2,1)S(1)}, u32[]{:S(2)}, u32[]{:S(2)}) collective-permute-start(bf16[32,8192]{1,0:T(8,128)(2,1)S(1)} %get-tuple-element.37), channel_id=1, source_target_pairs={{0,12},{30,13},{31,29},{32,44},{62,45},{63,61},{64,76},{94,77},{95... | collective-permute-start | bytes 1572872 | tf_op jit(solution)/shard_map/ppermute | solution.py:461
  64.2 60.6 %collective-permute-start.9 = (bf16[2,64,4096]{2,1,0:T(8,128)(2,1)}, bf16[2,64,4096]{2,1,0:T(8,128)(2,1)S(1)}, u32[]{:S(2)}, u32[]{:S(2)}) collective-permute-start(bf16[2,64,4096]{2,1,0:T(8,128)(2,1)} %get-tuple-element.30), channel_id=1, source_target_pairs={{8,0},{25,1},{22,30},{7,31},{40,32},{57,33},{54,62},{39,63},{72,64... | collective-permute-start | bytes 3145736 | tf_op jit(solution)/shard_map/ppermute | solution.py:471
  64.9 59.9 %collective-permute-start.8 = (bf16[2,64,4096]{2,1,0:T(8,128)(2,1)}, bf16[2,64,4096]{2,1,0:T(8,128)(2,1)S(1)}, u32[]{:S(2)}, u32[]{:S(2)}) collective-permute-start(bf16[2,64,4096]{2,1,0:T(8,128)(2,1)} %get-tuple-element.30), channel_id=1, source_target_pairs={{2,0},{7,1},{25,31},{34,32},{39,33},{57,63},{66,64},{71,65},{89,95... | collective-permute-start | bytes 3145736 | tf_op jit(solution)/shard_map/ppermute | solution.py:471
  65.7 22.2 %collective-permute-start.12 = (bf16[32,8192]{1,0:T(8,128)(2,1)}, bf16[32,8192]{1,0:T(8,128)(2,1)}, u32[]{:S(2)}, u32[]{:S(2)}) collective-permute-start(bf16[32,8192]{1,0:T(8,128)(2,1)} %get-tuple-element.38), channel_id=1, source_target_pairs={{0,14},{30,15},{31,31},{32,46},{62,47},{63,63},{64,78},{94,79},{95... | collective-permute-start | bytes 1572872 | tf_op jit(solution)/shard_map/ppermute | solution.py:461
  67.1 20.8 %collective-permute-start.13 = (bf16[32,8192]{1,0:T(8,128)(2,1)}, bf16[32,8192]{1,0:T(8,128)(2,1)}, u32[]{:S(2)}, u32[]{:S(2)}) collective-permute-start(bf16[32,8192]{1,0:T(8,128)(2,1)} %get-tuple-element.39), channel_id=1, source_target_pairs={{0,8},{30,9},{31,25},{1,24},{2,0},{8,4},{22,5},{7,16},{25,20},{32,... | collective-permute-start | bytes 1572872 | tf_op jit(solution)/shard_map/ppermute | solution.py:461
  68.6 32.5 %collective-permute-start.14 = (bf16[32,8192]{1,0:T(8,128)(2,1)}, bf16[32,8192]{1,0:T(8,128)(2,1)}, u32[]{:S(2)}, u32[]{:S(2)}) collective-permute-start(bf16[32,8192]{1,0:T(8,128)(2,1)} %get-tuple-element.40), channel_id=1, source_target_pairs={{0,10},{30,11},{31,27},{1,26},{2,2},{8,6},{22,7},{7,18},{25,22},{3... | collective-permute-start | bytes 1572872 | tf_op jit(solution)/shard_map/ppermute | solution.py:461
  69.9 1.2 copy-start
  72.1 31.9 %all-to-all-start.2 = ((bf16[16,16,1152]{2,1,0:T(8,128)(2,1)}), bf16[16,16,1152]{2,1,0:T(8,128)(2,1)S(1)}, u32[]{:S(2)}, u32[]{:S(2)}) async-start(bf16[16,16,1152]{2,1,0:T(8,128)(2,1)} %pair.1), calls=%async_computation.2 | async-start | bytes 1179648 | tf_op jit(solution)/shard_map/all_to_all | solution.py:460
  102.8 24.0 %collective-permute-start.15 = (bf16[16,8192]{1,0:T(8,128)(2,1)}, bf16[16,8192]{1,0:T(8,128)(2,1)S(1)}, u32[]{:S(2)}, u32[]{:S(2)}) collective-permute-start(bf16[16,8192]{1,0:T(8,128)(2,1)} %get-tuple-element.42), channel_id=1, source_target_pairs={{0,1},{1,0},{2,3},{3,2},{4,5},{5,4},{6,7},{7,6},{8,9},{9,8},{10,11... | collective-permute-start | bytes 786440 | tf_op jit(solution)/shard_map/ppermute | solution.py:470
  104.8 22.0 %all-to-all-start.3 = ((bf16[8,16,1024]{2,1,0:T(8,128)(2,1)}), bf16[8,16,1024]{2,1,0:T(8,128)(2,1)S(1)}, u32[]{:S(2)}, u32[]{:S(2)}) async-start(bf16[8,16,1024]{2,1,0:T(8,128)(2,1)} %get-tuple-element.36), calls=%async_computation.3 | async-start | bytes 524288 | tf_op jit(solution)/shard_map/all_to_all | solution.py:481
  111.0 3.5 %collective-permute-start.16 = (f32[1,128]{1,0:T(1,128)S(1)}, f32[1,128]{1,0:T(1,128)S(1)}, u32[]{:S(2)}, u32[]{:S(2)}) collective-permute-start(f32[1,128]{1,0:T(1,128)S(1)} %get-tuple-element.43), channel_id=1, source_target_pairs={{0,32},{32,0},{64,96},{96,64},{128,160},{160,128},{192,224},{224,1... | collective-permute-start | bytes 1544 | tf_op jit(solution)/shard_map/ppermute | solution.py:480
  114.5 4.8 %collective-permute-start.17 = (f32[1,128]{1,0:T(1,128)S(1)}, f32[1,128]{1,0:T(1,128)S(1)}, u32[]{:S(2)}, u32[]{:S(2)}) collective-permute-start(f32[1,128]{1,0:T(1,128)S(1)} %add.21), channel_id=1, source_target_pairs={{0,64},{32,96},{64,0},{96,32},{128,192},{160,224},{192,128},{224,1... | collective-permute-start | bytes 1544 | tf_op jit(solution)/shard_map/ppermute | solution.py:480
  119.3 7.0 %collective-permute-start.18 = (f32[1,128]{1,0:T(1,128)S(1)}, f32[1,128]{1,0:T(1,128)S(1)}, u32[]{:S(2)}, u32[]{:S(2)}) collective-permute-start(f32[1,128]{1,0:T(1,128)S(1)} %add.22), channel_id=1, source_target_pairs={{0,224},{32,192},{64,160},{96,128},{128,96},{160,64},{192,32},{224... | collective-permute-start | bytes 1544 | tf_op jit(solution)/shard_map/ppermute | solution.py:480

commit v6 on v5

--- a/solution.py
+++ b/solution.py
@@ -264,17 +264,13 @@
 
     @pl.when(c == pl.num_programs(0) - 1)
     def _():
-        gs = jnp.sum(gacc[...].T, axis=0, keepdims=True)
-        gate[...] = gs
-        opay[16] = jnp.zeros((QUART, COLS), BF)
-        opay[16, :, 0:HS] = split3(gs)
+        gate[...] = jnp.sum(gacc[...].T, axis=0, keepdims=True)
 
 
 def pair_kernel(pay, got, gate, dst):
     for d in range(16):
         dst[d, :, 0:COLS] = (pay[d] + got[d].astype(F32)).astype(BF)
-    other = jnp.sum(got[16, :, 0:HS].astype(F32), axis=0, keepdims=True)
-    gates = split3(gate[...] + other)
+    gates = split3(gate[...])
     for d in range(16):
         dst[d, :, COLS:WIDE] = gates
 
@@ -438,7 +434,7 @@
             shape(tokens, width),
             shape(2, NLAT, width),
             shape(16, QUART, COLS, dtype=F32),
-            shape(17, QUART, COLS),
+            shape(16, QUART, COLS),
             *[shape(2 * QUART, 2 * width)] * 4,
             shape(1, HS, dtype=F32),
         ],
@@ -453,6 +449,7 @@
         ],
     )(here, images, lead, tanh_gate, q, g, mine, other, *lent, *sent)
 
+    gpart = gpart + lax.ppermute(gpart, "dp", [(s, s ^ 1) for s in range(8)])
     theirs = lax.ppermute(opay, "c", swap)
     paired = call(pair_kernel, "pair", shape(16, QUART, WIDE), [VM, VM, VM], VM)(
         pay, theirs, gpart
@@ -476,7 +473,8 @@
         [VM],
         [VM, VM],
     )(parts)
-    for flip in (1, 2, 7):
+    gates = gates + lax.ppermute(gates, "c", swap)
+    for flip in (2, 7):
         gates = gates + lax.ppermute(gates, "dp", [(s, s ^ flip) for s in range(8)])
     final = lax.all_to_all(summed, IMG, 0, 0, tiled=True)
     latent_grad = call(

time: 130 us -> 125 us (0.962)
  waiting for transfers between devices: 30.2 us -> 27.9 us
  starting transfers between devices: 74.8 us -> 73 us
    ppermute x0 -> x2, waiting for transfers between devices: none -> 2.74 us  [the longest x1 1.62 us: body(): gpart = gpart + lax.ppermute(gpart, 'dp', [(s, s ^ 1) for s in range(8)])]
    ppermute x4, waiting for transfers between devices: 13.2 us -> 10.9 us  [body(): lax.ppermute(y, CTX, back(latent_pairs(s)))]
    ppermute x0 -> x2, starting transfers between devices: none -> 2.01 us  [the longest x1 2.01 us: body(): gpart = gpart + lax.ppermute(gpart, 'dp', [(s, s ^ 1) for s in range(8)])]
    all_to_all x1, starting transfers between devices: 15.8 us -> 13.8 us  [body(): parts = lax.all_to_all(paired, CHIP, 0, 0, tiled=True)]
    ppermute x3 -> x2, starting transfers between devices: 10.7 us -> 8.97 us  [body(): gates = gates + lax.ppermute(gates, 'dp', [(s, s ^ flip) for s in range(8)])]
    ppermute x3 -> x2, waiting for transfers between devices: 3.39 us -> 1.76 us  [body(): gates = gates + lax.ppermute(gates, 'dp', [(s, s ^ flip) for s in range(8)])]
  transfers between devices with their start and end apart: 23 -> 24, of which waited for: 7 -> 7; matrix products, arithmetic and copies ran while one was open for 0% -> 0% of each run, Pallas kernels for 6% -> 6%
where the time goes in v6:
time: 125 us; the launch traced here: 124 us
  starting transfers between devices  73 us (58%)
  waiting for transfers between devices  27.9 us (22%)
  Pallas kernels  18.1 us (14%)
  local copies, waits for them, and re-layouts  3.67 us (3%)
    all_to_all x1, starting transfers between devices, body(): parts = lax.all_to_all(paired, CHIP, 0, 0, tiled=True)  13.8 us
    all_to_all x1, starting transfers between devices, body(): lax.all_to_all(spread, CHIP, 0, 0, tiled=True).reshape(2, 4, 2, QUART, COLS)  11.3 us
    all_to_all x1, waiting for transfers between devices, body(): lax.all_to_all(spread, CHIP, 0, 0, tiled=True).reshape(2, 4, 2, QUART, COLS)  11 us
    ppermute x4, waiting for transfers between devices, body(): lax.ppermute(y, CTX, back(latent_pairs(s)))  10.9 us
    pallas_call x1, Pallas kernels, body(): call(attention_kernel, 'attention', [shape(tokens, width), shape(tokens,...  9.64 us
    ppermute x2, starting transfers between devices, body(): gates = gates + lax.ppermute(gates, 'dp', [(s, s ^ flip) for s in range(8)])  8.97 us
    all_to_all x1, starting transfers between devices, body(): mixed = lax.all_to_all(chunks, IMG, 0, 0, tiled=True)  7.26 us
    ppermute x1, starting transfers between devices, body(): other = lax.ppermute(mine, 'c', swap)  6.17 us
  transfers between devices with their start and end apart: 24, of which 7 were waited for; matrix products, arithmetic and copies ran while one was open for 0% of the time, Pallas kernels for 6%

profile of v6, /device:TPU:24, one launch (start us, length us, event | category | flops | bytes accessed | tf_op | source)
XLA Modules:
  0.0 124.1 jit_solution(11937769701942383914)
XLA Ops:
  0.7 0.9 copy-done.1
  2.3 1.3 %chunk.1 = bf16[8,16,1152]{2,1,0:T(8,128)(2,1)} custom-call(s32[4]{0:T(128)S(1)} %bitcast.16, bf16[16,8192]{1,0:T(8,128)(2,1)S(1)} %bitcast.14), custom_call_target="tpu_custom_call" | custom-call | tf_op jit(solution)/shard_map/chunk/pallas_call | solution.py:408
  3.6 7.3 %all-to-all-start = ((bf16[8,16,1152]{2,1,0:T(8,128)(2,1)}), bf16[8,16,1152]{2,1,0:T(8,128)(2,1)S(1)}, u32[]{:S(2)}, u32[]{:S(2)}) async-start(bf16[8,16,1152]{2,1,0:T(8,128)(2,1)} %chunk.1), calls=%async_computation | async-start | bytes 589824 | tf_op jit(solution)/shard_map/all_to_all | solution.py:409
  11.0 0.8 copy-done.2
  11.9 3.3 %collective-permute-start.5 = (bf16[32,8192]{1,0:T(8,128)(2,1)S(1)}, bf16[32,8192]{1,0:T(8,128)(2,1)S(1)}, u32[]{:S(2)}, u32[]{:S(2)}) collective-permute-start(bf16[32,8192]{1,0:T(8,128)(2,1)S(1)} %half.1), channel_id=1, source_target_pairs={{10,0},{11,30},{27,31},{26,1},{2,2},{6,8},{7,22},{18,7},{22,25},{4... | collective-permute-start | bytes 1572872 | tf_op jit(solution)/shard_map/ppermute | solution.py:414
  15.2 1.6 %collective-permute-start.6 = (bf16[2,64,4096]{2,1,0:T(8,128)(2,1)}, bf16[2,64,4096]{2,1,0:T(8,128)(2,1)}, u32[]{:S(2)}, u32[]{:S(2)}) collective-permute-start(bf16[2,64,4096]{2,1,0:T(8,128)(2,1)} %get-tuple-element.26), channel_id=1, source_target_pairs={{0,2},{1,7},{31,25},{32,34},{33,39},{63,57},{64,66},{65,71},{95,89... | collective-permute-start | bytes 3145736 | tf_op jit(solution)/shard_map/ppermute | solution.py:410
  17.5 1.7 %collective-permute-start.7 = (bf16[2,64,4096]{2,1,0:T(8,128)(2,1)}, bf16[2,64,4096]{2,1,0:T(8,128)(2,1)}, u32[]{:S(2)}, u32[]{:S(2)}) collective-permute-start(bf16[2,64,4096]{2,1,0:T(8,128)(2,1)} %get-tuple-element.27), channel_id=1, source_target_pairs={{0,8},{1,25},{30,22},{31,7},{32,40},{33,57},{62,54},{63,39},{64,72... | collective-permute-start | bytes 3145736 | tf_op jit(solution)/shard_map/ppermute | solution.py:410
  19.1 0.9 spread.1
  20.1 11.3 %all-to-all-start.1 = ((bf16[16,16,1024]{2,1,0:T(8,128)(2,1)}), bf16[16,16,1024]{2,1,0:T(8,128)(2,1)S(1)}, u32[]{:S(2)}, u32[]{:S(2)}) async-start(bf16[16,16,1024]{2,1,0:T(8,128)(2,1)} %get-tuple-element.25), calls=%async_computation.1 | async-start | bytes 1048576 | tf_op jit(solution)/shard_map/all_to_all | solution.py:423
  32.8 11.0 %all-to-all-done.1 = bf16[16,16,1024]{2,1,0:T(8,128)(2,1)S(1)} async-done(((bf16[16,16,1024]{2,1,0:T(8,128)(2,1)}), bf16[16,16,1024]{2,1,0:T(8,128)(2,1)S(1)}, u32[]{:S(2)}, u32[]{:S(2)}) %all-to-all-start.1) | async-done | bytes 524320 | tf_op jit(solution)/shard_map/all_to_all | solution.py:423
  43.8 6.2 %collective-permute-start = (bf16[2,4,2,16,1024]{4,3,2,1,0:T(8,128)(2,1)S(1)}, bf16[2,4,2,16,1024]{4,3,2,1,0:T(8,128)(2,1)S(1)}, u32[]{:S(2)}, u32[]{:S(2)}) collective-permute-start(bf16[2,4,2,16,1024]{4,3,2,1,0:T(8,128)(2,1)S(1)} %bitcast.11), channel_id=1, source_target_pairs={{0,1},{1,0},{2,3},{3,2},{4,5},{5,4},{6,7},{7,6},{8,9},{9,8},{10,11... | collective-permute-start | bytes 1572872 | tf_op jit(solution)/shard_map/ppermute | solution.py:424
  50.0 1.5 %collective-permute-done.other = bf16[2,4,2,16,1024]{4,3,2,1,0:T(8,128)(2,1)S(1)} collective-permute-done((bf16[2,4,2,16,1024]{4,3,2,1,0:T(8,128)(2,1)S(1)}, bf16[2,4,2,16,1024]{4,3,2,1,0:T(8,128)(2,1)S(1)}, u32[]{:S(2)}, u32[]{:S(2)}) %collective-permute-start) | collective-permute-done | bytes 524320 | tf_op jit(solution)/shard_map/ppermute | solution.py:424
  51.5 9.6 %attention.1 = (bf16[256,4096]{1,0:T(8,128)(2,1)}, bf16[256,4096]{1,0:T(8,128)(2,1)}, bf16[2,64,4096]{2,1,0:T(8,128)(2,1)}, f32[16,16,1024]{2,1,0:T(8,128)}, bf1...) custom-call(s32[1]{0:T(128)} %bitcast.here, ...), custom_call_target="tpu_custom_call" | custom-call | tf_op jit(solution)/shard_map/attention/pallas_call | solution.py:429
  61.2 2.3 %collective-permute-start.10 = (bf16[16,16,1024]{2,1,0:T(8,128)(2,1)S(1)}, bf16[16,16,1024]{2,1,0:T(8,128)(2,1)S(1)}, u32[]{:S(2)}, u32[]{:S(2)}) collective-permute-start(bf16[16,16,1024]{2,1,0:T(8,128)(2,1)S(1)} %get-tuple-element.34), channel_id=1, source_target_pairs={{0,1},{1,0},{2,3},{3,2},{4,5},{5,4},{6,7},{7,6},{8,9},{9,8},{10,11... | collective-permute-start | bytes 1572872 | tf_op jit(solution)/shard_map/ppermute | solution.py:453
  65.6 2.0 %collective-permute-start.11 = (f32[1,128]{1,0:T(1,128)S(1)}, f32[1,128]{1,0:T(1,128)S(1)}, u32[]{:S(2)}, u32[]{:S(2)}) collective-permute-start(f32[1,128]{1,0:T(1,128)S(1)} %get-tuple-element.35), channel_id=1, source_target_pairs={{0,32},{32,0},{64,96},{96,64},{128,160},{160,128},{192,224},{224,1... | collective-permute-start | bytes 1544 | tf_op jit(solution)/shard_map/ppermute | solution.py:452
  67.6 1.6 %collective-permute-done.11 = f32[1,128]{1,0:T(1,128)S(1)} collective-permute-done((f32[1,128]{1,0:T(1,128)S(1)}, f32[1,128]{1,0:T(1,128)S(1)}, u32[]{:S(2)}, u32[]{:S(2)}) %collective-permute-start.11) | collective-permute-done | bytes 544 | tf_op jit(solution)/shard_map/ppermute | solution.py:452
  69.3 1.4 %collective-permute-start.13 = (bf16[32,8192]{1,0:T(8,128)(2,1)}, bf16[32,8192]{1,0:T(8,128)(2,1)}, u32[]{:S(2)}, u32[]{:S(2)}) collective-permute-start(bf16[32,8192]{1,0:T(8,128)(2,1)} %get-tuple-element.38), channel_id=1, source_target_pairs={{0,14},{30,15},{31,31},{32,46},{62,47},{63,63},{64,78},{94,79},{95... | collective-permute-start | bytes 1572872 | tf_op jit(solution)/shard_map/ppermute | solution.py:458
  70.7 1.5 %collective-permute-start.14 = (bf16[32,8192]{1,0:T(8,128)(2,1)}, bf16[32,8192]{1,0:T(8,128)(2,1)}, u32[]{:S(2)}, u32[]{:S(2)}) collective-permute-start(bf16[32,8192]{1,0:T(8,128)(2,1)} %get-tuple-element.39), channel_id=1, source_target_pairs={{0,8},{30,9},{31,25},{1,24},{2,0},{8,4},{22,5},{7,16},{25,20},{32,... | collective-permute-start | bytes 1572872 | tf_op jit(solution)/shard_map/ppermute | solution.py:458
  72.2 1.3 %collective-permute-start.15 = (bf16[32,8192]{1,0:T(8,128)(2,1)}, bf16[32,8192]{1,0:T(8,128)(2,1)}, u32[]{:S(2)}, u32[]{:S(2)}) collective-permute-start(bf16[32,8192]{1,0:T(8,128)(2,1)} %get-tuple-element.40), channel_id=1, source_target_pairs={{0,10},{30,11},{31,27},{1,26},{2,2},{8,6},{22,7},{7,18},{25,22},{3... | collective-permute-start | bytes 1572872 | tf_op jit(solution)/shard_map/ppermute | solution.py:458
  73.5 1.2 copy-done
  74.7 1.0 pair.1
  75.7 13.8 %all-to-all-start.2 = ((bf16[16,16,1152]{2,1,0:T(8,128)(2,1)}), bf16[16,16,1152]{2,1,0:T(8,128)(2,1)S(1)}, u32[]{:S(2)}, u32[]{:S(2)}) async-start(bf16[16,16,1152]{2,1,0:T(8,128)(2,1)} %pair.1), calls=%async_computation.2 | async-start | bytes 1179648 | tf_op jit(solution)/shard_map/all_to_all | solution.py:457
  89.5 10.9 %collective-permute-done.15.r3 = bf16[32,8192]{1,0:T(8,128)(2,1)} collective-permute-done((bf16[32,8192]{1,0:T(8,128)(2,1)}, bf16[32,8192]{1,0:T(8,128)(2,1)}, u32[]{:S(2)}, u32[]{:S(2)}) %collective-permute-start.15) | collective-permute-done | bytes 524320 | tf_op jit(solution)/shard_map/ppermute | solution.py:458
  100.4 1.7 %sort.1 = (bf16[16,8192]{1,0:T(8,128)(2,1)S(1)}, bf16[16,8192]{1,0:T(8,128)(2,1)}) custom-call(s32[1]{0:T(128)} %bitcast.here, bf16[32,8192]{1,0:T(8,128)(2,1)S(1)} %collective-permute-done.12.r0, bf16[32,8192]{1,0:T(8,128)(2,1)} %collective-permute-done.13.r1, bf16[32,8192]{1,0:T(8,128)(2,1)} %collective-permute-done.14.r2, ...), custom_call_target="tpu_custom_call" | custom-call | tf_op jit(solution)/shard_map/sort/pallas_call | solution.py:459
  102.3 0.8 collect.1
  103.0 6.1 %all-to-all-start.3 = ((bf16[8,16,1024]{2,1,0:T(8,128)(2,1)}), bf16[8,16,1024]{2,1,0:T(8,128)(2,1)S(1)}, u32[]{:S(2)}, u32[]{:S(2)}) async-start(bf16[8,16,1024]{2,1,0:T(8,128)(2,1)} %get-tuple-element.36), calls=%async_computation.3 | async-start | bytes 524288 | tf_op jit(solution)/shard_map/all_to_all | solution.py:479
  109.1 1.1 collective-permute-done.17
  110.2 3.3 %collective-permute-start.18 = (f32[1,128]{1,0:T(1,128)S(1)}, f32[1,128]{1,0:T(1,128)S(1)}, u32[]{:S(2)}, u32[]{:S(2)}) collective-permute-start(f32[1,128]{1,0:T(1,128)S(1)} %add.25), channel_id=1, source_target_pairs={{0,64},{32,96},{64,0},{96,32},{128,192},{160,224},{192,128},{224,1... | collective-permute-start | bytes 1544 | tf_op jit(solution)/shard_map/ppermute | solution.py:478
  113.5 1.5 %collective-permute-done.18 = f32[1,128]{1,0:T(1,128)S(1)} collective-permute-done((f32[1,128]{1,0:T(1,128)S(1)}, f32[1,128]{1,0:T(1,128)S(1)}, u32[]{:S(2)}, u32[]{:S(2)}) %collective-permute-start.18) | collective-permute-done | bytes 544 | tf_op jit(solution)/shard_map/ppermute | solution.py:478
  115.0 5.7 %collective-permute-start.19 = (f32[1,128]{1,0:T(1,128)S(1)}, f32[1,128]{1,0:T(1,128)S(1)}, u32[]{:S(2)}, u32[]{:S(2)}) collective-permute-start(f32[1,128]{1,0:T(1,128)S(1)} %add.26), channel_id=1, source_target_pairs={{0,224},{32,192},{64,160},{96,128},{128,96},{160,64},{192,32},{224... | collective-permute-start | bytes 1544 | tf_op jit(solution)/shard_map/ppermute | solution.py:478
  120.7 1.3 %merge.1 = (bf16[256,4096]{1,0:T(8,128)(2,1)}, bf16[256,4096]{1,0:T(8,128)(2,1)}) custom-call(s32[1]{0:T(128)} %bitcast.here, s32[4]{0:T(128)S(1)} %bitcast.18, s32[1]{0:T(128)} %get-tuple-element.24.lead_ref, bf16[256,4096]{1,0:T(8,128)(2,1)} %get-tuple-element.28.o_in, ...), custom_call_target="tpu_custom_call", output_to_operand_aliasing={{0}: (3, {}), {1}: (4, {})} | custom-call | tf_op jit(solution)/shard_map/merge/pallas_call | solution.py:483
  122.8 1.4 %assemble.1 = bf16[16,8192]{1,0:T(8,128)(2,1)} custom-call(s32[1]{0:T(128)} %bitcast.here, s32[1]{0:T(128)} %get-tuple-element.24.lead_ref, bf16[8,16,1024]{2,1,0:T(8,128)(2,1)S(1)} %all-to-all-done.3.got, bf16[16,8192]{1,0:T(8,128)(2,1)S(1)} %get-tuple-element.41.own, bf16[16,8192]{1,0:T(8,128)(2,1)S(1)} %collective-permute-done.16.given), custom_call_target="tpu_custom_call" | custom-call | tf_op jit(solution)/shard_map/assemble/pallas_call | solution.py:480
  (44 shorter events, 6.0 us)
Async XLA Ops:
  0.6 10.3 %collective-permute-start.1 = (bf16[16,8192]{1,0:T(8,128)(2,1)}, bf16[16,8192]{1,0:T(8,128)(2,1)S(1)}, u32[]{:S(2)}, u32[]{:S(2)}) collective-permute-start(bf16[16,8192]{1,0:T(8,128)(2,1)} %bitcast.13), channel_id=1, source_target_pairs={{0,1},{1,0},{2,3},{3,2},{4,5},{5,4},{6,7},{7,6},{8,9},{9,8},{10,11... | collective-permute-start | bytes 786440 | tf_op jit(solution)/shard_map/ppermute | solution.py:412
  0.7 1.0 copy-start.1
  1.7 0.7 copy-start.3
  3.6 15.5 %all-to-all-start = ((bf16[8,16,1152]{2,1,0:T(8,128)(2,1)}), bf16[8,16,1152]{2,1,0:T(8,128)(2,1)S(1)}, u32[]{:S(2)}, u32[]{:S(2)}) async-start(bf16[8,16,1152]{2,1,0:T(8,128)(2,1)} %chunk.1), calls=%async_computation | async-start | bytes 589824 | tf_op jit(solution)/shard_map/all_to_all | solution.py:409
  10.9 0.9 copy-start.2
  11.0 39.0 %copy-start.5 = (f32[32]{0:T(128)S(1)}, f32[32]{0:T(128)}, u32[]{:S(2)}) copy-start(f32[32]{0:T(128)} %param.8) | copy-start | bytes 388
  11.0 40.5 %copy-start.4 = (s32[1,4]{1,0:T(1,128)S(1)}, s32[1,4]{1,0:T(1,128)}, u32[]{:S(2)}) copy-start(s32[1,4]{1,0:T(1,128)} %param.7) | copy-start | bytes 52
  11.9 20.2 %collective-permute-start.5 = (bf16[32,8192]{1,0:T(8,128)(2,1)S(1)}, bf16[32,8192]{1,0:T(8,128)(2,1)S(1)}, u32[]{:S(2)}, u32[]{:S(2)}) collective-permute-start(bf16[32,8192]{1,0:T(8,128)(2,1)S(1)} %half.1), channel_id=1, source_target_pairs={{10,0},{11,30},{27,31},{26,1},{2,2},{6,8},{7,22},{18,7},{22,25},{4... | collective-permute-start | bytes 1572872 | tf_op jit(solution)/shard_map/ppermute | solution.py:414
  15.2 34.8 %collective-permute-start.6 = (bf16[2,64,4096]{2,1,0:T(8,128)(2,1)}, bf16[2,64,4096]{2,1,0:T(8,128)(2,1)}, u32[]{:S(2)}, u32[]{:S(2)}) collective-permute-start(bf16[2,64,4096]{2,1,0:T(8,128)(2,1)} %get-tuple-element.26), channel_id=1, source_target_pairs={{0,2},{1,7},{31,25},{32,34},{33,39},{63,57},{64,66},{65,71},{95,89... | collective-permute-start | bytes 3145736 | tf_op jit(solution)/shard_map/ppermute | solution.py:410
  16.8 27.0 %collective-permute-start.4 = (bf16[32,8192]{1,0:T(8,128)(2,1)S(1)}, bf16[32,8192]{1,0:T(8,128)(2,1)S(1)}, u32[]{:S(2)}, u32[]{:S(2)}) collective-permute-start(bf16[32,8192]{1,0:T(8,128)(2,1)S(1)} %half.1), channel_id=1, source_target_pairs={{8,0},{9,30},{25,31},{24,1},{0,2},{4,8},{5,22},{16,7},{20,25},{40,... | collective-permute-start | bytes 1572872 | tf_op jit(solution)/shard_map/ppermute | solution.py:414
  17.5 32.5 %collective-permute-start.7 = (bf16[2,64,4096]{2,1,0:T(8,128)(2,1)}, bf16[2,64,4096]{2,1,0:T(8,128)(2,1)}, u32[]{:S(2)}, u32[]{:S(2)}) collective-permute-start(bf16[2,64,4096]{2,1,0:T(8,128)(2,1)} %get-tuple-element.27), channel_id=1, source_target_pairs={{0,8},{1,25},{30,22},{31,7},{32,40},{33,57},{62,54},{63,39},{64,72... | collective-permute-start | bytes 3145736 | tf_op jit(solution)/shard_map/ppermute | solution.py:410
  20.1 23.7 %all-to-all-start.1 = ((bf16[16,16,1024]{2,1,0:T(8,128)(2,1)}), bf16[16,16,1024]{2,1,0:T(8,128)(2,1)S(1)}, u32[]{:S(2)}, u32[]{:S(2)}) async-start(bf16[16,16,1024]{2,1,0:T(8,128)(2,1)} %get-tuple-element.25), calls=%async_computation.1 | async-start | bytes 1048576 | tf_op jit(solution)/shard_map/all_to_all | solution.py:423
  31.4 18.6 %collective-permute-start.3 = (bf16[32,8192]{1,0:T(8,128)(2,1)S(1)}, bf16[32,8192]{1,0:T(8,128)(2,1)S(1)}, u32[]{:S(2)}, u32[]{:S(2)}) collective-permute-start(bf16[32,8192]{1,0:T(8,128)(2,1)S(1)} %half.1), channel_id=1, source_target_pairs={{14,0},{15,30},{31,31},{46,32},{47,62},{63,63},{78,64},{79,94},{95... | collective-permute-start | bytes 1572872 | tf_op jit(solution)/shard_map/ppermute | solution.py:414
  32.1 17.9 %collective-permute-start.2 = (bf16[32,8192]{1,0:T(8,128)(2,1)S(1)}, bf16[32,8192]{1,0:T(8,128)(2,1)S(1)}, u32[]{:S(2)}, u32[]{:S(2)}) collective-permute-start(bf16[32,8192]{1,0:T(8,128)(2,1)S(1)} %half.1), channel_id=1, source_target_pairs={{12,0},{13,30},{29,31},{44,32},{45,62},{61,63},{76,64},{77,94},{93... | collective-permute-start | bytes 1572872 | tf_op jit(solution)/shard_map/ppermute | solution.py:414
  43.8 7.7 %collective-permute-start = (bf16[2,4,2,16,1024]{4,3,2,1,0:T(8,128)(2,1)S(1)}, bf16[2,4,2,16,1024]{4,3,2,1,0:T(8,128)(2,1)S(1)}, u32[]{:S(2)}, u32[]{:S(2)}) collective-permute-start(bf16[2,4,2,16,1024]{4,3,2,1,0:T(8,128)(2,1)S(1)} %bitcast.11), channel_id=1, source_target_pairs={{0,1},{1,0},{2,3},{3,2},{4,5},{5,4},{6,7},{7,6},{8,9},{9,8},{10,11... | collective-permute-start | bytes 1572872 | tf_op jit(solution)/shard_map/ppermute | solution.py:424
  61.2 9.6 %collective-permute-start.10 = (bf16[16,16,1024]{2,1,0:T(8,128)(2,1)S(1)}, bf16[16,16,1024]{2,1,0:T(8,128)(2,1)S(1)}, u32[]{:S(2)}, u32[]{:S(2)}) collective-permute-start(bf16[16,16,1024]{2,1,0:T(8,128)(2,1)S(1)} %get-tuple-element.34), channel_id=1, source_target_pairs={{0,1},{1,0},{2,3},{3,2},{4,5},{5,4},{6,7},{7,6},{8,9},{9,8},{10,11... | collective-permute-start | bytes 1572872 | tf_op jit(solution)/shard_map/ppermute | solution.py:453
  63.5 8.7 %collective-permute-start.12 = (bf16[32,8192]{1,0:T(8,128)(2,1)S(1)}, bf16[32,8192]{1,0:T(8,128)(2,1)S(1)}, u32[]{:S(2)}, u32[]{:S(2)}) collective-permute-start(bf16[32,8192]{1,0:T(8,128)(2,1)S(1)} %get-tuple-element.37), channel_id=1, source_target_pairs={{0,12},{30,13},{31,29},{32,44},{62,45},{63,61},{64,76},{94,77},{95... | collective-permute-start | bytes 1572872 | tf_op jit(solution)/shard_map/ppermute | solution.py:458
  64.2 56.6 %collective-permute-start.9 = (bf16[2,64,4096]{2,1,0:T(8,128)(2,1)}, bf16[2,64,4096]{2,1,0:T(8,128)(2,1)S(1)}, u32[]{:S(2)}, u32[]{:S(2)}) collective-permute-start(bf16[2,64,4096]{2,1,0:T(8,128)(2,1)} %get-tuple-element.30), channel_id=1, source_target_pairs={{8,0},{25,1},{22,30},{7,31},{40,32},{57,33},{54,62},{39,63},{72,64... | collective-permute-start | bytes 3145736 | tf_op jit(solution)/shard_map/ppermute | solution.py:468
  64.9 55.8 %collective-permute-start.8 = (bf16[2,64,4096]{2,1,0:T(8,128)(2,1)}, bf16[2,64,4096]{2,1,0:T(8,128)(2,1)S(1)}, u32[]{:S(2)}, u32[]{:S(2)}) collective-permute-start(bf16[2,64,4096]{2,1,0:T(8,128)(2,1)} %get-tuple-element.30), channel_id=1, source_target_pairs={{2,0},{7,1},{25,31},{34,32},{39,33},{57,63},{66,64},{71,65},{89,95... | collective-permute-start | bytes 3145736 | tf_op jit(solution)/shard_map/ppermute | solution.py:468
  65.6 3.6 %collective-permute-start.11 = (f32[1,128]{1,0:T(1,128)S(1)}, f32[1,128]{1,0:T(1,128)S(1)}, u32[]{:S(2)}, u32[]{:S(2)}) collective-permute-start(f32[1,128]{1,0:T(1,128)S(1)} %get-tuple-element.35), channel_id=1, source_target_pairs={{0,32},{32,0},{64,96},{96,64},{128,160},{160,128},{192,224},{224,1... | collective-permute-start | bytes 1544 | tf_op jit(solution)/shard_map/ppermute | solution.py:452
  69.3 20.2 %collective-permute-start.13 = (bf16[32,8192]{1,0:T(8,128)(2,1)}, bf16[32,8192]{1,0:T(8,128)(2,1)}, u32[]{:S(2)}, u32[]{:S(2)}) collective-permute-start(bf16[32,8192]{1,0:T(8,128)(2,1)} %get-tuple-element.38), channel_id=1, source_target_pairs={{0,14},{30,15},{31,31},{32,46},{62,47},{63,63},{64,78},{94,79},{95... | collective-permute-start | bytes 1572872 | tf_op jit(solution)/shard_map/ppermute | solution.py:458
  70.7 18.8 %collective-permute-start.14 = (bf16[32,8192]{1,0:T(8,128)(2,1)}, bf16[32,8192]{1,0:T(8,128)(2,1)}, u32[]{:S(2)}, u32[]{:S(2)}) collective-permute-start(bf16[32,8192]{1,0:T(8,128)(2,1)} %get-tuple-element.39), channel_id=1, source_target_pairs={{0,8},{30,9},{31,25},{1,24},{2,0},{8,4},{22,5},{7,16},{25,20},{32,... | collective-permute-start | bytes 1572872 | tf_op jit(solution)/shard_map/ppermute | solution.py:458
  72.2 28.2 %collective-permute-start.15 = (bf16[32,8192]{1,0:T(8,128)(2,1)}, bf16[32,8192]{1,0:T(8,128)(2,1)}, u32[]{:S(2)}, u32[]{:S(2)}) collective-permute-start(bf16[32,8192]{1,0:T(8,128)(2,1)} %get-tuple-element.40), channel_id=1, source_target_pairs={{0,10},{30,11},{31,27},{1,26},{2,2},{8,6},{22,7},{7,18},{25,22},{3... | collective-permute-start | bytes 1572872 | tf_op jit(solution)/shard_map/ppermute | solution.py:458
  73.5 1.2 copy-start
  75.7 26.5 %all-to-all-start.2 = ((bf16[16,16,1152]{2,1,0:T(8,128)(2,1)}), bf16[16,16,1152]{2,1,0:T(8,128)(2,1)S(1)}, u32[]{:S(2)}, u32[]{:S(2)}) async-start(bf16[16,16,1152]{2,1,0:T(8,128)(2,1)} %pair.1), calls=%async_computation.2 | async-start | bytes 1179648 | tf_op jit(solution)/shard_map/all_to_all | solution.py:457
  102.1 20.6 %collective-permute-start.16 = (bf16[16,8192]{1,0:T(8,128)(2,1)}, bf16[16,8192]{1,0:T(8,128)(2,1)S(1)}, u32[]{:S(2)}, u32[]{:S(2)}) collective-permute-start(bf16[16,8192]{1,0:T(8,128)(2,1)} %get-tuple-element.42), channel_id=1, source_target_pairs={{0,1},{1,0},{2,3},{3,2},{4,5},{5,4},{6,7},{7,6},{8,9},{9,8},{10,11... | collective-permute-start | bytes 786440 | tf_op jit(solution)/shard_map/ppermute | solution.py:467
  103.0 19.7 %all-to-all-start.3 = ((bf16[8,16,1024]{2,1,0:T(8,128)(2,1)}), bf16[8,16,1024]{2,1,0:T(8,128)(2,1)S(1)}, u32[]{:S(2)}, u32[]{:S(2)}) async-start(bf16[8,16,1024]{2,1,0:T(8,128)(2,1)} %get-tuple-element.36), calls=%async_computation.3 | async-start | bytes 524288 | tf_op jit(solution)/shard_map/all_to_all | solution.py:479
  109.1 1.1 collective-permute-start.17
  110.2 4.8 %collective-permute-start.18 = (f32[1,128]{1,0:T(1,128)S(1)}, f32[1,128]{1,0:T(1,128)S(1)}, u32[]{:S(2)}, u32[]{:S(2)}) collective-permute-start(f32[1,128]{1,0:T(1,128)S(1)} %add.25), channel_id=1, source_target_pairs={{0,64},{32,96},{64,0},{96,32},{128,192},{160,224},{192,128},{224,1... | collective-permute-start | bytes 1544 | tf_op jit(solution)/shard_map/ppermute | solution.py:478
  115.0 7.2 %collective-permute-start.19 = (f32[1,128]{1,0:T(1,128)S(1)}, f32[1,128]{1,0:T(1,128)S(1)}, u32[]{:S(2)}, u32[]{:S(2)}) collective-permute-start(f32[1,128]{1,0:T(1,128)S(1)} %add.26), channel_id=1, source_target_pairs={{0,224},{32,192},{64,160},{96,128},{128,96},{160,64},{192,32},{224... | collective-permute-start | bytes 1544 | tf_op jit(solution)/shard_map/ppermute | solution.py:478
